TPU v7x, 32 devices: a whole 2x2x4 slice. The times are simulated.
32 devices in a mesh: dp: 8 (over y, x, core), tensor: 4 (over z).
Axes of the slice: x: 2, y: 2, z: 4, core: 2. Of those that a mesh axis runs over, the one named last changes fastest.
Arguments:
- hidden_in: float32 [4096, 1536], P(('dp', 'tensor')), may hold values from -6 to 6
- text_states: bfloat16 [4096, 4096], P(('dp', 'tensor')), may hold values from -6 to 6
- time_embed: float32 [8, 6, 1536], P('dp'), may hold values from -3 to 3
- positions: int32 [3, 4096], P(None, 'dp'), may hold values from 0 to 34, as said below
- modulation: bfloat16 [6, 1536], P(None, 'dp'), may hold values from -2 to 2
- query_weight: bfloat16 [1536, 1536], P('dp', 'tensor'), may hold values from -0.15625 to 0.15625
- key_weight: bfloat16 [1536, 1536], P('dp', 'tensor'), may hold values from -0.15625 to 0.15625
- value_weight: bfloat16 [1536, 1536], P('dp', 'tensor'), may hold values from -0.15625 to 0.15625
- out_weight: bfloat16 [1536, 1536], P('tensor', 'dp'), may hold values from -1.25 to 1.25
- cross_query: bfloat16 [1536, 1536], P('dp', 'tensor'), may hold values from -0.15625 to 0.15625
- cross_key: bfloat16 [4096, 1536], P('dp', 'tensor'), may hold values from -0.09375 to 0.09375
- cross_value: bfloat16 [4096, 1536], P('dp', 'tensor'), may hold values from -0.09375 to 0.09375
- cross_out: bfloat16 [1536, 1536], P('tensor', 'dp'), may hold values from -1.25 to 1.25
- up_weight: bfloat16 [1536, 8960], P('dp', 'tensor'), may hold values from -0.15625 to 0.15625
- down_weight: bfloat16 [8960, 1536], P('tensor', 'dp'), may hold values from -0.0625 to 0.0625
- qk_gain: bfloat16 [12, 512], P('tensor', 'dp'), may hold values from 0.099609375 to 1.8984375
- norm_gain: bfloat16 [1536], P('dp'), may hold values from 0.099609375 to 1.8984375
- cotangent: float32 [4096, 1536], P(('dp', 'tensor')), may hold values from -6 to 6
Outputs:
- block_out: float32 [4096, 1536], P(('dp', 'tensor'))
- grad_hidden: float32 [4096, 1536], P(('dp', 'tensor'))
- grad_text: float32 [4096, 4096], P(('dp', 'tensor'))
- grad_time: float32 [8, 6, 1536], P('dp')
- grad_modulation: float32 [6, 1536], P(None, 'dp')
- grad_query: float32 [1536, 1536], P('dp', 'tensor')
- grad_key: float32 [1536, 1536], P('dp', 'tensor')
- grad_value: float32 [1536, 1536], P('dp', 'tensor')
- grad_out_weight: float32 [1536, 1536], P('tensor', 'dp')
- grad_cross_query: float32 [1536, 1536], P('dp', 'tensor')
- grad_cross_key: float32 [4096, 1536], P('dp', 'tensor')
- grad_cross_value: float32 [4096, 1536], P('dp', 'tensor')
- grad_cross_out: float32 [1536, 1536], P('tensor', 'dp')
- grad_up: float32 [1536, 8960], P('dp', 'tensor')
- grad_down: float32 [8960, 1536], P('tensor', 'dp')
- grad_qk_gain: float32 [12, 512], P('tensor', 'dp')
- grad_norm_gain: float32 [1536], P('dp')
Inputs may be any that keep to these rules, and one draw needn't show every extreme that they name: `positions`: in each of the 8 clips the 512 tokens run over a grid of frames by rows by columns, frames slowest and columns fastest, with 4 or 8 rows and 4 or 8 columns a frame; frame, row and column numbers are shifted by offsets of at most 3, 15 and 15 that are drawn per clip.
All inputs are finite; a program needn't handle non-finite values.
Results may differ from a plain program's by a relative error of at most 0.02.
Values may be sent and summed in bfloat16 or wider, within the bound.
A program may use at most 192 MiB of HBM per device.

v0:
```python
import jax
import jax.numpy as jnp
from jax import lax
from jax.sharding import PartitionSpec as P

HEAD_DIM = 128
D = 1536


EPSILON = 1e-06
CONTRACT_LAST = (((1,), (1,)), ((), ()))
CONTRACT_FIRST = (((0,), (0,)), ((), ()))


def layer_norm(values):
    center = values - jnp.mean(values, axis=-1, keepdims=True)
    spread = jnp.mean(center * center, axis=-1, keepdims=True)
    return center * lax.rsqrt(spread + EPSILON)


def modulate(values, shift, scale):
    return layer_norm(values) * (1.0 + scale) + shift


def gained_norm(values, weight):
    return layer_norm(values) * weight


def scaled(values, total, gain):
    return values * lax.rsqrt(total[:, None] / D + EPSILON) * gain


def gelu_tanh(values):
    return jax.nn.gelu(values, approximate=True)


def rotary_tables(positions, head_width):
    pairs = head_width // 2
    third = pairs // 3
    first = pairs - 2 * third
    freq_frame = jnp.power(10000.0, -jnp.arange(first, dtype=jnp.float32) / first)
    freq_side = jnp.power(10000.0, -jnp.arange(third, dtype=jnp.float32) / third)
    places = positions.astype(jnp.float32)
    angles = jnp.concatenate(
        [
            places[0][:, None] * freq_frame[None, :],
            places[1][:, None] * freq_side[None, :],
            places[2][:, None] * freq_side[None, :],
        ],
        axis=1,
    )
    return (jnp.cos(angles), jnp.sin(angles))


def rotate(values, cosine, sine):
    shape = values.shape
    paired = values.reshape(shape[0], shape[1], shape[2] // 2, 2)
    real_part = paired[..., 0]
    imag_part = paired[..., 1]
    cos_row = cosine[:, None, :]
    sin_row = sine[:, None, :]
    turned = jnp.stack(
        [real_part * cos_row - imag_part * sin_row, real_part * sin_row + imag_part * cos_row],
        axis=-1,
    )
    return turned.reshape(shape)


def product_back(grads, weight):
    return lax.dot_general(grads, weight, CONTRACT_LAST, preferred_element_type=jnp.float32)


def weight_grad(inputs, grads):
    return lax.dot_general(inputs, grads, CONTRACT_FIRST, preferred_element_type=jnp.float32)


def attend_forward(queries, keys, values):
    rows, heads, width = queries.shape
    block = min(512, rows)
    scale = width ** (-0.5)

    def one_block(query_block):
        scores = (
            jnp.einsum("qhd,khd->hqk", query_block, keys, preferred_element_type=jnp.float32)
            * scale
        )
        top = jnp.max(scores, axis=-1, keepdims=True)
        expo = jnp.exp(scores - top)
        summed = jnp.sum(expo, axis=-1, keepdims=True)
        probs = expo / summed
        result = jnp.einsum(
            "hqk,khd->qhd", probs.astype(jnp.bfloat16), values, preferred_element_type=jnp.float32
        )
        return (result, top[..., 0] + jnp.log(summed[..., 0]))

    result, logsum = lax.map(one_block, queries.reshape(rows // block, block, heads, width))
    return (result.reshape(rows, heads, width), logsum)


def attend_backward(queries, keys, values, logsum, grad_out):
    rows, heads, width = queries.shape
    block = min(512, rows)
    count = rows // block
    scale = width ** (-0.5)

    def one_block(carry, item):
        key_grad, value_grad = carry
        query_block, grad_block, logsum_block = item
        scores = (
            jnp.einsum("qhd,khd->hqk", query_block, keys, preferred_element_type=jnp.float32)
            * scale
        )
        probs = jnp.exp(scores - logsum_block[..., None])
        prob_grad = jnp.einsum(
            "qhd,khd->hqk", grad_block, values, preferred_element_type=jnp.float32
        )
        inner = jnp.sum(prob_grad * probs, axis=-1, keepdims=True)
        score_grad = (probs * (prob_grad - inner)).astype(jnp.bfloat16)
        query_grad = (
            jnp.einsum("hqk,khd->qhd", score_grad, keys, preferred_element_type=jnp.float32) * scale
        )
        key_grad = (
            key_grad
            + jnp.einsum(
                "hqk,qhd->khd", score_grad, query_block, preferred_element_type=jnp.float32
            )
            * scale
        )
        value_grad = value_grad + jnp.einsum(
            "hqk,qhd->khd",
            probs.astype(jnp.bfloat16),
            grad_block,
            preferred_element_type=jnp.float32,
        )
        return ((key_grad, value_grad), query_grad)

    start_carry = (jnp.zeros(keys.shape, jnp.float32), jnp.zeros(values.shape, jnp.float32))
    items = (
        queries.reshape(count, block, heads, width),
        grad_out.reshape(count, block, heads, width),
        logsum,
    )
    (key_grad, value_grad), query_grad = lax.scan(one_block, start_carry, items)
    return (query_grad.reshape(rows, heads, width), key_grad, value_grad)


def gather_sequence(values):
    return lax.all_gather(values, "tensor", axis=0, tiled=True)


def gather_grads(values):
    return lax.all_gather(values, "tensor", axis=0, tiled=True)


def total_squares(first, second):
    return lax.psum((jnp.sum(first * first, axis=-1), jnp.sum(second * second, axis=-1)), "tensor")


def total_norm_grads(first, second):
    return lax.psum((first, second), "tensor")


def scatter_branch(values, weight, rows):

    def term(start, count):
        return jnp.dot(values, weight, preferred_element_type=jnp.float32)

    return lax.psum_scatter(
        term(jnp.int32(0), rows * lax.axis_size("tensor")),
        "tensor",
        scatter_dimension=0,
        tiled=True,
    )


def summed_back(pairs):
    result = 0.0
    for grads, weight in pairs:
        result = result + product_back(grads, weight)
    return result


def scatter_grads(pairs, rows):

    def term(start, count):
        return summed_back(pairs)

    return lax.psum_scatter(
        term(jnp.int32(0), rows * lax.axis_size("tensor")),
        "tensor",
        scatter_dimension=0,
        tiled=True,
    )


def scatter_text(pairs, rows):

    def term(start, count):
        return summed_back(pairs)

    return lax.psum_scatter(
        term(jnp.int32(0), lax.axis_size("tensor") * rows).astype(jnp.bfloat16),
        "tensor",
        scatter_dimension=0,
        tiled=True,
    ).astype(jnp.float32)


def norm_pull(shaping, raw, total, gain, grad):
    _, pull = jax.vjp(shaping, raw, total, gain)
    return pull(grad)


def body(
    hidden_in,
    text_states,
    time_embed,
    positions,
    modulation,
    query_weight,
    key_weight,
    value_weight,
    out_weight,
    cross_query,
    cross_key,
    cross_value,
    cross_out,
    up_weight,
    down_weight,
    qk_gain,
    norm_gain,
    cotangent,
):

    def fetch_weights():
        columns = (
            lax.all_gather(query_weight, "dp", axis=0, tiled=True),
            lax.all_gather(key_weight, "dp", axis=0, tiled=True),
            lax.all_gather(value_weight, "dp", axis=0, tiled=True),
            lax.all_gather(cross_query, "dp", axis=0, tiled=True),
            lax.all_gather(cross_key, "dp", axis=0, tiled=True),
            lax.all_gather(cross_value, "dp", axis=0, tiled=True),
            lax.all_gather(up_weight, "dp", axis=0, tiled=True),
            lax.all_gather(norm_gain, "dp", axis=0, tiled=True),
        )
        others = (
            lax.all_gather(out_weight, "dp", axis=1, tiled=True),
            lax.all_gather(cross_out, "dp", axis=1, tiled=True),
            lax.all_gather(down_weight, "dp", axis=1, tiled=True),
            lax.all_gather(qk_gain, "dp", axis=1, tiled=True),
            lax.all_gather(modulation, "dp", axis=1, tiled=True),
        )
        return (columns, others)

    text_all = lax.all_gather(text_states, "tensor", axis=0, tiled=True)
    columns, others = fetch_weights()
    (
        query_full,
        key_full,
        value_full,
        cross_query_full,
        cross_key_full,
        cross_value_full,
        up_full,
        gain_low,
    ) = columns
    out_full, cross_out_full, down_full, gain_table, modulation_full = others
    local_rows = hidden_in.shape[0]
    heads_here = out_full.shape[0] // HEAD_DIM
    mixing = modulation_full.astype(jnp.float32) + time_embed[0]
    gains = gain_table.astype(jnp.float32).reshape(heads_here, 4, HEAD_DIM)
    gain_parts = [gains[:, index].reshape(-1) for index in range(4)]
    norm_weight = gain_low.astype(jnp.float32)
    cosine, sine = rotary_tables(positions, HEAD_DIM)
    self_input = modulate(hidden_in, mixing[0], mixing[1]).astype(jnp.bfloat16)
    self_whole = gather_sequence(self_input)
    length = self_whole.shape[0]
    query_raw = jnp.dot(self_whole, query_full, preferred_element_type=jnp.float32)
    key_raw = jnp.dot(self_whole, key_full, preferred_element_type=jnp.float32)
    value_low = (
        jnp.dot(self_whole, value_full, preferred_element_type=jnp.float32)
        .astype(jnp.bfloat16)
        .reshape(length, heads_here, HEAD_DIM)
    )
    query_total, key_total = total_squares(query_raw, key_raw)

    def self_shape(raw, total, gain):
        return rotate(scaled(raw, total, gain).reshape(length, heads_here, HEAD_DIM), cosine, sine)

    def cross_shape(raw, total, gain):
        return scaled(raw, total, gain).reshape(raw.shape[0], heads_here, HEAD_DIM)

    query_rot = self_shape(query_raw, query_total, gain_parts[0]).astype(jnp.bfloat16)
    key_rot = self_shape(key_raw, key_total, gain_parts[1]).astype(jnp.bfloat16)
    self_heads, self_logsum = attend_forward(query_rot, key_rot, value_low)
    self_attended = self_heads.reshape(length, -1).astype(jnp.bfloat16)
    self_branch = scatter_branch(self_attended, out_full, local_rows)
    resid_self = hidden_in + self_branch * mixing[2]
    cross_input = gained_norm(resid_self, norm_weight).astype(jnp.bfloat16)
    cross_whole = gather_sequence(cross_input)
    text_rows = text_all.shape[0]
    cross_query_raw = jnp.dot(cross_whole, cross_query_full, preferred_element_type=jnp.float32)
    cross_key_raw = jnp.dot(text_all, cross_key_full, preferred_element_type=jnp.float32)
    cross_value_low = (
        jnp.dot(text_all, cross_value_full, preferred_element_type=jnp.float32)
        .astype(jnp.bfloat16)
        .reshape(text_rows, heads_here, HEAD_DIM)
    )
    cross_query_total, cross_key_total = total_squares(cross_query_raw, cross_key_raw)
    cross_query_norm = cross_shape(cross_query_raw, cross_query_total, gain_parts[2]).astype(
        jnp.bfloat16
    )
    cross_key_norm = cross_shape(cross_key_raw, cross_key_total, gain_parts[3]).astype(jnp.bfloat16)
    cross_heads, cross_logsum = attend_forward(cross_query_norm, cross_key_norm, cross_value_low)
    cross_attended = cross_heads.reshape(length, -1).astype(jnp.bfloat16)
    cross_branch = scatter_branch(cross_attended, cross_out_full, local_rows)
    resid_cross = resid_self + cross_branch
    feed_input = modulate(resid_cross, mixing[3], mixing[4]).astype(jnp.bfloat16)
    feed_whole = gather_sequence(feed_input)
    up_raw = jnp.dot(feed_whole, up_full, preferred_element_type=jnp.float32)
    activated = gelu_tanh(up_raw).astype(jnp.bfloat16)
    feed_branch = scatter_branch(activated, down_full, local_rows)
    block_out = resid_cross + feed_branch * mixing[5]
    columns, others = fetch_weights()
    (
        query_full,
        key_full,
        value_full,
        cross_query_full,
        cross_key_full,
        cross_value_full,
        up_full,
        gain_low,
    ) = columns
    out_full, cross_out_full, down_full, gain_table, modulation_full = others
    grad_gate_feed = jnp.sum(cotangent * feed_branch, axis=0)
    feed_grad_whole = gather_grads((cotangent * mixing[5]).astype(jnp.bfloat16))
    grad_activated = product_back(feed_grad_whole, down_full)
    grad_down = weight_grad(activated, feed_grad_whole)
    _, gelu_pull = jax.vjp(gelu_tanh, up_raw)
    grad_up_raw = gelu_pull(grad_activated)[0].astype(jnp.bfloat16)
    grad_up = weight_grad(feed_whole, grad_up_raw)
    grad_feed_input = scatter_grads(((grad_up_raw, up_full),), local_rows)
    _, feed_pull = jax.vjp(modulate, resid_cross, mixing[3], mixing[4])
    grad_from_feed, grad_shift_feed, grad_scale_feed = feed_pull(grad_feed_input)
    grad_resid_cross = cotangent + grad_from_feed
    cross_grad_whole = gather_grads(grad_resid_cross.astype(jnp.bfloat16))
    grad_cross_attended = product_back(cross_grad_whole, cross_out_full).astype(jnp.bfloat16)
    grad_cross_out = weight_grad(cross_attended, cross_grad_whole)
    grad_cross_query_norm, grad_cross_key_norm, grad_cross_value_heads = attend_backward(
        cross_query_norm,
        cross_key_norm,
        cross_value_low,
        cross_logsum,
        grad_cross_attended.reshape(length, heads_here, HEAD_DIM),
    )
    query_local, query_part, grad_gain_cross_query = norm_pull(
        cross_shape, cross_query_raw, cross_query_total, gain_parts[2], grad_cross_query_norm
    )
    key_local, key_part, grad_gain_cross_key = norm_pull(
        cross_shape, cross_key_raw, cross_key_total, gain_parts[3], grad_cross_key_norm
    )
    query_whole_part, key_whole_part = total_norm_grads(query_part, key_part)
    grad_cross_query_raw = (query_local + 2.0 * cross_query_raw * query_whole_part[:, None]).astype(
        jnp.bfloat16
    )
    grad_cross_key_raw = (key_local + 2.0 * cross_key_raw * key_whole_part[:, None]).astype(
        jnp.bfloat16
    )
    grad_cross_value_low = grad_cross_value_heads.reshape(text_rows, -1).astype(jnp.bfloat16)
    grad_cross_query = weight_grad(cross_whole, grad_cross_query_raw)
    grad_cross_key = weight_grad(text_all, grad_cross_key_raw)
    grad_cross_value = weight_grad(text_all, grad_cross_value_low)
    grad_text = scatter_text(
        ((grad_cross_key_raw, cross_key_full), (grad_cross_value_low, cross_value_full)),
        text_states.shape[0],
    )
    grad_cross_input = scatter_grads(((grad_cross_query_raw, cross_query_full),), local_rows)
    _, cross_pull = jax.vjp(gained_norm, resid_self, norm_weight)
    grad_from_cross, grad_norm_part = cross_pull(grad_cross_input)
    grad_resid_self = grad_resid_cross + grad_from_cross
    grad_gate_self = jnp.sum(grad_resid_self * self_branch, axis=0)
    self_grad_whole = gather_grads((grad_resid_self * mixing[2]).astype(jnp.bfloat16))
    grad_self_attended = product_back(self_grad_whole, out_full).astype(jnp.bfloat16)
    grad_out_weight = weight_grad(self_attended, self_grad_whole)
    grad_query_rot, grad_key_rot, grad_value_heads = attend_backward(
        query_rot,
        key_rot,
        value_low,
        self_logsum,
        grad_self_attended.reshape(length, heads_here, HEAD_DIM),
    )
    query_local, query_part, grad_gain_query = norm_pull(
        self_shape, query_raw, query_total, gain_parts[0], grad_query_rot
    )
    key_local, key_part, grad_gain_key = norm_pull(
        self_shape, key_raw, key_total, gain_parts[1], grad_key_rot
    )
    query_whole_part, key_whole_part = total_norm_grads(query_part, key_part)
    grad_query_raw = (query_local + 2.0 * query_raw * query_whole_part[:, None]).astype(
        jnp.bfloat16
    )
    grad_key_raw = (key_local + 2.0 * key_raw * key_whole_part[:, None]).astype(jnp.bfloat16)
    grad_value_low = grad_value_heads.reshape(length, -1).astype(jnp.bfloat16)
    grad_query = weight_grad(self_whole, grad_query_raw)
    grad_key = weight_grad(self_whole, grad_key_raw)
    grad_value = weight_grad(self_whole, grad_value_low)
    grad_self_input = scatter_grads(
        ((grad_query_raw, query_full), (grad_key_raw, key_full), (grad_value_low, value_full)),
        local_rows,
    )
    _, self_pull = jax.vjp(modulate, hidden_in, mixing[0], mixing[1])
    grad_from_self, grad_shift_self, grad_scale_self = self_pull(grad_self_input)
    grad_hidden = grad_resid_self + grad_from_self
    time_part = jnp.stack(
        [
            grad_shift_self,
            grad_scale_self,
            grad_gate_self,
            grad_shift_feed,
            grad_scale_feed,
            grad_gate_feed,
        ],
        axis=0,
    )
    time_total, norm_total = (
        lax.psum(time_part.astype(jnp.bfloat16), "tensor").astype(jnp.float32),
        lax.psum(grad_norm_part.astype(jnp.bfloat16), "tensor").astype(jnp.float32),
    )
    gain_grads = jnp.stack(
        [
            part.reshape(heads_here, HEAD_DIM)
            for part in (grad_gain_query, grad_gain_key, grad_gain_cross_query, grad_gain_cross_key)
        ],
        axis=1,
    ).reshape(heads_here, 4 * HEAD_DIM)
    column_sums = (
        lax.psum_scatter(
            grad_query.astype(jnp.bfloat16), "dp", scatter_dimension=0, tiled=True
        ).astype(jnp.float32),
        lax.psum_scatter(
            grad_key.astype(jnp.bfloat16), "dp", scatter_dimension=0, tiled=True
        ).astype(jnp.float32),
        lax.psum_scatter(
            grad_value.astype(jnp.bfloat16), "dp", scatter_dimension=0, tiled=True
        ).astype(jnp.float32),
        lax.psum_scatter(
            grad_cross_query.astype(jnp.bfloat16), "dp", scatter_dimension=0, tiled=True
        ).astype(jnp.float32),
        lax.psum_scatter(
            grad_cross_key.astype(jnp.bfloat16), "dp", scatter_dimension=0, tiled=True
        ).astype(jnp.float32),
        lax.psum_scatter(
            grad_cross_value.astype(jnp.bfloat16), "dp", scatter_dimension=0, tiled=True
        ).astype(jnp.float32),
        lax.psum_scatter(
            grad_up.astype(jnp.bfloat16), "dp", scatter_dimension=0, tiled=True
        ).astype(jnp.float32),
        lax.psum_scatter(
            norm_total.astype(jnp.bfloat16), "dp", scatter_dimension=0, tiled=True
        ).astype(jnp.float32),
    )
    row_sums = (
        lax.psum_scatter(
            grad_out_weight.astype(jnp.bfloat16), "dp", scatter_dimension=1, tiled=True
        ).astype(jnp.float32),
        lax.psum_scatter(
            grad_cross_out.astype(jnp.bfloat16), "dp", scatter_dimension=1, tiled=True
        ).astype(jnp.float32),
        lax.psum_scatter(
            grad_down.astype(jnp.bfloat16), "dp", scatter_dimension=1, tiled=True
        ).astype(jnp.float32),
        lax.psum_scatter(
            gain_grads.astype(jnp.bfloat16), "dp", scatter_dimension=1, tiled=True
        ).astype(jnp.float32),
        lax.psum_scatter(
            time_total.astype(jnp.bfloat16), "dp", scatter_dimension=1, tiled=True
        ).astype(jnp.float32),
    )
    return (
        block_out,
        grad_hidden,
        grad_text,
        time_total[None],
        row_sums[4],
        column_sums[0],
        column_sums[1],
        column_sums[2],
        row_sums[0],
        column_sums[3],
        column_sums[4],
        column_sums[5],
        row_sums[1],
        column_sums[6],
        row_sums[2],
        row_sums[3],
        column_sums[7],
    )


def solution(mesh):
    return jax.shard_map(
        body,
        mesh=mesh,
        in_specs=(
            P(("dp", "tensor"), None),
            P(("dp", "tensor"), None),
            P("dp", None, None),
            P(None, "dp"),
            P(None, "dp"),
            P("dp", "tensor"),
            P("dp", "tensor"),
            P("dp", "tensor"),
            P("tensor", "dp"),
            P("dp", "tensor"),
            P("dp", "tensor"),
            P("dp", "tensor"),
            P("tensor", "dp"),
            P("dp", "tensor"),
            P("tensor", "dp"),
            P("tensor", "dp"),
            P("dp"),
            P(("dp", "tensor"), None),
        ),
        out_specs=(
            P(("dp", "tensor"), None),
            P(("dp", "tensor"), None),
            P(("dp", "tensor"), None),
            P("dp", None, None),
            P(None, "dp"),
            P("dp", "tensor"),
            P("dp", "tensor"),
            P("dp", "tensor"),
            P("tensor", "dp"),
            P("dp", "tensor"),
            P("dp", "tensor"),
            P("dp", "tensor"),
            P("tensor", "dp"),
            P("dp", "tensor"),
            P("tensor", "dp"),
            P("tensor", "dp"),
            P("dp"),
        ),
        check_vma=False,
    )
```

profile of v0, /device:TPU:0, one launch (start us, length us, event | category | flops | bytes accessed | tf_op | source)
XLA Modules:
  0.0 1760.4 jit_solution(1067973689122134549)
XLA Ops:
  8.0 10.7 all-gather
  27.0 8.7 all-gather.1
  37.1 38.9 %all-gather.20.cloned.1.call-done = bf16[512,1536]{1,0:T(8,128)(2,1)} async-done(((bf16[128,1536]{1,0:T(8,128)(2,1)}), bf16[512,1536]{1,0:T(8,128)(2,1)}) %all-gather.20.cloned.1.call-update) | async-done | bytes 1572880 | tf_op jit(solution)/shard_map/all_gather | solution.py:148
  78.8 22.1 %all-gather.24.cloned.1.call-done = bf16[1536,384]{1,0:T(8,128)(2,1)} async-done(((bf16[192,384]{1,0:T(8,128)(2,1)}), bf16[1536,384]{1,0:T(8,128)(2,1)}) %all-gather.24.cloned.1.call-update) | async-done | bytes 1179664 | tf_op jit(solution)/shard_map/all_gather | solution.py:237
  103.0 11.9 all-reduce.8
  131.7 20.9 %all-gather.28.cloned.1.call-done = bf16[384,1536]{0,1:T(8,128)(2,1)} async-done(((bf16[384,192]{0,1:T(8,128)(2,1)}), bf16[384,1536]{0,1:T(8,128)(2,1)}) %all-gather.28.cloned.1.call-update) | async-done | bytes 1179664 | tf_op jit(solution)/shard_map/all_gather | solution.py:247
  152.5 4.1 fusion.59
  161.1 13.8 all-reduce.4
  175.6 41.5 %reduce-scatter.24.cloned.1.call-done = f32[128,1536]{1,0:T(8,128)} async-done(((f32[512,1536]{1,0:T(8,128)}), f32[128,1536]{1,0:T(8,128)}) %reduce-scatter.24.cloned.1.call-update) | async-done | bytes 786448 | tf_op jit(solution)/shard_map/reduce_scatter | solution.py:168
  221.7 29.6 %all-gather.32.cloned.1.call-done = bf16[4096,384]{1,0:T(8,128)(2,1)} async-done(((bf16[512,384]{1,0:T(8,128)(2,1)}), bf16[4096,384]{1,0:T(8,128)(2,1)}) %all-gather.32.cloned.1.call-update) | async-done | bytes 3145744 | tf_op jit(solution)/shard_map/all_gather | solution.py:242
  251.3 82.4 %all-gather.30.cloned.1.call-done = bf16[512,4096]{1,0:T(8,128)(2,1)} async-done(((bf16[128,4096]{1,0:T(8,128)(2,1)}), bf16[512,4096]{1,0:T(8,128)(2,1)}) %all-gather.30.cloned.1.call-update) | async-done | bytes 4194320 | tf_op jit(solution)/shard_map/all_gather | solution.py:255
  333.7 5.8 convolution_convert_fusion.13
  339.4 27.0 %all-gather.38.cloned.1.call-done = bf16[4096,384]{1,0:T(8,128)(2,1)} async-done(((bf16[512,384]{1,0:T(8,128)(2,1)}), bf16[4096,384]{1,0:T(8,128)(2,1)}) %all-gather.38.cloned.1.call-update) | async-done | bytes 3145744 | tf_op jit(solution)/shard_map/all_gather | solution.py:241
  366.4 6.5 multiply_reduce_fusion.19
  372.9 19.4 %all-gather.36.cloned.1.call-done = bf16[1536,384]{1,0:T(8,128)(2,1)} async-done(((bf16[192,384]{1,0:T(8,128)(2,1)}), bf16[1536,384]{1,0:T(8,128)(2,1)}) %all-gather.36.cloned.1.call-update) | async-done | bytes 1179664 | tf_op jit(solution)/shard_map/all_gather | solution.py:240
  392.3 39.3 %all-gather.34.cloned.1.call-done = bf16[512,1536]{1,0:T(8,128)(2,1)} async-done(((bf16[128,1536]{1,0:T(8,128)(2,1)}), bf16[512,1536]{1,0:T(8,128)(2,1)}) %all-gather.34.cloned.1.call-update) | async-done | bytes 1572880 | tf_op jit(solution)/shard_map/all_gather | solution.py:148
  431.5 4.0 multiply_reduce_fusion.20
  435.6 10.3 all-reduce.7
  456.2 4.2 fusion.60
  461.1 59.8 %reduce-scatter.26.cloned.1.call-done = f32[128,1536]{1,0:T(8,128)} async-done(((f32[512,1536]{1,0:T(8,128)}), f32[128,1536]{1,0:T(8,128)}) %reduce-scatter.26.cloned.1.call-update) | async-done | bytes 786448 | tf_op jit(solution)/shard_map/reduce_scatter | solution.py:168
  525.7 45.7 %all-gather.44.cloned.1.call-done = bf16[1536,2240]{1,0:T(8,128)(2,1)} async-done(((bf16[192,2240]{1,0:T(8,128)(2,1)}), bf16[1536,2240]{1,0:T(8,128)(2,1)}) %all-gather.44.cloned.1.call-update) | async-done | bytes 6881296 | tf_op jit(solution)/shard_map/all_gather | solution.py:243
  571.5 39.1 %all-gather.42.cloned.1.call-done = bf16[512,1536]{1,0:T(8,128)(2,1)} async-done(((bf16[128,1536]{1,0:T(8,128)(2,1)}), bf16[512,1536]{1,0:T(8,128)(2,1)}) %all-gather.42.cloned.1.call-update) | async-done | bytes 1572880 | tf_op jit(solution)/shard_map/all_gather | solution.py:148
  610.6 9.3 fusion.61
  619.9 40.2 %all-gather.46.cloned.1.call-done = bf16[2240,1536]{0,1:T(8,128)(2,1)} async-done(((bf16[2240,192]{0,1:T(8,128)(2,1)}), bf16[2240,1536]{0,1:T(8,128)(2,1)}) %all-gather.46.cloned.1.call-update) | async-done | bytes 6881296 | tf_op jit(solution)/shard_map/all_gather | solution.py:249
  660.1 10.3 fusion.51
  670.5 60.4 %reduce-scatter.28.cloned.1.call-done = f32[128,1536]{1,0:T(8,128)} async-done(((f32[512,1536]{1,0:T(8,128)}), f32[128,1536]{1,0:T(8,128)}) %reduce-scatter.28.cloned.1.call-update) | async-done | bytes 786448 | tf_op jit(solution)/shard_map/reduce_scatter | solution.py:168
  730.9 3.4 multiply_reduce_fusion.7
  734.5 37.0 %all-gather.48.cloned.1.call-done = bf16[512,1536]{1,0:T(8,128)(2,1)} async-done(((bf16[128,1536]{1,0:T(8,128)(2,1)}), bf16[512,1536]{1,0:T(8,128)(2,1)}) %all-gather.48.cloned.1.call-update) | async-done | bytes 1572880 | tf_op jit(solution)/shard_map/all_gather | solution.py:152
  771.6 11.3 fusion.8
  784.3 8.6 fusion.62
  793.0 59.2 %reduce-scatter.30.cloned.1.call-done = f32[128,1536]{1,0:T(8,128)} async-done(((f32[512,1536]{1,0:T(8,128)}), f32[128,1536]{1,0:T(8,128)}) %reduce-scatter.30.cloned.1.call-update) | async-done | bytes 786448 | tf_op jit(solution)/shard_map/reduce_scatter | solution.py:188
  860.5 35.5 %all-gather.50.cloned.1.call-done = bf16[512,1536]{1,0:T(8,128)(2,1)} async-done(((bf16[128,1536]{1,0:T(8,128)(2,1)}), bf16[512,1536]{1,0:T(8,128)(2,1)}) %all-gather.50.cloned.1.call-update) | async-done | bytes 1572880 | tf_op jit(solution)/shard_map/all_gather | solution.py:152
  896.0 2.7 convolution_convert_fusion.11
  904.3 10.3 psum.74
  917.6 3.9 fusion.63
  921.6 58.7 %reduce-scatter.32.cloned.1.call-done = f32[128,1536]{1,0:T(8,128)} async-done(((f32[512,1536]{1,0:T(8,128)}), f32[128,1536]{1,0:T(8,128)}) %reduce-scatter.32.cloned.1.call-update) | async-done | bytes 786448 | tf_op jit(solution)/shard_map/reduce_scatter | solution.py:188
  993.7 31.4 %all-gather.52.cloned.1.call-done = bf16[512,1536]{1,0:T(8,128)(2,1)} async-done(((bf16[128,1536]{1,0:T(8,128)(2,1)}), bf16[512,1536]{1,0:T(8,128)(2,1)}) %all-gather.52.cloned.1.call-update) | async-done | bytes 1572880 | tf_op jit(solution)/shard_map/all_gather | solution.py:152
  1042.8 10.5 all-reduce.6
  1061.2 8.6 convolution_convert_fusion
  1071.3 7.7 convolution_convert_fusion.1
  1082.6 3.6 convolution_convert_fusion.5
  1088.1 5.6 fusion.1
  1095.6 3.5 convolution_convert_fusion.6
  1101.3 3.5 convolution_convert_fusion.8
  1104.9 3.6 convolution_convert_fusion.9
  1108.8 5.7 fusion
  1115.3 11.8 all-reduce.5
  1127.2 8.7 fusion.65
  1137.6 16.8 all-reduce.9
  1155.7 8.8 add_convert_fusion
  1164.5 23.1 %reduce-scatter.56.cloned.1.call-done = bf16[2240,192]{0,1:T(8,128)(2,1)} async-done(((bf16[2240,1536]{0,1:T(8,128)(2,1)}), bf16[2240,192]{0,1:T(8,128)(2,1)}) %reduce-scatter.56.cloned.1.call-update) | async-done | bytes 860176 | tf_op jit(solution)/shard_map/reduce_scatter | solution.py:470
  1190.0 67.0 %reduce-scatter.54.cloned.1.call-done = bf16[192,2240]{1,0:T(8,128)(2,1)} async-done(((bf16[1536,2240]{1,0:T(8,128)(2,1)}), bf16[192,2240]{1,0:T(8,128)(2,1)}) %reduce-scatter.54.cloned.1.call-update) | async-done | bytes 860176 | tf_op jit(solution)/shard_map/reduce_scatter | solution.py:456
  1259.5 37.4 %reduce-scatter.52.cloned.1.call-done = bf16[384,192]{0,1:T(8,128)(2,1)} async-done(((bf16[384,1536]{0,1:T(8,128)(2,1)}), bf16[384,192]{0,1:T(8,128)(2,1)}) %reduce-scatter.52.cloned.1.call-update) | async-done | bytes 147472 | tf_op jit(solution)/shard_map/reduce_scatter | solution.py:467
  1298.5 38.6 %reduce-scatter.46.cloned.1.call-done = bf16[192,384]{1,0:T(8,128)(2,1)} async-done(((bf16[1536,384]{1,0:T(8,128)(2,1)}), bf16[192,384]{1,0:T(8,128)(2,1)}) %reduce-scatter.46.cloned.1.call-update) | async-done | bytes 147472 | tf_op jit(solution)/shard_map/reduce_scatter | solution.py:447
  1338.7 48.0 %reduce-scatter.50.cloned.1.call-done = bf16[512,384]{0,1:T(8,128)(2,1)} async-done(((bf16[4096,384]{0,1:T(8,128)(2,1)}), bf16[512,384]{0,1:T(8,128)(2,1)}) %reduce-scatter.50.cloned.1.call-update) | async-done | bytes 393232 | tf_op jit(solution)/shard_map/reduce_scatter | solution.py:453
  1388.8 35.2 %reduce-scatter.60.cloned.1.call-done = bf16[64,3]{1,0:T(8,128)(2,1)} async-done(((bf16[512,3]{1,0:T(8,128)(2,1)}), bf16[64,3]{1,0:T(8,128)(2,1)}) %reduce-scatter.60.cloned.1.call-update) | async-done | bytes 400
  1425.3 38.5 %reduce-scatter.44.cloned.1.call-done = bf16[384,192]{0,1:T(8,128)(2,1)} async-done(((bf16[384,1536]{0,1:T(8,128)(2,1)}), bf16[384,192]{0,1:T(8,128)(2,1)}) %reduce-scatter.44.cloned.1.call-update) | async-done | bytes 147472 | tf_op jit(solution)/shard_map/reduce_scatter | solution.py:464
  1465.5 38.7 %reduce-scatter.42.cloned.1.call-done = bf16[192,384]{1,0:T(8,128)(2,1)} async-done(((bf16[1536,384]{1,0:T(8,128)(2,1)}), bf16[192,384]{1,0:T(8,128)(2,1)}) %reduce-scatter.42.cloned.1.call-update) | async-done | bytes 147472 | tf_op jit(solution)/shard_map/reduce_scatter | solution.py:444
  1505.8 38.4 %reduce-scatter.40.cloned.1.call-done = bf16[192,384]{1,0:T(8,128)(2,1)} async-done(((bf16[1536,384]{1,0:T(8,128)(2,1)}), bf16[192,384]{1,0:T(8,128)(2,1)}) %reduce-scatter.40.cloned.1.call-update) | async-done | bytes 147472 | tf_op jit(solution)/shard_map/reduce_scatter | solution.py:441
  1545.9 39.1 %reduce-scatter.38.cloned.1.call-done = bf16[192,384]{1,0:T(8,128)(2,1)} async-done(((bf16[1536,384]{1,0:T(8,128)(2,1)}), bf16[192,384]{1,0:T(8,128)(2,1)}) %reduce-scatter.38.cloned.1.call-update) | async-done | bytes 147472 | tf_op jit(solution)/shard_map/reduce_scatter | solution.py:438
  1586.6 48.0 %reduce-scatter.48.cloned.1.call-done = bf16[512,384]{0,1:T(8,128)(2,1)} async-done(((bf16[4096,384]{0,1:T(8,128)(2,1)}), bf16[512,384]{0,1:T(8,128)(2,1)}) %reduce-scatter.48.cloned.1.call-update) | async-done | bytes 393232 | tf_op jit(solution)/shard_map/reduce_scatter | solution.py:450
  1639.3 32.5 %reduce-scatter.58.cloned.1.call-done = bf16[192,6]{1,0:T(8,128)(2,1)} async-done(((bf16[1536,6]{1,0:T(8,128)(2,1)}), bf16[192,6]{1,0:T(8,128)(2,1)}) %reduce-scatter.58.cloned.1.call-update) | async-done | bytes 2320
  1673.3 77.5 %reduce-scatter.36.cloned.1.call-done = bf16[128,4096]{1,0:T(8,128)(2,1)} async-done(((bf16[512,4096]{1,0:T(8,128)(2,1)}), bf16[128,4096]{1,0:T(8,128)(2,1)}) %reduce-scatter.36.cloned.1.call-update) | async-done | bytes 1048592 | tf_op jit(solution)/shard_map/reduce_scatter | solution.py:201
  1750.9 2.8 convert_element_type.275
  (445 shorter events, 152.3 us)
Async XLA Ops:
  7.2 19.8 %copy-start.85 = (s32[3,512]{1,0:T(4,128)S(1)}, s32[3,512]{1,0:T(4,128)}, u32[]{:S(2)}) copy-start(s32[3,512]{1,0:T(4,128)} %param.21) | copy-start | bytes 18436
  7.2 19.8 %copy-start.102 = (bf16[3,64]{1,0:T(4,128)(2,1)S(1)}, bf16[3,64]{1,0:T(4,128)(2,1)}, u32[]{:S(2)}) copy-start(bf16[3,64]{1,0:T(4,128)(2,1)} %param.33) | copy-start | bytes 1156
  7.2 29.9 %all-gather.26.cloned.1.call-start = ((), (), s32[]{:S(2)}) async-start(), calls=%async_computation.22 | async-start | bytes 1327104 | tf_op jit(solution)/shard_map/all_gather | solution.py:238
  7.9 68.1 %all-gather.20.cloned.1.call-start = ((), (), s32[]{:S(2)}) async-start(), calls=%async_computation.19 | async-start | bytes 1966080 | tf_op jit(solution)/shard_map/all_gather | solution.py:148
  21.5 15.6 copy-start.86
  22.8 55.9 %copy-start.103 = (f32[128]{0:T(128)}, f32[128]{0:T(128)S(1)}, u32[]{:S(2)}) copy-start(f32[128]{0:T(128)S(1)} %multiply_reduce_fusion.24) | copy-start | bytes 1540
  22.9 14.3 copy-start.90
  25.0 75.9 %all-gather.24.cloned.1.call-start = ((), (), s32[]{:S(2)}) async-start(), calls=%async_computation.21 | async-start | bytes 1327104 | tf_op jit(solution)/shard_map/all_gather | solution.py:237
  25.7 101.0 %all-gather.22.cloned.1.call-start = ((), (), s32[]{:S(2)}) async-start(), calls=%async_computation.20 | async-start | bytes 1327104 | tf_op jit(solution)/shard_map/all_gather | solution.py:239
  26.3 126.2 %all-gather.28.cloned.1.call-start = ((), (), s32[]{:S(2)}) async-start(), calls=%async_computation.23 | async-start | bytes 1327104 | tf_op jit(solution)/shard_map/all_gather | solution.py:247
  26.9 190.2 %reduce-scatter.24.cloned.1.call-start = ((), (), s32[]{:S(2)}) async-start(), calls=%async_computation.24 | async-start | bytes 3932160 | tf_op jit(solution)/shard_map/reduce_scatter | solution.py:168
  36.4 79.0 %copy-start.70 = (f32[384]{0:T(512)}, f32[384]{0:T(512)S(1)}, u32[]{:S(2)}) copy-start(f32[384]{0:T(512)S(1)} %get-tuple-element.237) | copy-start | bytes 4612
  36.4 79.7 %copy-start.72 = (f32[384]{0:T(512)}, f32[384]{0:T(512)S(1)}, u32[]{:S(2)}) copy-start(f32[384]{0:T(512)S(1)} %get-tuple-element.238) | copy-start | bytes 4612
  37.1 79.7 %copy-start.41 = (f32[512,64]{0,1:T(8,128)}, f32[512,64]{0,1:T(8,128)S(1)}, u32[]{:S(2)}) copy-start(f32[512,64]{0,1:T(8,128)S(1)} %get-tuple-element.233) | copy-start | bytes 393220
  37.1 79.7 %copy-start.43 = (f32[512,64]{0,1:T(8,128)}, f32[512,64]{0,1:T(8,128)S(1)}, u32[]{:S(2)}) copy-start(f32[512,64]{0,1:T(8,128)S(1)} %get-tuple-element.234) | copy-start | bytes 393220
  76.0 24.8 %copy-start.107 = (bf16[512,1536]{1,0:T(8,128)(2,1)S(1)}, bf16[512,1536]{1,0:T(8,128)(2,1)}, u32[]{:S(2)}) copy-start(bf16[512,1536]{1,0:T(8,128)(2,1)} %all-gather.20.cloned.1.call-done) | copy-start | bytes 4718596
  78.7 37.3 %copy-start.13 = (f32[512,384]{0,1:T(8,128)}, f32[512,384]{0,1:T(8,128)S(1)}, u32[]{:S(2)}) copy-start(f32[512,384]{0,1:T(8,128)S(1)} %get-tuple-element.249) | copy-start | bytes 2359300
  103.0 13.7 copy-start.17
  123.4 6.0 copy-start.54
  156.6 94.7 %all-gather.32.cloned.1.call-start = ((), (), s32[]{:S(2)}) async-start(), calls=%async_computation.26 | async-start | bytes 3538944 | tf_op jit(solution)/shard_map/all_gather | solution.py:242
  157.4 176.3 %all-gather.30.cloned.1.call-start = ((), (), s32[]{:S(2)}) async-start(), calls=%async_computation.25 | async-start | bytes 5242880 | tf_op jit(solution)/shard_map/all_gather | solution.py:255
  158.1 208.3 %all-gather.38.cloned.1.call-start = ((), (), s32[]{:S(2)}) async-start(), calls=%async_computation.29 | async-start | bytes 3538944 | tf_op jit(solution)/shard_map/all_gather | solution.py:241
  158.9 233.4 %all-gather.36.cloned.1.call-start = ((), (), s32[]{:S(2)}) async-start(), calls=%async_computation.28 | async-start | bytes 1327104 | tf_op jit(solution)/shard_map/all_gather | solution.py:240
  159.5 272.1 %all-gather.34.cloned.1.call-start = ((), (), s32[]{:S(2)}) async-start(), calls=%async_computation.27 | async-start | bytes 1966080 | tf_op jit(solution)/shard_map/all_gather | solution.py:148
  220.9 235.3 %all-gather.40.cloned.1.call-start = ((), (), s32[]{:S(2)}) async-start(), calls=%async_computation.30 | async-start | bytes 1327104 | tf_op jit(solution)/shard_map/all_gather | solution.py:248
  221.5 299.4 %reduce-scatter.26.cloned.1.call-start = ((), (), s32[]{:S(2)}) async-start(), calls=%async_computation.31 | async-start | bytes 3932160 | tf_op jit(solution)/shard_map/reduce_scatter | solution.py:168
  460.4 111.1 %all-gather.44.cloned.1.call-start = ((), (), s32[]{:S(2)}) async-start(), calls=%async_computation.33 | async-start | bytes 7962624 | tf_op jit(solution)/shard_map/all_gather | solution.py:243
  461.0 149.6 %all-gather.42.cloned.1.call-start = ((), (), s32[]{:S(2)}) async-start(), calls=%async_computation.32 | async-start | bytes 1966080 | tf_op jit(solution)/shard_map/all_gather | solution.py:148
  524.7 135.4 %all-gather.46.cloned.1.call-start = ((), (), s32[]{:S(2)}) async-start(), calls=%async_computation.34 | async-start | bytes 7962624 | tf_op jit(solution)/shard_map/all_gather | solution.py:249
  525.3 205.6 %reduce-scatter.28.cloned.1.call-start = ((), (), s32[]{:S(2)}) async-start(), calls=%async_computation.35 | async-start | bytes 3932160 | tf_op jit(solution)/shard_map/reduce_scatter | solution.py:168
  670.5 101.1 %all-gather.48.cloned.1.call-start = ((), (), s32[]{:S(2)}) async-start(), calls=%async_computation.36 | async-start | bytes 1966080 | tf_op jit(solution)/shard_map/all_gather | solution.py:152
  734.3 117.9 %reduce-scatter.30.cloned.1.call-start = ((), (), s32[]{:S(2)}) async-start(), calls=%async_computation.37 | async-start | bytes 3932160 | tf_op jit(solution)/shard_map/reduce_scatter | solution.py:188
  793.0 103.1 %all-gather.50.cloned.1.call-start = ((), (), s32[]{:S(2)}) async-start(), calls=%async_computation.38 | async-start | bytes 1966080 | tf_op jit(solution)/shard_map/all_gather | solution.py:152
  852.2 5.6 copy-start.9
  858.7 121.6 %reduce-scatter.32.cloned.1.call-start = ((), (), s32[]{:S(2)}) async-start(), calls=%async_computation.39 | async-start | bytes 3932160 | tf_op jit(solution)/shard_map/reduce_scatter | solution.py:188
  921.6 103.5 %all-gather.52.cloned.1.call-start = ((), (), s32[]{:S(2)}) async-start(), calls=%async_computation.40 | async-start | bytes 1966080 | tf_op jit(solution)/shard_map/all_gather | solution.py:152
  987.8 148.1 %reduce-scatter.34.cloned.1.call-start = ((), (), s32[]{:S(2)}) async-start(), calls=%async_computation.41 | async-start | bytes 3932160 | tf_op jit(solution)/shard_map/reduce_scatter | solution.py:188
  1035.6 5.4 copy-start.14
  1035.6 5.4 copy-start.18
  1035.6 5.4 copy-start.67
  1035.6 5.4 copy-start.69
  1039.3 14.0 copy-start.73
  1039.3 14.2 copy-start.71
  1059.9 127.7 %reduce-scatter.56.cloned.1.call-start = ((), (), s32[]{:S(2)}) async-start(), calls=%async_computation.52 | async-start | bytes 7962624 | tf_op jit(solution)/shard_map/reduce_scatter | solution.py:470
  1069.9 187.1 %reduce-scatter.54.cloned.1.call-start = ((), (), s32[]{:S(2)}) async-start(), calls=%async_computation.51 | async-start | bytes 7962624 | tf_op jit(solution)/shard_map/reduce_scatter | solution.py:456
  1079.0 217.9 %reduce-scatter.52.cloned.1.call-start = ((), (), s32[]{:S(2)}) async-start(), calls=%async_computation.50 | async-start | bytes 1327104 | tf_op jit(solution)/shard_map/reduce_scatter | solution.py:467
  1082.6 254.5 %reduce-scatter.46.cloned.1.call-start = ((), (), s32[]{:S(2)}) async-start(), calls=%async_computation.47 | async-start | bytes 1327104 | tf_op jit(solution)/shard_map/reduce_scatter | solution.py:447
  1086.3 300.4 %reduce-scatter.50.cloned.1.call-start = ((), (), s32[]{:S(2)}) async-start(), calls=%async_computation.49 | async-start | bytes 3538944 | tf_op jit(solution)/shard_map/reduce_scatter | solution.py:453
  1093.8 5.3 copy-start.37
  1093.8 5.3 copy-start.108
  1093.8 330.2 %reduce-scatter.60.cloned.1.call-start = ((), (), s32[]{:S(2)}) async-start(), calls=%async_computation.54 | async-start | bytes 147456
  1095.3 368.6 %reduce-scatter.44.cloned.1.call-start = ((), (), s32[]{:S(2)}) async-start(), calls=%async_computation.46 | async-start | bytes 1327104 | tf_op jit(solution)/shard_map/reduce_scatter | solution.py:464
  1099.1 405.1 %reduce-scatter.42.cloned.1.call-start = ((), (), s32[]{:S(2)}) async-start(), calls=%async_computation.45 | async-start | bytes 1327104 | tf_op jit(solution)/shard_map/reduce_scatter | solution.py:444
  1101.2 443.0 %reduce-scatter.40.cloned.1.call-start = ((), (), s32[]{:S(2)}) async-start(), calls=%async_computation.44 | async-start | bytes 1327104 | tf_op jit(solution)/shard_map/reduce_scatter | solution.py:441
  1104.8 480.2 %reduce-scatter.38.cloned.1.call-start = ((), (), s32[]{:S(2)}) async-start(), calls=%async_computation.43 | async-start | bytes 1327104 | tf_op jit(solution)/shard_map/reduce_scatter | solution.py:438
  1108.5 526.1 %reduce-scatter.48.cloned.1.call-start = ((), (), s32[]{:S(2)}) async-start(), calls=%async_computation.48 | async-start | bytes 3538944 | tf_op jit(solution)/shard_map/reduce_scatter | solution.py:450
  1114.5 557.3 %reduce-scatter.58.cloned.1.call-start = ((), (), s32[]{:S(2)}) async-start(), calls=%async_computation.53 | async-start | bytes 442368
  1127.2 8.7 copy-start.5
  1127.2 8.7 copy-start.87
  1127.2 8.7 copy-start.91
  1155.4 595.5 %reduce-scatter.36.cloned.1.call-start = ((), (), s32[]{:S(2)}) async-start(), calls=%async_computation.42 | async-start | bytes 5242880 | tf_op jit(solution)/shard_map/reduce_scatter | solution.py:201
  1259.5 378.4 %copy-start.104 = (f32[128]{0:T(128)S(1)}, f32[128]{0:T(128)}, u32[]{:S(2)}) copy-start(f32[128]{0:T(128)} %copy-done.103) | copy-start | bytes 1540
  1259.5 378.4 %copy-start.28 = (f32[128,1536]{1,0:T(8,128)S(1)}, f32[128,1536]{1,0:T(8,128)}, u32[]{:S(2)}) copy-start(f32[128,1536]{1,0:T(8,128)} %reduce-scatter.34.cloned.1.call-done) | copy-start | bytes 2359300
  1338.7 299.5 %copy-start.8 = (f32[128,1536]{1,0:T(8,128)S(1)}, f32[128,1536]{1,0:T(8,128)}, u32[]{:S(2)}) copy-start(f32[128,1536]{1,0:T(8,128)} %copy-done.7) | copy-start | bytes 2359300
  (86 other events, 175.2 us)
Sparse Core Ops, SparseCore 0:
  9.9 26.7 all-gather.25
  38.9 37.0 all-gather.19
  77.9 22.9 all-gather.23
  102.6 24.0 all-gather.21
  128.4 24.0 all-gather.27
  156.8 60.2 reduce-scatter.23
  218.9 32.3 all-gather.31
  252.9 80.7 all-gather.29
  335.6 30.8 all-gather.37
  368.2 24.0 all-gather.35
  394.4 37.0 all-gather.33
  433.3 22.9 all-gather.39
  460.6 60.2 reduce-scatter.25
  522.6 48.8 all-gather.43
  573.5 37.0 all-gather.41
  612.4 47.7 all-gather.45
  670.6 60.2 reduce-scatter.27
  734.4 37.1 all-gather.47
  793.1 59.0 reduce-scatter.29
  858.9 37.1 all-gather.49
  921.7 58.5 reduce-scatter.31
  987.9 37.0 all-gather.51
  1060.0 58.5 reduce-scatter.33
  1122.0 65.5 reduce-scatter.55
  1191.5 65.4 reduce-scatter.53
  1260.1 36.7 reduce-scatter.51
  1300.3 36.7 reduce-scatter.45
  1340.5 46.2 reduce-scatter.49
  1390.6 33.3 reduce-scatter.59
  1427.0 36.7 reduce-scatter.43
  1467.4 36.7 reduce-scatter.41
  1507.4 36.7 reduce-scatter.39
  1548.2 36.7 reduce-scatter.37
  1588.4 46.2 reduce-scatter.47
  1638.0 33.8 reduce-scatter.57
  1674.1 76.7 reduce-scatter.35
where the time goes:
time: 1770 us; the launch traced here: 1760 us
  waiting for transfers between devices  1360 us (77%)
  matrix products  163 us (9%)
  blocking collectives  105 us (6%)
  other arithmetic  78.9 us (4%)
  local copies, waits for them, and re-layouts  32.9 us (2%)
    reduce_scatter x3, waiting for transfers between devices, scatter_branch(): lax.psum_scatter(term(jnp.int32(0), rows * lax.axis_size('tensor')), 'ten...  162 us
    reduce_scatter x3, waiting for transfers between devices, scatter_grads(): lax.psum_scatter(term(jnp.int32(0), rows * lax.axis_size('tensor')), 'ten...  118 us
    all_gather x3, waiting for transfers between devices, gather_sequence(): return lax.all_gather(values, 'tensor', axis=0, tiled=True)  117 us
    all_gather x3, waiting for transfers between devices, gather_grads(): return lax.all_gather(values, 'tensor', axis=0, tiled=True)  104 us
    all_gather x1, waiting for transfers between devices, body(): text_all = lax.all_gather(text_states, 'tensor', axis=0, tiled=True)  82.4 us
    reduce_scatter x1, waiting for transfers between devices, scatter_text(): lax.psum_scatter(term(jnp.int32(0), lax.axis_size('tensor') * rows).astyp...  77.5 us
    unnamed x38, waiting for transfers between devices  74.7 us
    reduce_scatter x1, waiting for transfers between devices, body(): lax.psum_scatter(grad_up.astype(jnp.bfloat16), 'dp', scatter_dimension=0,...  67 us
  transfers between devices with their start and end apart: 36, of which 34 were waited for; matrix products, arithmetic and copies ran while one was open for 9% of the time, Pallas kernels for 0%

commit v1 on v0

v1 whole, which is shorter than its diff:
```python
import functools

import jax
import jax.numpy as jnp
from jax import lax
from jax.experimental import pallas as pl
from jax.experimental.pallas import tpu as pltpu
from jax.sharding import PartitionSpec as P

MESH = pl.DeviceIdType.MESH
VMEM_BYTES = 60 * 2**20

HEAD_DIM = 128
D = 1536


EPSILON = 1e-06
CONTRACT_LAST = (((1,), (1,)), ((), ()))
CONTRACT_FIRST = (((0,), (0,)), ((), ()))


def layer_norm(values):
    center = values - jnp.mean(values, axis=-1, keepdims=True)
    spread = jnp.mean(center * center, axis=-1, keepdims=True)
    return center * lax.rsqrt(spread + EPSILON)


def modulate(values, shift, scale):
    return layer_norm(values) * (1.0 + scale) + shift


def gained_norm(values, weight):
    return layer_norm(values) * weight


def scaled(values, total, gain):
    return values * lax.rsqrt(total[:, None] / D + EPSILON) * gain


def gelu_tanh(values):
    return jax.nn.gelu(values, approximate=True)


def rotary_tables(positions, head_width):
    pairs = head_width // 2
    third = pairs // 3
    first = pairs - 2 * third
    freq_frame = jnp.power(10000.0, -jnp.arange(first, dtype=jnp.float32) / first)
    freq_side = jnp.power(10000.0, -jnp.arange(third, dtype=jnp.float32) / third)
    places = positions.astype(jnp.float32)
    angles = jnp.concatenate(
        [
            places[0][:, None] * freq_frame[None, :],
            places[1][:, None] * freq_side[None, :],
            places[2][:, None] * freq_side[None, :],
        ],
        axis=1,
    )
    return (jnp.cos(angles), jnp.sin(angles))


def rotate(values, cosine, sine):
    shape = values.shape
    paired = values.reshape(shape[0], shape[1], shape[2] // 2, 2)
    real_part = paired[..., 0]
    imag_part = paired[..., 1]
    cos_row = cosine[:, None, :]
    sin_row = sine[:, None, :]
    turned = jnp.stack(
        [real_part * cos_row - imag_part * sin_row, real_part * sin_row + imag_part * cos_row],
        axis=-1,
    )
    return turned.reshape(shape)


def product_back(grads, weight):
    return lax.dot_general(grads, weight, CONTRACT_LAST, preferred_element_type=jnp.float32)


def weight_grad(inputs, grads):
    return lax.dot_general(inputs, grads, CONTRACT_FIRST, preferred_element_type=jnp.float32)


def attend_forward(queries, keys, values):
    rows, heads, width = queries.shape
    block = min(512, rows)
    scale = width ** (-0.5)

    def one_block(query_block):
        scores = (
            jnp.einsum("qhd,khd->hqk", query_block, keys, preferred_element_type=jnp.float32)
            * scale
        )
        top = jnp.max(scores, axis=-1, keepdims=True)
        expo = jnp.exp(scores - top)
        summed = jnp.sum(expo, axis=-1, keepdims=True)
        probs = expo / summed
        result = jnp.einsum(
            "hqk,khd->qhd", probs.astype(jnp.bfloat16), values, preferred_element_type=jnp.float32
        )
        return (result, top[..., 0] + jnp.log(summed[..., 0]))

    result, logsum = lax.map(one_block, queries.reshape(rows // block, block, heads, width))
    return (result.reshape(rows, heads, width), logsum)


def attend_backward(queries, keys, values, logsum, grad_out):
    rows, heads, width = queries.shape
    block = min(512, rows)
    count = rows // block
    scale = width ** (-0.5)

    def one_block(carry, item):
        key_grad, value_grad = carry
        query_block, grad_block, logsum_block = item
        scores = (
            jnp.einsum("qhd,khd->hqk", query_block, keys, preferred_element_type=jnp.float32)
            * scale
        )
        probs = jnp.exp(scores - logsum_block[..., None])
        prob_grad = jnp.einsum(
            "qhd,khd->hqk", grad_block, values, preferred_element_type=jnp.float32
        )
        inner = jnp.sum(prob_grad * probs, axis=-1, keepdims=True)
        score_grad = (probs * (prob_grad - inner)).astype(jnp.bfloat16)
        query_grad = (
            jnp.einsum("hqk,khd->qhd", score_grad, keys, preferred_element_type=jnp.float32) * scale
        )
        key_grad = (
            key_grad
            + jnp.einsum(
                "hqk,qhd->khd", score_grad, query_block, preferred_element_type=jnp.float32
            )
            * scale
        )
        value_grad = value_grad + jnp.einsum(
            "hqk,qhd->khd",
            probs.astype(jnp.bfloat16),
            grad_block,
            preferred_element_type=jnp.float32,
        )
        return ((key_grad, value_grad), query_grad)

    start_carry = (jnp.zeros(keys.shape, jnp.float32), jnp.zeros(values.shape, jnp.float32))
    items = (
        queries.reshape(count, block, heads, width),
        grad_out.reshape(count, block, heads, width),
        logsum,
    )
    (key_grad, value_grad), query_grad = lax.scan(one_block, start_carry, items)
    return (query_grad.reshape(rows, heads, width), key_grad, value_grad)


def when(cond, run):
    if cond is None:
        run()
    else:
        pl.when(cond)(run)


def flip(index, bit):
    return index + bit - 2 * bit * (index // bit % 2)


def normed(values):
    center = values - jnp.mean(values, axis=-1, keepdims=True)
    inverse = lax.rsqrt(jnp.mean(center * center, axis=-1, keepdims=True) + EPSILON)
    return center * inverse, inverse


def normed_back(unit, inverse, grad):
    mean_grad = jnp.mean(grad, axis=-1, keepdims=True)
    mean_dot = jnp.mean(grad * unit, axis=-1, keepdims=True)
    return (grad - mean_grad - unit * mean_dot) * inverse


class Links:
    def __init__(self, send, recv, local, dp_size, tensor_size):
        self.send, self.recv, self.local = send, recv, local
        self.count = 0
        self.local_count = 0
        self.dp_size, self.size = dp_size, tensor_size
        self.dp = lax.axis_index("dp")
        self.z = lax.axis_index("tensor")

    def slot(self):
        self.count += 1
        return self.count - 1

    def copy(self, source, target, device, slot):
        return pltpu.make_async_remote_copy(
            src_ref=source,
            dst_ref=target,
            send_sem=self.send.at[slot],
            recv_sem=self.recv.at[slot],
            device_id=device,
            device_id_type=MESH,
        )

    def here(self, source, target):
        self.local_count += 1
        return pltpu.make_async_copy(source, target, self.local.at[self.local_count - 1])

    def greet(self, groups):
        barrier = pltpu.get_barrier_semaphore()
        peers = []
        if "line" in groups:
            peers += [
                ((self.dp, self.z - 1), self.z > 0),
                ((self.dp, self.z + 1), self.z < self.size - 1),
            ]
        if "zall" in groups:
            peers += [
                ((self.dp, lax.rem(self.z + k, self.size)), None) for k in range(1, self.size)
            ]
        if "dpall" in groups:
            peers += [
                ((lax.rem(self.dp + k, self.dp_size), self.z), None)
                for k in range(1, self.dp_size)
            ]
        if "bits" in groups:
            bit = 1
            while bit < self.dp_size:
                peers.append(((flip(self.dp, bit), self.z), None))
                bit *= 2
        if "diag" in groups:
            peers.append(((flip(flip(self.dp, 2), 4), self.z), None))
        for device, cond in peers:
            when(
                cond,
                lambda device=device: pl.semaphore_signal(
                    barrier, inc=1, device_id=device, device_id_type=MESH
                ),
            )
        expected = sum(1 for _, cond in peers if cond is None)
        for _, cond in peers:
            if cond is not None:
                expected = expected + cond.astype(jnp.int32)
        pl.semaphore_wait(barrier, expected)


def piece_of(ref, block, rows, start, count):
    return ref.at[pl.ds(pl.multiple_of(block * rows + start, 16), count)]


class LineGather:
    def __init__(self, links, whole, rows, pieces):
        self.links, self.whole, self.rows, self.count = links, whole, rows, rows // pieces
        self.pieces = pieces
        hops = links.size - 1
        self.right = [[links.slot() for _ in range(pieces)] for _ in range(hops)]
        self.left = [[links.slot() for _ in range(pieces)] for _ in range(hops)]

    def block(self, index, piece):
        return piece_of(self.whole, index, self.rows, piece * self.count, self.count)

    def move(self, index, piece, way, slot):
        part = self.block(index, piece)
        return self.links.copy(part, part, (self.links.dp, self.links.z + way), slot)

    def start(self, piece):
        z, last = self.links.z, self.links.size - 1
        when(z < last, lambda: self.move(z, piece, 1, self.right[0][piece]).start())
        when(z > 0, lambda: self.move(z, piece, -1, self.left[0][piece]).start())

    def step(self, hop, piece):
        z, last = self.links.z, self.links.size - 1

        def from_left():
            self.move(z - 1 - hop, piece, -1, self.right[hop][piece]).wait_recv()
            if hop + 1 < last:
                when(
                    z < last,
                    lambda: self.move(z - 1 - hop, piece, 1, self.right[hop + 1][piece]).start(),
                )

        def from_right():
            self.move(z + 1 + hop, piece, 1, self.left[hop][piece]).wait_recv()
            if hop + 1 < last:
                when(
                    z > 0,
                    lambda: self.move(z + 1 + hop, piece, -1, self.left[hop + 1][piece]).start(),
                )

        when(z - 1 - hop >= 0, from_left)
        when(z + 1 + hop <= last, from_right)

    def steps(self, piece):
        for hop in range(self.links.size - 1):
            self.step(hop, piece)

    def finish(self):
        z, last = self.links.z, self.links.size - 1
        for hop in range(last):
            for piece in range(self.pieces):
                when(
                    (z - hop >= 0) & (z < last),
                    lambda: self.move(z - hop, piece, 1, self.right[hop][piece]).wait_send(),
                )
                when(
                    (z + hop <= last) & (z > 0),
                    lambda: self.move(z + hop, piece, -1, self.left[hop][piece]).wait_send(),
                )


class LineReduce:
    def __init__(self, links, partial, land_right, land_left, rows, pieces):
        self.links, self.partial, self.rows, self.count = links, partial, rows, rows // pieces
        self.land = {1: land_right, -1: land_left}
        self.pieces = pieces
        last = links.size - 1
        self.slots = {
            way: [None] + [[links.slot() for _ in range(pieces)] for _ in range(last)]
            for way in (1, -1)
        }

    def landing(self, way, distance, piece):
        return self.land[way].at[distance - 1, pl.ds(piece * self.count, self.count)]

    def part(self, index, piece):
        return piece_of(self.partial, index, self.rows, piece * self.count, self.count)

    def move(self, source, way, distance, piece):
        return self.links.copy(
            source,
            self.landing(way, distance, piece),
            (self.links.dp, self.links.z + way),
            self.slots[way][distance][piece],
        )

    def arrived(self, way, distance, piece):
        self.links.copy(
            self.landing(way, distance, piece),
            self.landing(way, distance, piece),
            (self.links.dp, self.links.z - way),
            self.slots[way][distance][piece],
        ).wait_recv()

    def first(self, piece):
        z, last = self.links.z, self.links.size - 1

        def from_first():
            for distance in range(last, 0, -1):
                self.move(self.part(distance, piece), 1, distance, piece).start()

        def from_last():
            for distance in range(last, 0, -1):
                self.move(self.part(last - distance, piece), -1, distance, piece).start()

        when(z == 0, from_first)
        when(z == last, from_last)

    def clear(self):
        z, last = self.links.z, self.links.size - 1

        def zero(way):
            self.land[way][0] = jnp.zeros(self.land[way].shape[1:], self.land[way].dtype)

        when(z == 0, lambda: zero(1))
        when(z == last, lambda: zero(-1))

    def step(self, piece):
        z, last = self.links.z, self.links.size - 1
        for distance in range(last - 1, 0, -1):
            for way in (1, -1):
                inside = (
                    (z > 0) & (z + distance <= last)
                    if way == 1
                    else (z < last) & (z - distance >= 0)
                )

                def go(way=way, distance=distance):
                    self.arrived(way, distance + 1, piece)
                    held = self.landing(way, distance + 1, piece)
                    own = self.part(z + way * distance, piece)
                    held[...] = (
                        held[...].astype(jnp.float32) + own[...].astype(jnp.float32)
                    ).astype(held.dtype)
                    self.move(held, way, distance, piece).start()

                when(inside, go)

    def total(self, piece):
        z, last = self.links.z, self.links.size - 1
        when(z > 0, lambda: self.arrived(1, 1, piece))
        when(z < last, lambda: self.arrived(-1, 1, piece))
        return (
            self.part(z, piece)[...].astype(jnp.float32)
            + self.landing(1, 1, piece)[...].astype(jnp.float32)
            + self.landing(-1, 1, piece)[...].astype(jnp.float32)
        )

    def finish(self):
        z, last = self.links.z, self.links.size - 1
        for distance in range(1, last + 1):
            for piece in range(self.pieces):
                held = self.landing(1, distance, piece)
                when(
                    z + distance <= last,
                    lambda: self.move(held, 1, distance, piece).wait_send(),
                )
                back = self.landing(-1, distance, piece)
                when(
                    z - distance >= 0,
                    lambda: self.move(back, -1, distance, piece).wait_send(),
                )


class CubeGather:
    def __init__(self, links, shard, whole):
        self.links, self.shard, self.whole = links, shard, whole
        self.rows = shard.shape[0]
        self.slots = [links.slot() for _ in range(8)]
        dp = links.dp
        self.core, self.side, self.over = flip(dp, 1), flip(dp, 2), flip(dp, 4)
        self.far = flip(flip(dp, 2), 4)
        self.sent = []

    def block(self, index, start=0, count=None):
        return piece_of(self.whole, index, self.rows, start, count or self.rows)

    def send(self, source, target, device, slot):
        move = self.links.copy(source, target, (device, self.links.z), self.slots[slot])
        move.start()
        self.sent.append(move)

    def got(self, part, slot):
        self.links.copy(part, part, (self.core, self.links.z), self.slots[slot]).wait_recv()

    def start(self):
        mine = self.block(self.links.dp)
        self.own = self.links.here(self.shard, mine)
        self.own.start()
        self.send(self.shard, mine, self.side, 1)
        self.send(self.shard, mine, self.over, 2)
        self.send(self.shard, mine, self.core, 0)

    def forward(self):
        half = self.rows // 2
        self.got(self.block(self.side), 1)
        part = self.block(self.side, 0, half)
        self.send(part, part, self.over, 3)
        part = self.block(self.side)
        self.send(part, part, self.core, 5)
        self.got(self.block(self.over), 2)
        part = self.block(self.over, half, half)
        self.send(part, part, self.side, 4)
        part = self.block(self.over)
        self.send(part, part, self.core, 6)

    def tail(self):
        half = self.rows // 2
        self.got(self.block(self.far, 0, half), 3)
        self.got(self.block(self.far, half, half), 4)
        part = self.block(self.far)
        self.send(part, part, self.core, 7)

    def finish(self):
        self.got(self.block(self.core), 0)
        self.got(self.block(flip(self.core, 2)), 5)
        self.got(self.block(flip(self.core, 4)), 6)
        self.got(self.block(flip(flip(self.core, 2), 4)), 7)
        for move in self.sent:
            move.wait_send()
        self.own.wait()


class CubeReduce:
    def __init__(self, links, grads, out, own, near, others):
        self.links, self.grads, self.out = links, grads, out
        self.own, self.near, self.others = own, near, others
        self.rows = out.shape[0]
        self.core_slots = [links.slot() for _ in range(4)]
        self.chip_slots = [links.slot() for _ in range(3)]
        self.core = links.dp % 2
        self.chip = links.dp // 2
        self.sent = []

    def block(self, chip, core):
        return piece_of(self.grads, 2 * chip + core, self.rows, 0, self.rows)

    def chips(self):
        return [flip(self.chip, 1), flip(self.chip, 2), flip(flip(self.chip, 1), 2)]

    def start(self):
        links = self.links
        self.copies = []
        for chip in range(4):
            local = links.here(self.block(chip, self.core), self.own.at[chip])
            local.start()
            move = links.copy(
                self.block(chip, 1 - self.core),
                self.near.at[chip],
                (flip(links.dp, 1), links.z),
                self.core_slots[chip],
            )
            move.start()
            self.copies.append((local, move))

    def middle(self):
        links = self.links
        for local, move in self.copies:
            local.wait()
            move.wait_recv()

        def add(step, _):
            rows = pl.ds(pl.multiple_of(step * 16, 16), 16)
            for chip in range(4):
                self.near[chip, rows, :] = (
                    self.near[chip, rows, :].astype(jnp.float32)
                    + self.own[chip, rows, :].astype(jnp.float32)
                ).astype(jnp.bfloat16)
            return 0

        lax.fori_loop(0, self.rows // 16, add, 0)
        for index, chip in enumerate(self.chips()):
            move = links.copy(
                self.near.at[chip],
                self.others.at[index],
                (2 * chip + self.core, links.z),
                self.chip_slots[index],
            )
            move.start()
            self.sent.append(move)

    def finish(self):
        for move in self.sent:
            move.wait_recv()

        def add(step, _):
            rows = pl.ds(pl.multiple_of(step * 16, 16), 16)
            self.out[rows, :] = (
                self.near[self.chip, rows, :].astype(jnp.float32)
                + self.others[0, rows, :].astype(jnp.float32)
                + self.others[1, rows, :].astype(jnp.float32)
                + self.others[2, rows, :].astype(jnp.float32)
            )
            return 0

        lax.fori_loop(0, self.rows // 16, add, 0)
        for move in self.sent:
            move.wait_send()
        for _, move in self.copies:
            move.wait_send()


def cube_scratch(shapes):
    parts = []
    for rows, columns in shapes:
        parts += [
            pltpu.VMEM((4, rows, columns), jnp.bfloat16),
            pltpu.VMEM((4, rows, columns), jnp.bfloat16),
            pltpu.VMEM((3, rows, columns), jnp.bfloat16),
        ]
    return parts


class Plan:
    def __init__(self, mesh):
        self.dp = mesh.shape["dp"]
        self.tensor = mesh.shape["tensor"]
        self.cube = self.dp == 8
        self.calls = 0

    def call(self, name, body, inputs, outputs, scratch, copies):
        self.calls += 1
        spaces = {True: pltpu.VMEM, False: pltpu.HBM}
        count_in, count_out = len(inputs), len(outputs)

        def kernel(*refs):
            ins = refs[:count_in]
            outs = refs[count_in : count_in + count_out]
            rest = refs[count_in + count_out :]
            links = Links(rest[0], rest[1], rest[2], self.dp, self.tensor)
            body(links, ins, outs, rest[3:])

        return pl.pallas_call(
            kernel,
            name=name,
            out_shape=[jax.ShapeDtypeStruct(shape, kind) for shape, kind, _ in outputs],
            in_specs=[pl.BlockSpec(memory_space=spaces[near]) for _, near in inputs],
            out_specs=[pl.BlockSpec(memory_space=spaces[near]) for _, _, near in outputs],
            scratch_shapes=[
                pltpu.SemaphoreType.DMA((copies,)),
                pltpu.SemaphoreType.DMA((copies,)),
                pltpu.SemaphoreType.DMA((64,)),
                *scratch,
            ],
            compiler_params=pltpu.CompilerParams(
                collective_id=self.calls, has_side_effects=True, vmem_limit_bytes=VMEM_BYTES
            ),
        )(*[array for array, _ in inputs])

    def gather_outputs(self, shards):
        return [
            ((self.dp * shard.shape[0], shard.shape[1]), shard.dtype, False) for shard in shards
        ]

    def open(self, hidden, time_rows, small, shards):
        rows, width = hidden.shape
        part = width // self.dp
        gain_part = small.shape[1] - part
        moving = shards if self.cube else []

        def body(links, ins, outs, scratch):
            hidden_ref, time_ref, small_ref = ins[:3]
            table_ref, gain_ref, whole_ref = outs[:3]
            (land,) = scratch
            links.greet({"line", "dpall"})
            gathers = [CubeGather(links, a, b) for a, b in zip(ins[3:], outs[3:])]
            dp, z = links.dp, links.z
            moves = []
            for step in range(1, self.dp):
                target = lax.rem(dp + step, self.dp)
                move = links.copy(small_ref, land.at[dp], (target, z), links.slot())
                move.start()
                moves.append(move)
            for item in gathers:
                item.start()
            land[dp] = small_ref[...]
            unit, _ = normed(hidden_ref[...])
            for move in moves:
                move.wait_recv()
            table = jnp.concatenate([land[k][:, :part] for k in range(self.dp)], axis=1)
            gain_ref[...] = jnp.concatenate([land[k][:, part:] for k in range(self.dp)], axis=1)
            table = table + time_ref[...]
            table_ref[...] = table
            line = LineGather(links, whole_ref, rows, 4)
            first = unit * (1.0 + table[1:2]) + table[0:1]
            whole_ref[pl.ds(pl.multiple_of(z * rows, 16), rows), :] = first.astype(jnp.bfloat16)
            for piece in range(4):
                line.start(piece)
            for piece in range(4):
                line.steps(piece)
                if piece < len(gathers):
                    gathers[piece].forward()
            for item in gathers[4:]:
                item.forward()
            for item in gathers:
                item.tail()
            for item in gathers:
                item.finish()
            line.finish()
            for move in moves:
                move.wait_send()

        results = self.call(
            "open",
            body,
            [(hidden, True), (time_rows, True), (small, True)] + [(s, False) for s in moving],
            [
                ((8, width), jnp.float32, True),
                ((8, gain_part * self.dp), jnp.float32, True),
                ((rows * self.tensor, width), jnp.bfloat16, True),
            ]
            + self.gather_outputs(moving),
            [pltpu.VMEM((self.dp, 8, small.shape[1]), jnp.float32)],
            160,
        )
        return results[:3], self.gathered(results[3:], shards)

    def gathered(self, moved, shards):
        if self.cube:
            return list(moved)
        return [lax.all_gather(shard, "dp", axis=0, tiled=True) for shard in shards]

    def reduced(self, moved, grads):
        if self.cube:
            return list(moved)
        return [
            lax.psum_scatter(grad, "dp", scatter_dimension=0, tiled=True).astype(jnp.float32)
            for grad in grads
        ]

    def between(self, name, partial, near, kinds, post, gather, shards=(), grads=(), extra=None):
        width = partial.shape[1]
        rows = partial.shape[0] // self.tensor
        pieces = 4
        shards, grads = list(shards), list(grads)
        moving = shards if self.cube else []
        summing = grads if self.cube else []
        count_near, count_kinds = len(near), len(kinds)
        lands = 2 if extra is None else 4
        sums = [(g.shape[0] // self.dp, g.shape[1]) for g in summing]

        def body(links, ins, outs, scratch):
            partial_ref = ins[0]
            ins = ins[1:]
            if extra is not None:
                second_ref = ins[0]
                ins = ins[1:]
            near_refs = ins[:count_near]
            shard_refs = ins[count_near : count_near + len(moving)]
            grad_refs = ins[count_near + len(moving) :]
            kind_refs = outs[:count_kinds]
            outs = outs[count_kinds:]
            if gather:
                whole_ref = outs[0]
                outs = outs[1:]
            full_refs = outs[: len(moving)]
            sum_refs = outs[len(moving) :]
            groups = {"line"}
            if moving or summing:
                groups |= {"bits"}
            if summing:
                groups |= {"diag"}
            links.greet(groups)
            reduce = LineReduce(links, partial_ref, scratch[0], scratch[1], rows, pieces)
            later = (
                LineReduce(links, second_ref, scratch[2], scratch[3], rows, pieces)
                if extra is not None
                else None
            )
            line = LineGather(links, whole_ref, rows, pieces) if gather else None
            gathers = [CubeGather(links, a, b) for a, b in zip(shard_refs, full_refs)]
            reduces = [
                CubeReduce(links, g, o, *scratch[lands + 3 * k : lands + 3 * k + 3])
                for k, (g, o) in enumerate(zip(grad_refs, sum_refs))
            ]
            for piece in range(pieces):
                reduce.first(piece)
            for item in reduces:
                item.start()
            for item in gathers:
                item.start()
            reduce.clear()
            if later is not None:
                later.clear()
            for piece in range(pieces):
                reduce.step(piece)
                where = pl.ds(piece * (rows // pieces), rows // pieces)
                result = post(reduce.total(piece), where, near_refs, kind_refs, piece == 0)
                if gather:
                    line.block(links.z, piece)[...] = result
                    line.start(piece)
                    if piece > 0:
                        line.steps(piece - 1)
                if later is not None:
                    later.first(piece)
                if piece == 0:
                    for item in reduces:
                        item.middle()
                if piece == 2:
                    for item in gathers:
                        item.forward()
            if gather:
                line.steps(pieces - 1)
            if later is not None:
                for piece in range(pieces):
                    later.step(piece)
                    where = pl.ds(piece * (rows // pieces), rows // pieces)
                    extra[1](later.total(piece), where, near_refs, kind_refs, piece == 0)
            for item in gathers:
                item.tail()
            for item in gathers:
                item.finish()
            for item in reduces:
                item.finish()
            reduce.finish()
            if later is not None:
                later.finish()
            if gather:
                line.finish()

        inputs = [(partial, True)]
        if extra is not None:
            inputs.append((extra[0], True))
        inputs += [(item, True) for item in near]
        inputs += [(item, False) for item in moving + summing]
        outputs = [(shape, jnp.float32, True) for shape in kinds]
        if gather:
            outputs.append((partial.shape, jnp.bfloat16, True))
        outputs += self.gather_outputs(moving)
        outputs += [(shape, jnp.float32, True) for shape in sums]
        results = self.call(
            name,
            body,
            inputs,
            outputs,
            [pltpu.VMEM((self.tensor - 1, rows, width), jnp.bfloat16) for _ in range(lands)]
            + cube_scratch(sums),
            200,
        )
        kept = count_kinds + (1 if gather else 0)
        full = self.gathered(results[kept : kept + len(moving)], shards)
        summed = self.reduced(results[kept + len(moving) :], grads)
        return results[:kept], full, summed

    def line_sum(self, name, values):
        def body(links, ins, outs, scratch):
            (land,) = scratch
            links.greet({"zall"})
            moves = []
            for step in range(1, self.tensor):
                target = lax.rem(links.z + step, self.tensor)
                move = links.copy(ins[0], land.at[step - 1], (links.dp, target), links.slot())
                move.start()
                moves.append(move)
            total = ins[0][...]
            for step, move in enumerate(moves):
                move.wait_recv()
                total = total + land[step]
            outs[0][...] = total
            for move in moves:
                move.wait_send()

        return self.call(
            name,
            body,
            [(values, True)],
            [(values.shape, jnp.float32, True)],
            [pltpu.VMEM((self.tensor - 1, *values.shape), jnp.float32)],
            8,
        )[0]

    def close(self, time_part, gain_part, grads):
        grads = list(grads)
        summing = grads if self.cube else []
        sums = [(g.shape[0] // self.dp, g.shape[1]) for g in summing]
        bits = [1 << k for k in range(self.dp.bit_length() - 1)]

        def body(links, ins, outs, scratch):
            time_ref, gain_ref = ins[:2]
            total_ref, all_ref, gains_ref = outs[:3]
            land, held, held_gain, come, come_gain = scratch[:5]
            links.greet({"zall", "bits", "diag"} if self.cube else {"zall", "bits"})
            reduces = [
                CubeReduce(links, g, o, *scratch[5 + 3 * k : 8 + 3 * k])
                for k, (g, o) in enumerate(zip(ins[2:], outs[3:]))
            ]
            moves = []
            for step in range(1, self.tensor):
                target = lax.rem(links.z + step, self.tensor)
                move = links.copy(time_ref, land.at[links.z], (links.dp, target), links.slot())
                move.start()
                moves.append(move)
            for item in reduces:
                item.start()
            land[links.z] = time_ref[...]
            held_gain[0] = gain_ref[...]
            for move in moves:
                move.wait_recv()
            total = land[0]
            for index in range(1, self.tensor):
                total = total + land[index]
            total_ref[...] = total
            held[0] = total
            for index, bit in enumerate(bits):
                target = (flip(links.dp, bit), links.z)
                one = links.copy(held.at[index], come.at[index], target, links.slot())
                two = links.copy(held_gain.at[index], come_gain.at[index], target, links.slot())
                one.start()
                two.start()
                if index == 0:
                    for item in reduces:
                        item.middle()
                one.wait_recv()
                two.wait_recv()
                held[index + 1] = held[index] + come[index]
                held_gain[index + 1] = held_gain[index] + come_gain[index]
                moves += [one, two]
            all_ref[...] = held[len(bits)]
            gains_ref[...] = held_gain[len(bits)]
            for item in reduces:
                item.finish()
            for move in moves:
                move.wait_send()

        levels = len(bits)
        results = self.call(
            "close",
            body,
            [(time_part, True), (gain_part, True)] + [(g, False) for g in summing],
            [
                (time_part.shape, jnp.float32, True),
                (time_part.shape, jnp.float32, True),
                (gain_part.shape, jnp.float32, True),
            ]
            + [(shape, jnp.float32, True) for shape in sums],
            [
                pltpu.VMEM((self.tensor, *time_part.shape), jnp.float32),
                pltpu.VMEM((levels + 1, *time_part.shape), jnp.float32),
                pltpu.VMEM((levels + 1, *gain_part.shape), jnp.float32),
                pltpu.VMEM((levels, *time_part.shape), jnp.float32),
                pltpu.VMEM((levels, *gain_part.shape), jnp.float32),
            ]
            + cube_scratch(sums),
            80,
        )
        return results[:3], self.reduced(results[3:], grads)


def summed_back(pairs):
    result = 0.0
    for grads, weight in pairs:
        result = result + product_back(grads, weight)
    return result


def norm_pull(shaping, raw, total, gain, grad):
    _, pull = jax.vjp(shaping, raw, total, gain)
    return pull(grad)


def body(
    plan,
    hidden_in,
    text_states,
    time_embed,
    positions,
    modulation,
    query_weight,
    key_weight,
    value_weight,
    out_weight,
    cross_query,
    cross_key,
    cross_value,
    cross_out,
    up_weight,
    down_weight,
    qk_gain,
    norm_gain,
    cotangent,
):
    plan.calls = 0
    low = jnp.bfloat16
    rows, width = hidden_in.shape
    length = rows * plan.tensor
    heads_here = out_weight.shape[0] // HEAD_DIM
    text_all = lax.all_gather(text_states, "tensor", axis=0, tiled=True)

    part = width // plan.dp
    top = jnp.concatenate([modulation, norm_gain[None], jnp.zeros((1, part), low)], axis=0)
    side = jnp.pad(qk_gain, ((0, 8 - heads_here), (0, 0)))
    small = jnp.concatenate([top, side], axis=1).astype(jnp.float32)
    time_rows = jnp.pad(time_embed[0], ((0, 2), (0, 0)))
    (mixing, gain_rows, self_whole), full = plan.open(
        hidden_in, time_rows, small, [query_weight, key_weight, value_weight, out_weight.T]
    )
    query_full, key_full, value_full, out_full = full
    gains = gain_rows[:heads_here].reshape(heads_here, 4, HEAD_DIM)
    gain_parts = [gains[:, index].reshape(-1) for index in range(4)]
    cosine, sine = rotary_tables(positions, HEAD_DIM)
    feed_grad_whole = lax.all_gather(
        (cotangent * mixing[5]).astype(low), "tensor", axis=0, tiled=True
    )

    query_raw = jnp.dot(self_whole, query_full, preferred_element_type=jnp.float32)
    key_raw = jnp.dot(self_whole, key_full, preferred_element_type=jnp.float32)
    value_low = (
        jnp.dot(self_whole, value_full, preferred_element_type=jnp.float32)
        .astype(low)
        .reshape(length, heads_here, HEAD_DIM)
    )

    def squares(name, first, second):
        sums = jnp.stack([jnp.sum(first * first, axis=-1), jnp.sum(second * second, axis=-1)])
        total = plan.line_sum(name, jnp.pad(sums, ((0, 6), (0, 0))))
        return total[0], total[1]

    def totals(name, first, second):
        total = plan.line_sum(name, jnp.pad(jnp.stack([first, second]), ((0, 6), (0, 0))))
        return total[0], total[1]

    query_total, key_total = squares("squares_self", query_raw, key_raw)

    def self_shape(raw, total, gain):
        return rotate(scaled(raw, total, gain).reshape(length, heads_here, HEAD_DIM), cosine, sine)

    def cross_shape(raw, total, gain):
        return scaled(raw, total, gain).reshape(raw.shape[0], heads_here, HEAD_DIM)

    query_rot = self_shape(query_raw, query_total, gain_parts[0]).astype(low)
    key_rot = self_shape(key_raw, key_total, gain_parts[1]).astype(low)
    self_heads, self_logsum = attend_forward(query_rot, key_rot, value_low)
    self_attended = self_heads.reshape(length, -1).astype(low)
    self_partial = product_back(self_attended, out_full).astype(low)

    def after_self(total, where, near, kinds, first):
        hidden_ref, mixing_ref = near
        branch_ref, resid_ref = kinds
        branch_ref[where, :] = total
        resid = hidden_ref[where, :] + total * mixing_ref[2:3]
        resid_ref[where, :] = resid
        unit, _ = normed(resid)
        return (unit * mixing_ref[6:7]).astype(low)

    (self_branch, resid_self, cross_whole), full, _ = plan.between(
        "after_self",
        self_partial,
        [hidden_in, mixing],
        [(rows, width), (rows, width)],
        after_self,
        True,
        shards=[cross_key, cross_value, cross_query, cross_out.T],
    )
    cross_key_full, cross_value_full, cross_query_full, cross_out_full = full

    text_rows = text_all.shape[0]
    cross_query_raw = jnp.dot(cross_whole, cross_query_full, preferred_element_type=jnp.float32)
    cross_key_raw = jnp.dot(text_all, cross_key_full, preferred_element_type=jnp.float32)
    cross_value_low = (
        jnp.dot(text_all, cross_value_full, preferred_element_type=jnp.float32)
        .astype(low)
        .reshape(text_rows, heads_here, HEAD_DIM)
    )
    cross_query_total, cross_key_total = squares("squares_cross", cross_query_raw, cross_key_raw)
    cross_query_norm = cross_shape(cross_query_raw, cross_query_total, gain_parts[2]).astype(low)
    cross_key_norm = cross_shape(cross_key_raw, cross_key_total, gain_parts[3]).astype(low)
    cross_heads, cross_logsum = attend_forward(cross_query_norm, cross_key_norm, cross_value_low)
    cross_attended = cross_heads.reshape(length, -1).astype(low)
    cross_partial = product_back(cross_attended, cross_out_full).astype(low)

    def after_cross(total, where, near, kinds, first):
        resid_ref, mixing_ref = near
        resid = resid_ref[where, :] + total
        kinds[0][where, :] = resid
        unit, _ = normed(resid)
        return (unit * (1.0 + mixing_ref[4:5]) + mixing_ref[3:4]).astype(low)

    (resid_cross, feed_whole), full, _ = plan.between(
        "after_cross",
        cross_partial,
        [resid_self, mixing],
        [(rows, width)],
        after_cross,
        True,
        shards=[up_weight, down_weight.T],
    )
    up_full, down_full = full

    up_raw = jnp.dot(feed_whole, up_full, preferred_element_type=jnp.float32)
    activated = gelu_tanh(up_raw).astype(low)
    feed_partial = product_back(activated, down_full).astype(low)
    grad_activated = jnp.dot(feed_grad_whole, down_full, preferred_element_type=jnp.float32)
    grad_down = weight_grad(feed_grad_whole, activated).astype(low)
    _, gelu_pull = jax.vjp(gelu_tanh, up_raw)
    grad_up_raw = gelu_pull(grad_activated)[0].astype(low)
    feed_back = product_back(grad_up_raw, up_full).astype(low)

    def add_sum(ref, row, values, first):
        total = jnp.sum(values, axis=0, keepdims=True)
        ref[row : row + 1, :] = total if first else ref[row : row + 1, :] + total

    def before_feed(total, where, near, kinds, first):
        resid_ref, cotangent_ref, mixing_ref = near
        grad_ref, sums_ref, _ = kinds
        unit, inverse = normed(resid_ref[where, :])
        add_sum(sums_ref, 0, total, first)
        add_sum(sums_ref, 1, total * unit, first)
        grad = cotangent_ref[where, :] + normed_back(
            unit, inverse, total * (1.0 + mixing_ref[4:5])
        )
        grad_ref[where, :] = grad
        return grad.astype(low)

    def after_feed(total, where, near, kinds, first):
        resid_ref, cotangent_ref, mixing_ref = near
        _, sums_ref, out_ref = kinds
        out_ref[where, :] = resid_ref[where, :] + total * mixing_ref[5:6]
        add_sum(sums_ref, 2, cotangent_ref[where, :] * total, first)

    (grad_resid_cross, feed_sums, block_out, cross_grad_whole), _, sums = plan.between(
        "before_feed",
        feed_back,
        [resid_cross, cotangent, mixing],
        [(rows, width), (8, width), (rows, width)],
        before_feed,
        True,
        grads=[grad_down],
        extra=(feed_partial, after_feed),
    )
    (sum_down,) = sums

    grad_up = weight_grad(feed_whole, grad_up_raw).astype(low)
    grad_cross_attended = jnp.dot(
        cross_grad_whole, cross_out_full, preferred_element_type=jnp.float32
    ).astype(low)
    grad_cross_out = weight_grad(cross_grad_whole, cross_attended).astype(low)
    grad_cross_query_norm, grad_cross_key_norm, grad_cross_value_heads = attend_backward(
        cross_query_norm,
        cross_key_norm,
        cross_value_low,
        cross_logsum,
        grad_cross_attended.reshape(length, heads_here, HEAD_DIM),
    )
    query_local, query_part, grad_gain_cross_query = norm_pull(
        cross_shape, cross_query_raw, cross_query_total, gain_parts[2], grad_cross_query_norm
    )
    key_local, key_part, grad_gain_cross_key = norm_pull(
        cross_shape, cross_key_raw, cross_key_total, gain_parts[3], grad_cross_key_norm
    )
    query_whole_part, key_whole_part = totals("parts_cross", query_part, key_part)
    grad_cross_query_raw = (query_local + 2.0 * cross_query_raw * query_whole_part[:, None]).astype(
        low
    )
    grad_cross_key_raw = (key_local + 2.0 * cross_key_raw * key_whole_part[:, None]).astype(low)
    grad_cross_value_low = grad_cross_value_heads.reshape(text_rows, -1).astype(low)
    cross_back = product_back(grad_cross_query_raw, cross_query_full).astype(low)

    def before_cross(total, where, near, kinds, first):
        resid_ref, grad_ref, branch_ref, mixing_ref = near
        out_ref, sums_ref = kinds
        unit, inverse = normed(resid_ref[where, :])
        add_sum(sums_ref, 1, total * unit, first)
        grad = grad_ref[where, :] + normed_back(unit, inverse, total * mixing_ref[6:7])
        out_ref[where, :] = grad
        add_sum(sums_ref, 0, grad * branch_ref[where, :], first)
        return (grad * mixing_ref[2:3]).astype(low)

    (grad_resid_self, cross_sums, self_grad_whole), _, sums = plan.between(
        "before_cross",
        cross_back,
        [resid_self, grad_resid_cross, self_branch, mixing],
        [(rows, width), (8, width)],
        before_cross,
        True,
        grads=[grad_up],
    )
    (sum_up,) = sums
    grad_text = lax.psum_scatter(
        summed_back(
            ((grad_cross_key_raw, cross_key_full), (grad_cross_value_low, cross_value_full))
        ).astype(low),
        "tensor",
        scatter_dimension=0,
        tiled=True,
    ).astype(jnp.float32)
    grad_cross_query = weight_grad(cross_whole, grad_cross_query_raw).astype(low)
    grad_cross_key = weight_grad(text_all, grad_cross_key_raw).astype(low)
    grad_cross_value = weight_grad(text_all, grad_cross_value_low).astype(low)

    grad_self_attended = jnp.dot(
        self_grad_whole, out_full, preferred_element_type=jnp.float32
    ).astype(low)
    grad_out = weight_grad(self_grad_whole, self_attended).astype(low)
    grad_query_rot, grad_key_rot, grad_value_heads = attend_backward(
        query_rot,
        key_rot,
        value_low,
        self_logsum,
        grad_self_attended.reshape(length, heads_here, HEAD_DIM),
    )
    query_local, query_part, grad_gain_query = norm_pull(
        self_shape, query_raw, query_total, gain_parts[0], grad_query_rot
    )
    key_local, key_part, grad_gain_key = norm_pull(
        self_shape, key_raw, key_total, gain_parts[1], grad_key_rot
    )
    query_whole_part, key_whole_part = totals("parts_self", query_part, key_part)
    grad_query_raw = (query_local + 2.0 * query_raw * query_whole_part[:, None]).astype(low)
    grad_key_raw = (key_local + 2.0 * key_raw * key_whole_part[:, None]).astype(low)
    grad_value_low = grad_value_heads.reshape(length, -1).astype(low)
    self_back = summed_back(
        ((grad_query_raw, query_full), (grad_key_raw, key_full), (grad_value_low, value_full))
    ).astype(low)

    def before_self(total, where, near, kinds, first):
        hidden_ref, grad_ref, mixing_ref = near
        out_ref, sums_ref = kinds
        unit, inverse = normed(hidden_ref[where, :])
        add_sum(sums_ref, 0, total, first)
        add_sum(sums_ref, 1, total * unit, first)
        out_ref[where, :] = grad_ref[where, :] + normed_back(
            unit, inverse, total * (1.0 + mixing_ref[1:2])
        )

    (grad_hidden, self_sums), _, sums = plan.between(
        "before_self",
        self_back,
        [hidden_in, grad_resid_self, mixing],
        [(rows, width), (8, width)],
        before_self,
        False,
        grads=[grad_cross_key, grad_cross_value, grad_cross_query, grad_cross_out],
    )
    sum_cross_key, sum_cross_value, sum_cross_query, sum_cross_out = sums
    grad_query = weight_grad(self_whole, grad_query_raw).astype(low)
    grad_key = weight_grad(self_whole, grad_key_raw).astype(low)
    grad_value = weight_grad(self_whole, grad_value_low).astype(low)

    time_part = jnp.concatenate(
        [
            self_sums[:2],
            cross_sums[:1],
            feed_sums[:3],
            cross_sums[1:2],
            jnp.zeros((1, width), jnp.float32),
        ],
        axis=0,
    )
    gain_part = jnp.stack(
        [
            item.reshape(heads_here, HEAD_DIM)
            for item in (grad_gain_query, grad_gain_key, grad_gain_cross_query, grad_gain_cross_key)
        ],
        axis=1,
    ).reshape(heads_here, 4 * HEAD_DIM)
    (time_total, all_total, gain_total), sums = plan.close(
        time_part,
        jnp.pad(gain_part, ((0, 8 - heads_here), (0, 0))),
        [grad_query, grad_key, grad_value, grad_out],
    )
    sum_query, sum_key, sum_value, sum_out = sums
    dp = lax.axis_index("dp")
    mine = lax.dynamic_slice_in_dim(all_total, dp * part, part, axis=1)
    gain_width = qk_gain.shape[1]
    gain_mine = lax.dynamic_slice_in_dim(
        gain_total[:heads_here], dp * gain_width, gain_width, axis=1
    )
    return (
        block_out,
        grad_hidden,
        grad_text,
        time_total[None, :6],
        mine[:6],
        sum_query,
        sum_key,
        sum_value,
        sum_out.T,
        sum_cross_query,
        sum_cross_key,
        sum_cross_value,
        sum_cross_out.T,
        sum_up,
        sum_down.T,
        gain_mine,
        mine[6],
    )


def solution(mesh):
    return jax.shard_map(
        functools.partial(body, Plan(mesh)),
        mesh=mesh,
        in_specs=(
            P(("dp", "tensor"), None),
            P(("dp", "tensor"), None),
            P("dp", None, None),
            P(None, "dp"),
            P(None, "dp"),
            P("dp", "tensor"),
            P("dp", "tensor"),
            P("dp", "tensor"),
            P("tensor", "dp"),
            P("dp", "tensor"),
            P("dp", "tensor"),
            P("dp", "tensor"),
            P("tensor", "dp"),
            P("dp", "tensor"),
            P("tensor", "dp"),
            P("tensor", "dp"),
            P("dp"),
            P(("dp", "tensor"), None),
        ),
        out_specs=(
            P(("dp", "tensor"), None),
            P(("dp", "tensor"), None),
            P(("dp", "tensor"), None),
            P("dp", None, None),
            P(None, "dp"),
            P("dp", "tensor"),
            P("dp", "tensor"),
            P("dp", "tensor"),
            P("tensor", "dp"),
            P("dp", "tensor"),
            P("dp", "tensor"),
            P("dp", "tensor"),
            P("tensor", "dp"),
            P("dp", "tensor"),
            P("tensor", "dp"),
            P("tensor", "dp"),
            P("dp"),
        ),
        check_vma=False,
    )
```

time: 1770 us -> 844 us (0.48)
  waiting for transfers between devices: 1360 us -> 0.75 us
  Pallas kernels: 0 us -> 585 us
  blocking collectives: 105 us -> 0 us
  matrix products: 163 us -> 127 us
  other arithmetic: 78.9 us -> 47.5 us
  local copies, waits for them, and re-layouts: 32.9 us -> 63.3 us
    reduce_scatter x17 -> x1, waiting for transfers between devices: 774 us -> 0.01 us  [body(): lax.psum_scatter(summed_back(((grad_cross_key_raw, cross_key_full), (grad...]
    pallas_call x0 -> x11, Pallas kernels: none -> 585 us  [call(): pl.pallas_call(kernel, name=name, out_shape=[jax.ShapeDtypeStruct(shape,...]
    all_gather x16 -> x1, waiting for transfers between devices: 430 us -> 0.02 us  [body(): lax.all_gather((cotangent * mixing[5]).astype(low), 'tensor', axis=0, til...]
    all_gather x1, waiting for transfers between devices: 82.4 us -> 0.01 us  [body(): text_all = lax.all_gather(text_states, 'tensor', axis=0, tiled=True)]
    unnamed x38 -> x3, waiting for transfers between devices: 74.7 us -> 0.71 us
    psum x5 -> x0, blocking collectives: 59.8 us -> none  [the longest x2 22.2 us: total_squares(): lax.psum((jnp.sum(first * first, axis=-1), jnp.sum(second * second, axis=...]
    unnamed x2 -> x0, blocking collectives: 25.6 us -> none
    dot_general x10, matrix products: 51.4 us -> 29.5 us  [product_back(): lax.dot_general(grads, weight, CONTRACT_LAST, preferred_element_type=jnp....]
  transfers between devices with their start and end apart: 36 -> 3, of which waited for: 34 -> 0; matrix products, arithmetic and copies ran while one was open for 9% -> 15% of each run, Pallas kernels for 0% -> 47%
where the time goes in v1:
time: 844 us; the launch traced here: 839 us
  Pallas kernels  585 us (69%)
  matrix products  127 us (15%)
  local copies, waits for them, and re-layouts  63.3 us (8%)
  other arithmetic  47.5 us (6%)
  between operations  15.1 us (2%)
    pallas_call x11, Pallas kernels, call(): pl.pallas_call(kernel, name=name, out_shape=[jax.ShapeDtypeStruct(shape,...  585 us
    dot_general x10, matrix products, weight_grad(): lax.dot_general(inputs, grads, CONTRACT_FIRST, preferred_element_type=jnp...  35 us
    dot_general x10, matrix products, product_back(): lax.dot_general(grads, weight, CONTRACT_LAST, preferred_element_type=jnp....  29.5 us
    unnamed x181, local copies, waits for them, and re-layouts  17 us
  transfers between devices with their start and end apart: 3, of which 0 were waited for; matrix products, arithmetic and copies ran while one was open for 15% of the time, Pallas kernels for 47%

profile of v1, /device:TPU:0, one launch (start us, length us, event | category | flops | bytes accessed | tf_op | source)
XLA Modules:
  0.0 839.0 jit_solution(4321563787232133782)
XLA Ops:
  11.4 107.6 %open.1 = (f32[8,1536]{1,0:T(8,128)}, f32[8,512]{1,0:T(8,128)}, bf16[512,1536]{1,0:T(8,128)(2,1)}, bf16[1536,384]{1,0:T(8,128)(2,1)}, bf16[1536,384]{1,0:T(8,128...) custom-call(f32[128,1536]{1,0:T(8,128)} %refs_1_.3, f32[8,1536]{1,0:T(8,128)} %pad.37.refs_1_, ...), custom_call_target="tpu_custom_call" | custom-call | tf_op jit(solution)/shard_map/open/pallas_call | solution.py:577
  121.9 3.5 convolution_convert_fusion.17
  127.8 9.0 %squares_self.1 = f32[8,512]{1,0:T(8,128)} custom-call(f32[8,512]{1,0:T(8,128)} %select_maximum_fusion.3.refs_0_), custom_call_target="tpu_custom_call" | custom-call | tf_op jit(solution)/shard_map/squares_self/pallas_call | solution.py:577
  139.6 2.1 subtract_convert_fusion
  141.7 1.8 pad_maximum_fusion
  144.5 1.7 multiply_reduce_fusion.3
  146.8 1.6 fusion.27
  148.4 3.6 convolution_convert_fusion.8.refs_0_
  152.0 77.9 %after_self.1 = (f32[128,1536]{1,0:T(8,128)}, f32[128,1536]{1,0:T(8,128)}, bf16[512,1536]{1,0:T(8,128)(2,1)}, bf16[4096,384]{1,0:T(8,128)(2,1)}, bf16[4096,384]{...) custom-call(bf16[512,1536]{1,0:T(8,128)(2,1)} %convolution_convert_fusion.8.refs_0_, ...), custom_call_target="tpu_custom_call" | custom-call | tf_op jit(solution)/shard_map/after_self/pallas_call | solution.py:577
  229.9 4.0 multiply_reduce_fusion.11
  233.9 5.9 multiply_reduce_fusion.10
  240.4 7.6 squares_cross.1
  252.9 2.2 copy-done.10
  255.1 1.8 convolution_convert_fusion.18
  258.4 2.2 convolution_convert_fusion.7.refs_0_
  260.6 76.4 %after_cross.1 = (f32[128,1536]{1,0:T(8,128)}, bf16[512,1536]{1,0:T(8,128)(2,1)}, bf16[1536,2240]{1,0:T(8,128)(2,1)}, bf16[1536,2240]{1,0:T(8,128)(2,1)}) custom-call(bf16[512,1536]{1,0:T(8,128)(2,1)} %convolution_convert_fusion.7.refs_0_, f32[128,1536]{1,0:T(8,128)} %get-tuple-element.159.refs_1_, f32[8,1536]{1,0:T(8,128)} %get-tuple-element.147.refs_2_.refs_4_.refs_3_, ...), custom_call_target="tpu_custom_call" | custom-call | tf_op jit(solution)/shard_map/after_cross/pallas_call | solution.py:577
  337.1 9.5 %fusion.51 = f32[512,2240]{0,1:T(8,128)} fusion(bf16[512,1536]{1,0:T(8,128)(2,1)} %all-gather.3.cloned.1.call-done, bf16[1536,2240]{1,0:T(8,128)(2,1)} %get-tuple-element.160), kind=kOutput, calls=%fused_computation.159 | convolution fusion | flops 3523215360 | bytes 13041664 | tf_op jit(solution)/shard_map/dot_general | solution.py:1036
  346.6 11.6 %fusion.8 = (bf16[512,2240]{0,1:T(8,128)(2,1)S(1)}, f32[512,2240]{0,1:T(8,128)}) fusion(f32[512,2240]{0,1:T(8,128)} %fusion.51, bf16[512,1536]{1,0:T(8,128)(2,1)S(1)} %copy-done.79, bf16[1536,2240]{1,0:T(8,128)(2,1)S(1)} %copy-done.71), kind=kOutput, calls=%fused_computation.15 | convolution fusion | flops 3546152960 | bytes 19922944 | tf_op jit(solution)/shard_map/dot_general | solution.py:1033
  358.2 5.0 convolution_convert_fusion.6.refs_0_
  363.2 5.7 convolution_convert_fusion
  368.9 5.6 convolution_convert_fusion.5.refs_1_
  374.5 6.0 convolution_convert_fusion.1
  380.5 10.1 %copy.85.refs_5_ = bf16[1536,2240]{1,0:T(8,128)(2,1)} copy(bf16[1536,2240]{0,1:T(8,128)(2,1)} %convolution_convert_fusion.1) | data formatting | bytes 13762560 | tf_op jit(solution)/shard_map/convert_element_type | solution.py:1037
  390.6 102.8 %before_feed.1 = (f32[128,1536]{1,0:T(8,128)}, f32[8,1536]{1,0:T(8,128)}, f32[128,1536]{1,0:T(8,128)}, bf16[512,1536]{1,0:T(8,128)(2,1)}, f32[192,2240]{1,0:T(8,128)}) custom-call(bf16[512,1536]{1,0:T(8,128)(2,1)} %convolution_convert_fusion.6.refs_0_, bf16[512,1536]{1,0:T(8,128)(2,1)} %convolution_convert_fusion.5.refs_1_, ...), custom_call_target="tpu_custom_call" | custom-call | tf_op jit(solution)/shard_map/before_feed/pallas_call | solution.py:577
  493.4 2.7 convolution_convert_fusion.16
  499.5 1.5 convolution_multiply_fusion.2
  502.2 10.1 %copy.90.refs_5_ = bf16[1536,2240]{1,0:T(8,128)(2,1)} copy(bf16[1536,2240]{0,1:T(8,128)(2,1)} %convolution_convert_fusion) | data formatting | bytes 13762560 | tf_op jit(solution)/shard_map/convert_element_type | solution.py:1076
  512.3 2.2 fusion.35
  514.5 2.2 fusion.34
  518.2 9.8 %parts_cross.1 = f32[8,512]{1,0:T(8,128)} custom-call(f32[8,512]{1,0:T(8,128)} %select_maximum_fusion.1.refs_0_), custom_call_target="tpu_custom_call" | custom-call | tf_op jit(solution)/shard_map/parts_cross/pallas_call | solution.py:577
  528.8 1.5 add_convert_fusion.1
  530.4 1.7 add_convert_fusion.4
  532.8 2.2 convolution_convert_fusion.4.refs_0_
  535.0 74.8 %before_cross.1 = (f32[128,1536]{1,0:T(8,128)}, f32[8,1536]{1,0:T(8,128)}, bf16[512,1536]{1,0:T(8,128)(2,1)}, f32[192,2240]{1,0:T(8,128)}) custom-call(bf16[512,1536]{1,0:T(8,128)(2,1)} %convolution_convert_fusion.4.refs_0_, f32[128,1536]{1,0:T(8,128)} %get-tuple-element.159.refs_1_, f32[128,1536]{1,0:T(8,128)} %get-tuple-element.166.refs_2_, ...), custom_call_target="tpu_custom_call" | custom-call | tf_op jit(solution)/shard_map/before_cross/pallas_call | solution.py:577
  609.7 3.5 convolution_convert_fusion.15
  613.2 2.4 fusion.53
  615.7 4.4 add_convert_fusion
  620.1 1.9 multiply_reduce_fusion
  622.1 2.0 multiply_convert_fusion.1
  625.9 2.8 fusion.25
  628.7 2.5 reshape_reshape.19
  631.1 2.9 fusion.24
  634.1 2.5 reshape.339
  636.6 4.1 multiply_add_fusion.1
  642.2 2.6 reshape.340
  644.8 2.2 multiply_reduce_fusion.4
  648.3 2.5 pad_add_fusion.1
  650.8 2.6 reshape.338
  653.3 1.7 multiply_reduce_fusion.5
  657.8 10.8 %parts_self.1 = f32[8,512]{1,0:T(8,128)} custom-call(f32[8,512]{1,0:T(8,128)} %select_maximum_fusion.refs_0_), custom_call_target="tpu_custom_call" | custom-call | tf_op jit(solution)/shard_map/parts_self/pallas_call | solution.py:577
  669.4 1.5 add_convert_fusion.2
  671.0 1.7 add_convert_fusion.3
  672.8 3.1 convolution_convert_fusion.13.refs_7_
  675.9 2.0 convolution_convert_fusion.14.refs_6_
  681.4 2.2 fusion.9.refs_0_
  684.3 4.1 fusion.refs_4_
  688.4 4.5 fusion.1.refs_5_
  692.8 67.6 %before_self.1 = (f32[128,1536]{1,0:T(8,128)}, f32[8,1536]{1,0:T(8,128)}, f32[512,384]{1,0:T(8,128)}, f32[512,384]{1,0:T(8,128)}, f32[192,384]{1,0:T(8,128)}, /*index=5*/f32[192,384]{1,0:T(8,128)}) custom-call(bf16[512,1536]{1,0:T(8,128)(2,1)} %fusion.9.refs_0_, f32[128,1536]{1,0:T(8,128)} %refs_1_.3, f32[128,1536]{1,0:T(8,128)} %get-tuple-element.169.refs_2_, ...), custom_call_target="tpu_custom_call" | custom-call | tf_op jit(solution)/shard_map/before_self/pallas_call | solution.py:577
  763.0 3.5 convolution_convert_fusion.9.refs_5_
  766.5 2.0 convolution_convert_fusion.10.refs_4_
  768.5 2.0 convolution_convert_fusion.12.refs_2_
  770.6 2.0 convolution_convert_fusion.11.refs_3_
  772.6 40.9 %close.1 = (f32[8,1536]{1,0:T(8,128)}, f32[8,1536]{1,0:T(8,128)}, f32[8,512]{1,0:T(8,128)}, f32[192,384]{1,0:T(8,128)}, f32[192,384]{1,0:T(8,128)}, /*index=5*/f32[192,384]{1,0:T(8,128)}, f32[192,384]{1,0:T(8,128)}) custom-call(f32[8,1536]{1,0:T(8,128)} %concatenate.23.refs_0_, f32[8,512]{1,0:T(8,128)} %pad.47.refs_1_, ...), custom_call_target="tpu_custom_call" | custom-call | tf_op jit(solution)/shard_map/close/pallas_call | solution.py:577
  819.2 2.8 convert_element_type.244
  (256 shorter events, 58.8 us)
Async XLA Ops:
  7.2 112.8 %copy-start.8 = (f32[128,1536]{1,0:T(8,128)S(1)}, f32[128,1536]{1,0:T(8,128)}, u32[]{:S(2)}) copy-start(f32[128,1536]{1,0:T(8,128)} %refs_3_.7) | copy-start | bytes 2359300
  7.2 113.9 %copy-start.68 = (s32[3,512]{1,0:T(4,128)S(1)}, s32[3,512]{1,0:T(4,128)}, u32[]{:S(2)}) copy-start(s32[3,512]{1,0:T(4,128)} %param.21) | copy-start | bytes 18436
  7.2 226.7 %all-gather.5.cloned.1.call-start = ((), (), s32[]{:S(2)}) async-start(), calls=%async_computation.2 | async-start | bytes 5242880 | tf_op jit(solution)/shard_map/all_gather | solution.py:931
  7.9 329.1 %all-gather.3.cloned.1.call-start = ((), (), s32[]{:S(2)}) async-start(), calls=%async_computation.1 | async-start | bytes 1966080 | tf_op jit(solution)/shard_map/all_gather | solution.py:945
  119.0 6.4 copy-start.30
  120.8 698.4 %reduce-scatter.2.cloned.1.call-start = ((), (), s32[]{:S(2)}) async-start(), calls=%async_computation.3 | async-start | bytes 5242880 | tf_op jit(solution)/shard_map/reduce_scatter | solution.py:1122
  121.8 3.6 copy-start.74
  121.9 15.8 %copy-start.50 = (f32[3,128]{1,0:T(4,128)}, f32[3,128]{1,0:T(4,128)S(1)}, u32[]{:S(2)}) copy-start(f32[3,128]{1,0:T(4,128)S(1)} %get-tuple-element.249) | copy-start | bytes 4612
  121.9 16.4 %copy-start.52 = (f32[3,128]{1,0:T(4,128)}, f32[3,128]{1,0:T(4,128)S(1)}, u32[]{:S(2)}) copy-start(f32[3,128]{1,0:T(4,128)S(1)} %get-tuple-element.248) | copy-start | bytes 4612
  121.9 126.9 %copy-start.54 = (f32[3,128]{1,0:T(4,128)}, f32[3,128]{1,0:T(4,128)S(1)}, u32[]{:S(2)}) copy-start(f32[3,128]{1,0:T(4,128)S(1)} %get-tuple-element.247) | copy-start | bytes 4612
  121.9 128.2 %copy-start.56 = (f32[3,128]{1,0:T(4,128)}, f32[3,128]{1,0:T(4,128)S(1)}, u32[]{:S(2)}) copy-start(f32[3,128]{1,0:T(4,128)S(1)} %get-tuple-element.246) | copy-start | bytes 4612
  121.9 4.4 copy-start.28
  126.3 11.4 %copy-start.2 = (f32[512,384]{0,1:T(8,128)}, f32[512,384]{0,1:T(8,128)S(1)}, u32[]{:S(2)}) copy-start(f32[512,384]{0,1:T(8,128)S(1)} %get-tuple-element.286) | copy-start | bytes 2359300
  127.1 11.8 %copy-start.3 = (f32[512,384]{0,1:T(8,128)}, f32[512,384]{0,1:T(8,128)S(1)}, u32[]{:S(2)}) copy-start(f32[512,384]{0,1:T(8,128)S(1)} %get-tuple-element.284) | copy-start | bytes 2359300
  139.5 3.9 copy-start.32
  139.6 3.9 copy-start.33
  233.9 5.9 copy-start.70
  248.8 2.8 copy-start.60
  251.6 3.5 copy-start.10
  252.4 4.6 copy-start
  337.1 9.5 %copy-start.71 = (bf16[1536,2240]{1,0:T(8,128)(2,1)S(1)}, bf16[1536,2240]{1,0:T(8,128)(2,1)}, u32[]{:S(2)}) copy-start(bf16[1536,2240]{1,0:T(8,128)(2,1)} %get-tuple-element.162) | copy-start | bytes 20643844
  337.1 9.5 %copy-start.79 = (bf16[512,1536]{1,0:T(8,128)(2,1)S(1)}, bf16[512,1536]{1,0:T(8,128)(2,1)}, u32[]{:S(2)}) copy-start(bf16[512,1536]{1,0:T(8,128)(2,1)} %get-tuple-element.161) | copy-start | bytes 4718596
  346.6 22.3 %slice-start = ((s8[7077888]{0:T(1024)(128)(4,1)}), s8[2883584]{0:T(1024)(128)(4,1)S(1)}, s32[]{:S(2)}) async-start(s8[7077888]{0:T(1024)(128)(4,1)} %bitcast.254), calls=%async_computation.4 | async-start | bytes 5767168
  358.2 10.7 %slice-start.1 = ((s8[7077888]{0:T(1024)(128)(4,1)}), s8[4194304]{0:T(1024)(128)(4,1)S(1)}, s32[]{:S(2)}) async-start(s8[7077888]{0:T(1024)(128)(4,1)} %bitcast.254), calls=%async_computation.5 | async-start | bytes 8388608
  363.2 5.7 copy-start.80
  368.9 5.6 copy-start.77
  493.4 4.2 copy-start.42
  502.2 10.1 %copy-start.55 = (f32[3,128]{1,0:T(4,128)S(1)}, f32[3,128]{1,0:T(4,128)}, u32[]{:S(2)}) copy-start(f32[3,128]{1,0:T(4,128)} %copy-done.54) | copy-start | bytes 4612
  502.2 12.3 %copy-start.57 = (f32[3,128]{1,0:T(4,128)S(1)}, f32[3,128]{1,0:T(4,128)}, u32[]{:S(2)}) copy-start(f32[3,128]{1,0:T(4,128)} %copy-done.56) | copy-start | bytes 4612
  512.3 16.5 %copy-start.63 = (f32[1,512]{1,0:T(1,128)S(1)}, f32[1,512]{1,0:T(1,128)}, u32[]{:S(2)}) copy-start(f32[1,512]{1,0:T(1,128)} %copy-done.62) | copy-start | bytes 6148
  512.3 18.0 %copy-start.61 = (f32[1,512]{1,0:T(1,128)S(1)}, f32[1,512]{1,0:T(1,128)}, u32[]{:S(2)}) copy-start(f32[1,512]{1,0:T(1,128)} %copy-done.60) | copy-start | bytes 6148
  527.9 4.8 copy-start.25
  530.3 82.9 %copy-start.14 = (bf16[512,384]{0,1:T(8,128)(2,1)}, bf16[512,384]{0,1:T(8,128)(2,1)S(1)}, u32[]{:S(2)}) copy-start(bf16[512,384]{0,1:T(8,128)(2,1)S(1)} %add_convert_fusion.1) | copy-start | bytes 1179652
  609.7 3.5 copy-start.9
  622.0 3.2 copy-start.66
  636.6 8.2 copy-start.53
  642.2 11.2 %copy-start.51 = (f32[3,128]{1,0:T(4,128)S(1)}, f32[3,128]{1,0:T(4,128)}, u32[]{:S(2)}) copy-start(f32[3,128]{1,0:T(4,128)} %copy-done.50) | copy-start | bytes 4612
  650.8 4.3 copy-start.69
  650.8 5.6 copy-start.67
  668.6 4.2 copy-start.78
  671.0 8.8 %copy-start.21 = (bf16[512,384]{0,1:T(8,128)(2,1)}, bf16[512,384]{0,1:T(8,128)(2,1)S(1)}, u32[]{:S(2)}) copy-start(bf16[512,384]{0,1:T(8,128)(2,1)S(1)} %add_convert_fusion.2) | copy-start | bytes 1179652
  671.0 4.9 copy-start.17
  671.0 4.9 copy-start.76
  672.8 5.2 copy-start.18
  675.9 2.8 copy-start.31
  681.4 2.9 copy-start.73
  684.3 4.1 copy-start.24
  692.8 69.5 %copy-start.49 = (f32[3,1536]{1,0:T(4,128)S(1)}, f32[3,1536]{1,0:T(4,128)}, u32[]{:S(2)}) copy-start(f32[3,1536]{1,0:T(4,128)} %slice.110) | copy-start | bytes 55300
  692.8 70.2 %copy-start.38 = (bf16[3,128,512]{2,1,0:T(8,128)(2,1)S(1)}, bf16[3,128,512]{2,1,0:T(8,128)(2,1)}, u32[]{:S(2)}) copy-start(bf16[3,128,512]{2,1,0:T(8,128)(2,1)} %fusion.27) | copy-start | bytes 1179652
  760.5 6.0 copy-start.20
  760.5 6.0 copy-start.75
  766.5 4.1 copy-start.22
  772.6 49.4 %copy-start.34 = (f32[128,1536]{1,0:T(8,128)S(1)}, f32[128,1536]{1,0:T(8,128)}, u32[]{:S(2)}) copy-start(f32[128,1536]{1,0:T(8,128)} %get-tuple-element.320) | copy-start | bytes 2359300
  813.5 9.4 %copy-start.37 = (f32[128,1536]{1,0:T(8,128)S(1)}, f32[128,1536]{1,0:T(8,128)}, u32[]{:S(2)}) copy-start(f32[128,1536]{1,0:T(8,128)} %get-tuple-element.321) | copy-start | bytes 2359300
  819.1 4.6 copy-start.48
  819.1 5.4 copy-start.47
  819.1 6.1 copy-start.46
  822.0 3.9 copy-start.45
  822.0 4.7 copy-start.44
  822.0 5.4 copy-start.36
  822.9 5.4 copy-start.35
  823.8 5.4 copy-start.43
  824.5 5.4 copy-start.13
  828.2 2.8 copy-start.12
  (22 other events, 41.5 us)
Sparse Core Ops, SparseCore 0:
  9.6 105.8 all-gather.4
  120.9 38.8 all-gather.2
  620.2 76.7 reduce-scatter.1

commit v2 on v1

v2 whole, which is shorter than its diff:
```python
import functools

import jax
import jax.numpy as jnp
from jax import lax
from jax.experimental import pallas as pl
from jax.experimental.pallas import tpu as pltpu
from jax.sharding import PartitionSpec as P

MESH = pl.DeviceIdType.MESH
VMEM_BYTES = 60 * 2**20

HEAD_DIM = 128
D = 1536


EPSILON = 1e-06
CONTRACT_LAST = (((1,), (1,)), ((), ()))
CONTRACT_FIRST = (((0,), (0,)), ((), ()))


def rotary_tables(positions, head_width):
    pairs = head_width // 2
    third = pairs // 3
    first = pairs - 2 * third
    freq_frame = jnp.power(10000.0, -jnp.arange(first, dtype=jnp.float32) / first)
    freq_side = jnp.power(10000.0, -jnp.arange(third, dtype=jnp.float32) / third)
    places = positions.astype(jnp.float32)
    angles = jnp.concatenate(
        [
            places[0][:, None] * jnp.repeat(freq_frame, 2)[None, :],
            places[1][:, None] * jnp.repeat(freq_side, 2)[None, :],
            places[2][:, None] * jnp.repeat(freq_side, 2)[None, :],
        ],
        axis=1,
    )
    sign = jnp.where(jnp.arange(head_width) % 2 == 0, -1.0, 1.0)
    return (jnp.cos(angles), jnp.sin(angles) * sign)


def product_back(grads, weight):
    return lax.dot_general(grads, weight, CONTRACT_LAST, preferred_element_type=jnp.float32)


def weight_grad(inputs, grads):
    return lax.dot_general(inputs, grads, CONTRACT_FIRST, preferred_element_type=jnp.float32)


def when(cond, run):
    if cond is None:
        run()
    else:
        pl.when(cond)(run)


def flip(index, bit):
    return index + bit - 2 * bit * (index // bit % 2)


def normed(values):
    center = values - jnp.mean(values, axis=-1, keepdims=True)
    inverse = lax.rsqrt(jnp.mean(center * center, axis=-1, keepdims=True) + EPSILON)
    return center * inverse, inverse


def normed_back(unit, inverse, grad):
    mean_grad = jnp.mean(grad, axis=-1, keepdims=True)
    mean_dot = jnp.mean(grad * unit, axis=-1, keepdims=True)
    return (grad - mean_grad - unit * mean_dot) * inverse


class Links:
    def __init__(self, send, recv, local, dp_size, tensor_size):
        self.send, self.recv, self.local = send, recv, local
        self.count = 0
        self.local_count = 0
        self.dp_size, self.size = dp_size, tensor_size
        self.dp = lax.axis_index("dp")
        self.z = lax.axis_index("tensor")

    def slot(self):
        self.count += 1
        return self.count - 1

    def copy(self, source, target, device, slot):
        return pltpu.make_async_remote_copy(
            src_ref=source,
            dst_ref=target,
            send_sem=self.send.at[slot],
            recv_sem=self.recv.at[slot],
            device_id=device,
            device_id_type=MESH,
        )

    def here(self, source, target):
        self.local_count += 1
        return pltpu.make_async_copy(source, target, self.local.at[self.local_count - 1])

    def greet(self, groups):
        barrier = pltpu.get_barrier_semaphore()
        peers = []
        if "line" in groups and "zall" not in groups:
            peers += [
                ((self.dp, self.z - 1), self.z > 0),
                ((self.dp, self.z + 1), self.z < self.size - 1),
            ]
        if "zall" in groups:
            peers += [
                ((self.dp, lax.rem(self.z + k, self.size)), None) for k in range(1, self.size)
            ]
        if "dpall" in groups:
            peers += [
                ((lax.rem(self.dp + k, self.dp_size), self.z), None)
                for k in range(1, self.dp_size)
            ]
        if "bits" in groups:
            bit = 1
            while bit < self.dp_size:
                peers.append(((flip(self.dp, bit), self.z), None))
                bit *= 2
        if "diag" in groups:
            peers.append(((flip(flip(self.dp, 2), 4), self.z), None))
        for device, cond in peers:
            when(
                cond,
                lambda device=device: pl.semaphore_signal(
                    barrier, inc=1, device_id=device, device_id_type=MESH
                ),
            )
        expected = sum(1 for _, cond in peers if cond is None)
        for _, cond in peers:
            if cond is not None:
                expected = expected + cond.astype(jnp.int32)
        pl.semaphore_wait(barrier, expected)


def piece_of(ref, block, rows, start, count):
    return ref.at[pl.ds(pl.multiple_of(block * rows + start, 16), count)]


class LineGather:
    def __init__(self, links, whole, rows, pieces):
        self.links, self.whole, self.rows, self.count = links, whole, rows, rows // pieces
        self.pieces = pieces
        hops = links.size - 1
        self.right = [[links.slot() for _ in range(pieces)] for _ in range(hops)]
        self.left = [[links.slot() for _ in range(pieces)] for _ in range(hops)]

    def block(self, index, piece):
        return piece_of(self.whole, index, self.rows, piece * self.count, self.count)

    def move(self, index, piece, way, slot):
        part = self.block(index, piece)
        return self.links.copy(part, part, (self.links.dp, self.links.z + way), slot)

    def start(self, piece):
        z, last = self.links.z, self.links.size - 1
        when(z < last, lambda: self.move(z, piece, 1, self.right[0][piece]).start())
        when(z > 0, lambda: self.move(z, piece, -1, self.left[0][piece]).start())

    def step(self, hop, piece):
        z, last = self.links.z, self.links.size - 1

        def from_left():
            self.move(z - 1 - hop, piece, -1, self.right[hop][piece]).wait_recv()
            if hop + 1 < last:
                when(
                    z < last,
                    lambda: self.move(z - 1 - hop, piece, 1, self.right[hop + 1][piece]).start(),
                )

        def from_right():
            self.move(z + 1 + hop, piece, 1, self.left[hop][piece]).wait_recv()
            if hop + 1 < last:
                when(
                    z > 0,
                    lambda: self.move(z + 1 + hop, piece, -1, self.left[hop + 1][piece]).start(),
                )

        when(z - 1 - hop >= 0, from_left)
        when(z + 1 + hop <= last, from_right)

    def steps(self, piece):
        for hop in range(self.links.size - 1):
            self.step(hop, piece)

    def finish(self):
        z, last = self.links.z, self.links.size - 1
        for hop in range(last):
            for piece in range(self.pieces):
                when(
                    (z - hop >= 0) & (z < last),
                    lambda: self.move(z - hop, piece, 1, self.right[hop][piece]).wait_send(),
                )
                when(
                    (z + hop <= last) & (z > 0),
                    lambda: self.move(z + hop, piece, -1, self.left[hop][piece]).wait_send(),
                )


class LineReduce:
    def __init__(self, links, partial, land_right, land_left, rows, pieces):
        self.links, self.partial, self.rows, self.count = links, partial, rows, rows // pieces
        self.land = {1: land_right, -1: land_left}
        self.pieces = pieces
        last = links.size - 1
        self.slots = {
            way: [None] + [[links.slot() for _ in range(pieces)] for _ in range(last)]
            for way in (1, -1)
        }

    def landing(self, way, distance, piece):
        return self.land[way].at[distance - 1, pl.ds(piece * self.count, self.count)]

    def part(self, index, piece):
        return piece_of(self.partial, index, self.rows, piece * self.count, self.count)

    def move(self, source, way, distance, piece):
        return self.links.copy(
            source,
            self.landing(way, distance, piece),
            (self.links.dp, self.links.z + way),
            self.slots[way][distance][piece],
        )

    def arrived(self, way, distance, piece):
        self.links.copy(
            self.landing(way, distance, piece),
            self.landing(way, distance, piece),
            (self.links.dp, self.links.z - way),
            self.slots[way][distance][piece],
        ).wait_recv()

    def first(self, piece):
        z, last = self.links.z, self.links.size - 1

        def from_first():
            for distance in range(last, 0, -1):
                self.move(self.part(distance, piece), 1, distance, piece).start()

        def from_last():
            for distance in range(last, 0, -1):
                self.move(self.part(last - distance, piece), -1, distance, piece).start()

        when(z == 0, from_first)
        when(z == last, from_last)

    def clear(self):
        z, last = self.links.z, self.links.size - 1

        def zero(way):
            self.land[way][0] = jnp.zeros(self.land[way].shape[1:], self.land[way].dtype)

        when(z == 0, lambda: zero(1))
        when(z == last, lambda: zero(-1))

    def step(self, distance, piece):
        z, last = self.links.z, self.links.size - 1
        for way in (1, -1):
            inside = (
                (z > 0) & (z + distance <= last)
                if way == 1
                else (z < last) & (z - distance >= 0)
            )

            def go(way=way):
                self.arrived(way, distance + 1, piece)
                held = self.landing(way, distance + 1, piece)
                own = self.part(z + way * distance, piece)
                held[...] = (
                    held[...].astype(jnp.float32) + own[...].astype(jnp.float32)
                ).astype(held.dtype)
                self.move(held, way, distance, piece).start()

            when(inside, go)

    def total(self, piece):
        z, last = self.links.z, self.links.size - 1
        when(z > 0, lambda: self.arrived(1, 1, piece))
        when(z < last, lambda: self.arrived(-1, 1, piece))
        return (
            self.part(z, piece)[...].astype(jnp.float32)
            + self.landing(1, 1, piece)[...].astype(jnp.float32)
            + self.landing(-1, 1, piece)[...].astype(jnp.float32)
        )

    def finish(self):
        z, last = self.links.z, self.links.size - 1
        for distance in range(1, last + 1):
            for piece in range(self.pieces):
                held = self.landing(1, distance, piece)
                when(
                    z + distance <= last,
                    lambda: self.move(held, 1, distance, piece).wait_send(),
                )
                back = self.landing(-1, distance, piece)
                when(
                    z - distance >= 0,
                    lambda: self.move(back, -1, distance, piece).wait_send(),
                )


def reduce_stages(reduce):
    return [
        functools.partial(reduce.step, distance)
        for distance in range(reduce.links.size - 2, 0, -1)
    ]


def wave(stages, pieces, queue):
    count = pieces + len(stages) - 1
    done = 0
    for step in range(count):
        for index, stage in enumerate(stages):
            if 0 <= step - index < pieces:
                stage(step - index)
        until = len(queue) * (step + 1) // count
        for run in queue[done:until]:
            run()
        done = until


class CubeGather:
    def __init__(self, links, shard, whole):
        self.links, self.shard, self.whole = links, shard, whole
        self.rows = shard.shape[0]
        self.slots = [links.slot() for _ in range(8)]
        dp = links.dp
        self.core, self.side, self.over = flip(dp, 1), flip(dp, 2), flip(dp, 4)
        self.far = flip(flip(dp, 2), 4)
        self.sent = []

    def block(self, index, start=0, count=None):
        return piece_of(self.whole, index, self.rows, start, count or self.rows)

    def send(self, source, target, device, slot):
        move = self.links.copy(source, target, (device, self.links.z), self.slots[slot])
        move.start()
        self.sent.append(move)

    def got(self, part, slot):
        self.links.copy(part, part, (self.core, self.links.z), self.slots[slot]).wait_recv()

    def start(self):
        mine = self.block(self.links.dp)
        self.own = self.links.here(self.shard, mine)
        self.own.start()
        self.send(self.shard, mine, self.side, 1)
        self.send(self.shard, mine, self.over, 2)
        self.send(self.shard, mine, self.core, 0)

    def forward(self):
        half = self.rows // 2
        self.got(self.block(self.side), 1)
        part = self.block(self.side, 0, half)
        self.send(part, part, self.over, 3)
        part = self.block(self.side)
        self.send(part, part, self.core, 5)
        self.got(self.block(self.over), 2)
        part = self.block(self.over, half, half)
        self.send(part, part, self.side, 4)
        part = self.block(self.over)
        self.send(part, part, self.core, 6)

    def tail(self):
        half = self.rows // 2
        self.got(self.block(self.far, 0, half), 3)
        self.got(self.block(self.far, half, half), 4)
        part = self.block(self.far)
        self.send(part, part, self.core, 7)

    def finish(self):
        self.got(self.block(self.core), 0)
        self.got(self.block(flip(self.core, 2)), 5)
        self.got(self.block(flip(self.core, 4)), 6)
        self.got(self.block(flip(flip(self.core, 2), 4)), 7)
        for move in self.sent:
            move.wait_send()
        self.own.wait()


class DirectGather:
    def __init__(self, links, whole, rows):
        self.links, self.whole, self.rows = links, whole, rows
        self.slots = [links.slot() for _ in range(links.size - 1)]

    def start(self, source):
        links = self.links
        mine = piece_of(self.whole, links.z, self.rows, 0, self.rows)
        self.moves = [
            links.copy(source, mine, (links.dp, lax.rem(links.z + step, links.size)), slot)
            for step, slot in enumerate(self.slots, 1)
        ]
        for move in self.moves:
            move.start()

    def finish(self):
        for move in self.moves:
            move.wait_recv()
        for move in self.moves:
            move.wait_send()


class DirectReduce:
    def __init__(self, links, partial, land, rows):
        self.links, self.partial, self.land, self.rows = links, partial, land, rows
        self.slots = [links.slot() for _ in range(links.size - 1)]

    def start(self):
        links = self.links
        self.moves = []
        for step, slot in enumerate(self.slots, 1):
            target = lax.rem(links.z + step, links.size)
            move = links.copy(
                piece_of(self.partial, target, self.rows, 0, self.rows),
                self.land.at[step - 1],
                (links.dp, target),
                slot,
            )
            move.start()
            self.moves.append(move)

    def arrive(self):
        for move in self.moves:
            move.wait_recv()

    def total(self, start, count):
        total = piece_of(self.partial, self.links.z, self.rows, start, count)[...]
        total = total.astype(jnp.float32)
        for index in range(self.links.size - 1):
            total = total + self.land[index, start : start + count, :].astype(jnp.float32)
        return total

    def finish(self):
        for move in self.moves:
            move.wait_send()


class Exchange:
    def __init__(self, links, mine, land, turned):
        self.links, self.mine, self.land, self.turned = links, mine, land, turned
        self.slots = [links.slot() for _ in range(links.size - 1)]

    def start(self, columns):
        links = self.links
        lane = lax.broadcasted_iota(jnp.int32, (columns[0].shape[0], 128), 1)
        flat = jnp.zeros(lane.shape, jnp.float32)
        for index, column in enumerate(columns):
            flat = jnp.where(lane == index, column, flat)
        self.mine[...] = flat.T[:8]
        self.moves = [
            links.copy(
                self.mine,
                self.land.at[step - 1],
                (links.dp, lax.rem(links.z + step, links.size)),
                slot,
            )
            for step, slot in enumerate(self.slots, 1)
        ]
        for move in self.moves:
            move.start()

    def finish(self, shape=lambda total: total):
        total = self.mine[...]
        for step, move in enumerate(self.moves):
            move.wait_recv()
            total = total + self.land[step]
        self.turned[...] = jnp.zeros(self.turned.shape, jnp.float32)
        self.turned[0:8, :] = shape(total)
        for move in self.moves:
            move.wait_send()
        return self.turned[...].T


class CoreSum:
    def __init__(self, links, left, right, product, near):
        self.links, self.left, self.right = links, left, right
        self.product, self.near = product, near
        self.rows = near.shape[1]
        self.slots = [links.slot() for _ in range(4)]
        self.core = links.dp % 2
        self.moves = []

    def multiply(self, chip):
        links, count = self.links, 2 * self.rows
        self.product[chip * count : (chip + 1) * count, :] = weight_grad(
            self.left[:, chip * count : (chip + 1) * count], self.right[...]
        ).astype(jnp.bfloat16)
        move = links.copy(
            piece_of(self.product, 2 * chip + 1 - self.core, self.rows, 0, self.rows),
            self.near.at[chip],
            (flip(links.dp, 1), links.z),
            self.slots[chip],
        )
        move.start()
        self.moves.append(move)

    def add(self):
        for move in self.moves:
            move.wait_recv()

        def one(step, _):
            rows = pl.ds(pl.multiple_of(step * 16, 16), 16)
            for chip in range(4):
                own = pl.ds(
                    pl.multiple_of((2 * chip + self.core) * self.rows + step * 16, 16), 16
                )
                self.near[chip, rows, :] = (
                    self.near[chip, rows, :].astype(jnp.float32)
                    + self.product[own, :].astype(jnp.float32)
                ).astype(jnp.bfloat16)
            return 0

        lax.fori_loop(0, self.rows // 16, one, 0)

    def clear(self):
        for move in self.moves:
            move.wait_send()

    def steps(self):
        return [functools.partial(self.multiply, chip) for chip in range(4)] + [self.add]


class ChipSum:
    def __init__(self, links, near, out, others, own=None):
        self.links, self.near, self.out, self.others, self.own = links, near, out, others, own
        self.slots = [links.slot() for _ in range(3)]
        self.core, self.chip = links.dp % 2, links.dp // 2
        self.rows = out.shape[0]

    def start(self):
        links = self.links
        chips = [flip(self.chip, 1), flip(self.chip, 2), flip(flip(self.chip, 1), 2)]
        self.moves = [
            links.copy(
                self.near.at[chip],
                self.others.at[index],
                (2 * chip + self.core, links.z),
                self.slots[index],
            )
            for index, chip in enumerate(chips)
        ]
        for move in self.moves:
            move.start()
        if self.own is not None:
            self.local = links.here(self.near.at[self.chip], self.own)
            self.local.start()

    def finish(self):
        for move in self.moves:
            move.wait_recv()
        if self.own is not None:
            self.local.wait()

        def one(step, _):
            rows = pl.ds(pl.multiple_of(step * 16, 16), 16)
            mine = self.own[rows, :] if self.own is not None else self.near[self.chip, rows, :]
            total = mine.astype(jnp.float32)
            for index in range(3):
                total = total + self.others[index, rows, :].astype(jnp.float32)
            self.out[rows, :] = total
            return 0

        lax.fori_loop(0, self.rows // 16, one, 0)
        for move in self.moves:
            move.wait_send()


def attend(query, key, value, out, logs, heads, chunk=256):
    scale = HEAD_DIM**-0.5
    for head in range(heads):
        lanes = slice(head * HEAD_DIM, (head + 1) * HEAD_DIM)

        def one(step, _, head=head, lanes=lanes):
            rows = pl.ds(pl.multiple_of(step * chunk, chunk), chunk)
            scores = product_back(query[rows, lanes], key[:, lanes]) * scale
            top = jnp.max(scores, axis=-1, keepdims=True)
            expo = jnp.exp(scores - top)
            summed = jnp.sum(expo, axis=-1, keepdims=True)
            probs = (expo * (1.0 / summed)).astype(jnp.bfloat16)
            out[rows, lanes] = jnp.dot(
                probs, value[:, lanes], preferred_element_type=jnp.float32
            ).astype(jnp.bfloat16)
            logs[rows, head : head + 1] = top + jnp.log(summed)
            return 0

        lax.fori_loop(0, query.shape[0] // chunk, one, 0)


def attend_back(query, key, value, logs, grad, grads, heads, chunk=256):
    scale = HEAD_DIM**-0.5
    grad_query, grad_key, grad_value = grads
    grad_key[...] = jnp.zeros(grad_key.shape, jnp.float32)
    grad_value[...] = jnp.zeros(grad_value.shape, jnp.float32)
    for head in range(heads):
        lanes = slice(head * HEAD_DIM, (head + 1) * HEAD_DIM)

        def one(step, _, head=head, lanes=lanes):
            rows = pl.ds(pl.multiple_of(step * chunk, chunk), chunk)
            scores = product_back(query[rows, lanes], key[:, lanes]) * scale
            probs = jnp.exp(scores - logs[rows, head : head + 1])
            prob_grad = product_back(grad[rows, lanes], value[:, lanes])
            inner = jnp.sum(prob_grad * probs, axis=-1, keepdims=True)
            score_grad = (probs * (prob_grad - inner)).astype(jnp.bfloat16)
            grad_query[rows, lanes] = (
                jnp.dot(score_grad, key[:, lanes], preferred_element_type=jnp.float32) * scale
            )
            grad_key[:, lanes] += weight_grad(score_grad, query[rows, lanes]) * scale
            grad_value[:, lanes] += weight_grad(probs.astype(jnp.bfloat16), grad[rows, lanes])
            return 0

        lax.fori_loop(0, query.shape[0] // chunk, one, 0)


def swapped(values):
    lane = lax.broadcasted_iota(jnp.int32, values.shape, 1)
    width = values.shape[1]
    return jnp.where(lane % 2 == 0, pltpu.roll(values, width - 1, 1), pltpu.roll(values, 1, 1))


def turn(values, cosine, sine, back):
    other = swapped(values) * sine
    return values * cosine - other if back else values * cosine + other


def square_columns(*arrays):
    return [jnp.sum(array * array, axis=-1, keepdims=True) for array in arrays]


def shape_norm(raw, inverse, gain, angles, out, heads, chunk=128):
    for head in range(heads):
        lanes = slice(head * HEAD_DIM, (head + 1) * HEAD_DIM)
        for start in range(0, raw.shape[0], chunk):
            rows = slice(start, start + chunk)
            values = raw[rows, lanes] * inverse[rows] * gain[head]
            if angles is not None:
                values = turn(values, angles[0][rows, :], angles[1][rows, :], False)
            out[rows, lanes] = values.astype(jnp.bfloat16)


def norm_dots(raw, inverse, gain, angles, grad, gain_out, heads, chunk=128):
    columns = []
    for start in range(0, raw.shape[0], chunk):
        rows = slice(start, start + chunk)
        column = jnp.zeros((chunk, 1), jnp.float32)
        for head in range(heads):
            lanes = slice(head * HEAD_DIM, (head + 1) * HEAD_DIM)
            values = grad[rows, lanes]
            if angles is not None:
                values = turn(values, angles[0][rows, :], angles[1][rows, :], True)
                grad[rows, lanes] = values
            part = values * raw[rows, lanes]
            column = column + jnp.sum(part * gain[head], axis=-1, keepdims=True)
            total = jnp.sum(part * inverse[rows], axis=0, keepdims=True)
            where = slice(head, head + 1)
            gain_out[where, :] = total if start == 0 else gain_out[where, :] + total
        columns.append(column)
    return jnp.concatenate(columns, axis=0)


def norm_pull(raw, inverse, gain, dots, grad, out, heads, chunk=128):
    for start in range(0, raw.shape[0], chunk):
        rows = slice(start, start + chunk)
        scale = inverse[rows]
        cut = dots[rows] * scale * scale * scale * (1.0 / D)
        for head in range(heads):
            lanes = slice(head * HEAD_DIM, (head + 1) * HEAD_DIM)
            out[rows, lanes] = (
                grad[rows, lanes] * gain[head] * scale - raw[rows, lanes] * cut
            ).astype(jnp.bfloat16)


def gains_of(gain_ref, kind, heads):
    lanes = slice(kind * HEAD_DIM, (kind + 1) * HEAD_DIM)
    return [gain_ref[head : head + 1, lanes] for head in range(heads)]


def exchange_scratch(length, size):
    return [
        pltpu.VMEM((8, length), jnp.float32),
        pltpu.VMEM((size - 1, 8, length), jnp.float32),
        pltpu.VMEM((128, length), jnp.float32),
    ]


class Plan:
    def __init__(self, mesh):
        self.dp = mesh.shape["dp"]
        self.tensor = mesh.shape["tensor"]
        self.cube = self.dp == 8
        self.calls = 0
        self.pieces = 4

    def call(self, name, body, inputs, outputs, scratch, copies):
        self.calls += 1
        spaces = {True: pltpu.VMEM, False: pltpu.HBM}
        count_in, count_out = len(inputs), len(outputs)

        def kernel(*refs):
            ins = refs[:count_in]
            outs = refs[count_in : count_in + count_out]
            rest = refs[count_in + count_out :]
            links = Links(rest[0], rest[1], rest[2], self.dp, self.tensor)
            body(links, ins, outs, rest[3:])

        return pl.pallas_call(
            kernel,
            name=name,
            out_shape=[jax.ShapeDtypeStruct(shape, kind) for shape, kind, _ in outputs],
            in_specs=[pl.BlockSpec(memory_space=spaces[near]) for _, near in inputs],
            out_specs=[pl.BlockSpec(memory_space=spaces[near]) for _, _, near in outputs],
            scratch_shapes=[
                pltpu.SemaphoreType.DMA((copies,)),
                pltpu.SemaphoreType.DMA((copies,)),
                pltpu.SemaphoreType.DMA((64,)),
                *scratch,
            ],
            compiler_params=pltpu.CompilerParams(
                collective_id=self.calls, has_side_effects=True, vmem_limit_bytes=VMEM_BYTES
            ),
        )(*[array for array, _ in inputs])

    def gather_outputs(self, shards):
        return [
            ((self.dp * shard.shape[0], shard.shape[1]), shard.dtype, False) for shard in shards
        ]

    def open(self, hidden, time_rows, small, shards):
        rows, width = hidden.shape
        part = width // self.dp
        gain_part = small.shape[1] - part
        moving = shards if self.cube else []

        def body(links, ins, outs, scratch):
            hidden_ref, time_ref, small_ref = ins[:3]
            table_ref, gain_ref, whole_ref = outs[:3]
            (land,) = scratch
            links.greet({"line", "dpall"})
            gathers = [CubeGather(links, a, b) for a, b in zip(ins[3:], outs[3:])]
            dp, z = links.dp, links.z
            moves = []
            for step in range(1, self.dp):
                target = lax.rem(dp + step, self.dp)
                move = links.copy(small_ref, land.at[dp], (target, z), links.slot())
                move.start()
                moves.append(move)
            for item in gathers:
                item.start()
            land[dp] = small_ref[...]
            unit, _ = normed(hidden_ref[...])
            for move in moves:
                move.wait_recv()
            table = jnp.concatenate([land[k][:, :part] for k in range(self.dp)], axis=1)
            gain_ref[...] = jnp.concatenate([land[k][:, part:] for k in range(self.dp)], axis=1)
            table = table + time_ref[...]
            table_ref[...] = table
            line = LineGather(links, whole_ref, rows, 4)
            first = unit * (1.0 + table[1:2]) + table[0:1]
            whole_ref[pl.ds(pl.multiple_of(z * rows, 16), rows), :] = first.astype(jnp.bfloat16)
            for piece in range(4):
                line.start(piece)
            for piece in range(4):
                line.steps(piece)
                if piece < len(gathers):
                    gathers[piece].forward()
            for item in gathers[4:]:
                item.forward()
            for item in gathers:
                item.tail()
            for item in gathers:
                item.finish()
            line.finish()
            for move in moves:
                move.wait_send()

        results = self.call(
            "open",
            body,
            [(hidden, True), (time_rows, True), (small, True)] + [(s, False) for s in moving],
            [
                ((8, width), jnp.float32, True),
                ((8, gain_part * self.dp), jnp.float32, True),
                ((rows * self.tensor, width), jnp.bfloat16, True),
            ]
            + self.gather_outputs(moving),
            [pltpu.VMEM((self.dp, 8, small.shape[1]), jnp.float32)],
            160,
        )
        return results[:3], self.gathered(results[3:], shards)

    def gathered(self, moved, shards):
        if self.cube:
            return list(moved)
        return [lax.all_gather(shard, "dp", axis=0, tiled=True) for shard in shards]

    def phase(
        self,
        name,
        near,
        kinds,
        scratch,
        pre,
        post,
        gather,
        shape,
        shards=(),
        lines=(),
        sums=(),
        jobs=(),
        tasks=None,
        begin=None,
        end=None,
        exchange=True,
    ):
        length, width = shape
        rows = length // self.tensor
        pieces = self.pieces
        shards, lines, sums = list(shards), list(lines), list(sums)
        moving = shards if self.cube else []
        adding = sums if self.cube else []
        jobs = list(jobs)
        here = [job for job in jobs if job[4]] if self.cube else []
        count_near, count_kinds, count_scratch = len(near), len(kinds), len(scratch)

        job_scratch, job_outputs = [], []
        products, seats = {}, []
        for left, right, part, columns, now in jobs:
            if not self.cube:
                seats.append(("out", len(job_outputs)))
                job_outputs.append(((self.dp * part, columns), jnp.bfloat16, True))
                continue
            key = (part, columns)
            if key not in products:
                products[key] = len(job_scratch)
                job_scratch.append(pltpu.VMEM((8 * part, columns), jnp.bfloat16))
            if now:
                seats.append((products[key], len(job_scratch), len(job_outputs)))
                job_scratch.append(pltpu.VMEM((4, part, columns), jnp.bfloat16))
                job_scratch.append(pltpu.VMEM((3, part, columns), jnp.bfloat16))
                job_outputs.append(((part, columns), jnp.float32, True))
            else:
                seats.append((products[key], None, len(job_outputs)))
                job_outputs.append(((4, part, columns), jnp.bfloat16, True))
        sum_scratch, sum_outputs = [], []
        for item in adding:
            _, part, columns = item.shape
            sum_scratch.append(pltpu.VMEM((3, part, columns), jnp.bfloat16))
            sum_scratch.append(pltpu.VMEM((part, columns), jnp.bfloat16))
            sum_outputs.append(((part, columns), jnp.float32, True))

        def body(links, ins, outs, rest):
            near_refs, ins = ins[:count_near], ins[count_near:]
            shard_refs, ins = ins[: len(moving)], ins[len(moving) :]
            line_refs, sum_refs = ins[: len(lines)], ins[len(lines) :]
            kind_refs, outs = outs[:count_kinds], outs[count_kinds:]
            if gather:
                whole_ref, outs = outs[0], outs[1:]
            full_refs, outs = outs[: len(moving)], outs[len(moving) :]
            line_outs, outs = outs[: len(lines)], outs[len(lines) :]
            job_refs, added_refs = outs[: len(jobs)], outs[len(jobs) :]
            partial_ref, land_right, land_left = rest[:3]
            user, rest = rest[3 : 3 + count_scratch], rest[3 + count_scratch :]
            job_rest, sum_rest = rest[: len(job_scratch)], rest[len(job_scratch) :]

            groups = {"zall"} if exchange else {"line"}
            if moving or adding or jobs:
                groups |= {"bits"} if self.cube else set()
            if adding or here:
                groups |= {"diag"}
            links.greet(groups)
            gathers = [CubeGather(links, a, b) for a, b in zip(shard_refs, full_refs)]
            straight = [
                DirectGather(links, b, a.shape[0]) for a, b in zip(line_refs, line_outs)
            ]
            old = [
                ChipSum(links, a, b, sum_rest[2 * k], sum_rest[2 * k + 1])
                for k, (a, b) in enumerate(zip(sum_refs, added_refs))
            ]
            for item in gathers + old:
                item.start()
            copies = []
            for item, source in zip(straight, line_refs):
                item.start(source)
                copies.append(
                    links.here(source, piece_of(item.whole, links.z, item.rows, 0, item.rows))
                )
                copies[-1].start()
            state = begin(links, near_refs, kind_refs, user) if begin else None
            pre(links, near_refs, kind_refs, user, partial_ref)

            queue = list(tasks(near_refs, kind_refs, user)) if tasks else []
            fresh, busy, cleared = [], {}, []
            for (left, right, part, columns, now), seat in zip(jobs, seats):
                left_ref, right_ref = left(near_refs, kind_refs, user), right(near_refs, kind_refs, user)
                out = job_refs[seat[-1]]
                if not self.cube:

                    def whole(start, left_ref=left_ref, right_ref=right_ref, out=out):
                        count = out.shape[0] // 4
                        where = slice(start * count, (start + 1) * count)
                        out[where, :] = weight_grad(left_ref[:, where], right_ref[...]).astype(
                            jnp.bfloat16
                        )

                    queue += [functools.partial(whole, start) for start in range(4)]
                    continue
                held = job_rest[seat[1]] if now else out
                item = CoreSum(links, left_ref, right_ref, job_rest[seat[0]], held)
                if seat[0] in busy:
                    queue.append(busy[seat[0]].clear)
                    cleared.append(busy[seat[0]])
                busy[seat[0]] = item
                queue += item.steps()
                if now:
                    chip = ChipSum(links, held, out, job_rest[seat[1] + 1])
                    queue.append(chip.start)
                    fresh.append(chip)
            queue += [item.forward for item in gathers]
            queue += [item.tail for item in gathers]

            reduce = LineReduce(links, partial_ref, land_right, land_left, rows, pieces)
            line = LineGather(links, whole_ref, rows, pieces) if gather else None
            for piece in range(pieces):
                reduce.first(piece)
            reduce.clear()

            def settle(piece):
                where = pl.ds(piece * (rows // pieces), rows // pieces)
                result = post(reduce.total(piece), where, near_refs, kind_refs, piece == 0)
                if gather:
                    line.block(links.z, piece)[...] = result
                    line.start(piece)

            stages = reduce_stages(reduce) + [settle]
            if gather:
                stages += [functools.partial(line.step, hop) for hop in range(links.size - 1)]
            wave(stages, pieces, queue)
            for item in gathers + old + fresh + straight:
                item.finish()
            for item in busy.values():
                item.clear()
            for copy in copies:
                copy.wait()
            if end:
                end(state, links, near_refs, kind_refs, user)
            reduce.finish()
            if gather:
                line.finish()

        inputs = [(item, True) for item in near]
        inputs += [(item, False) for item in moving + lines + adding]
        outputs = [(form, kind, True) for form, kind in kinds]
        if gather:
            outputs.append(((length, width), jnp.bfloat16, True))
        outputs += self.gather_outputs(moving)
        outputs += [
            ((item.shape[0] * self.tensor, item.shape[1]), item.dtype, False) for item in lines
        ]
        outputs += job_outputs + sum_outputs
        results = list(
            self.call(
                name,
                body,
                inputs,
                outputs,
                [
                    pltpu.VMEM((length, width), jnp.bfloat16),
                    pltpu.VMEM((self.tensor - 1, rows, width), jnp.bfloat16),
                    pltpu.VMEM((self.tensor - 1, rows, width), jnp.bfloat16),
                    *scratch,
                    *job_scratch,
                    *sum_scratch,
                ],
                240,
            )
        )
        kept, results = results[:count_kinds], results[count_kinds:]
        whole, results = (results[0], results[1:]) if gather else (None, results)
        full, results = self.gathered(results[: len(moving)], shards), results[len(moving) :]
        lined, results = results[: len(lines)], results[len(lines) :]
        made, added = results[: len(jobs)], results[len(jobs) :]
        if not self.cube:
            made = [
                self.scatter(item) if job[4] else item for item, job in zip(made, jobs)
            ]
            added = [self.scatter(item) for item in sums]
        return kept, whole, full, lined, made, added

    def scatter(self, grad):
        return lax.psum_scatter(grad, "dp", scatter_dimension=0, tiled=True).astype(jnp.float32)

    def close(self, time_part, gain_part):
        bits = [1 << k for k in range(self.dp.bit_length() - 1)]

        def body(links, ins, outs, scratch):
            time_ref, gain_ref = ins[:2]
            total_ref, all_ref, gains_ref = outs[:3]
            land, held, held_gain, come, come_gain = scratch[:5]
            links.greet({"zall", "bits"})
            moves = []
            for step in range(1, self.tensor):
                target = lax.rem(links.z + step, self.tensor)
                move = links.copy(time_ref, land.at[links.z], (links.dp, target), links.slot())
                move.start()
                moves.append(move)
            land[links.z] = time_ref[...]
            held_gain[0] = gain_ref[...]
            for move in moves:
                move.wait_recv()
            total = land[0]
            for index in range(1, self.tensor):
                total = total + land[index]
            total_ref[...] = total
            held[0] = total
            for index, bit in enumerate(bits):
                target = (flip(links.dp, bit), links.z)
                one = links.copy(held.at[index], come.at[index], target, links.slot())
                two = links.copy(held_gain.at[index], come_gain.at[index], target, links.slot())
                one.start()
                two.start()
                one.wait_recv()
                two.wait_recv()
                held[index + 1] = held[index] + come[index]
                held_gain[index + 1] = held_gain[index] + come_gain[index]
                moves += [one, two]
            all_ref[...] = held[len(bits)]
            gains_ref[...] = held_gain[len(bits)]
            for move in moves:
                move.wait_send()

        levels = len(bits)
        results = self.call(
            "close",
            body,
            [(time_part, True), (gain_part, True)],
            [
                (time_part.shape, jnp.float32, True),
                (time_part.shape, jnp.float32, True),
                (gain_part.shape, jnp.float32, True),
            ],
            [
                pltpu.VMEM((self.tensor, *time_part.shape), jnp.float32),
                pltpu.VMEM((levels + 1, *time_part.shape), jnp.float32),
                pltpu.VMEM((levels + 1, *gain_part.shape), jnp.float32),
                pltpu.VMEM((levels, *time_part.shape), jnp.float32),
                pltpu.VMEM((levels, *gain_part.shape), jnp.float32),
            ],
            80,
        )
        return results


def add_sum(ref, row, values, first):
    total = jnp.sum(values, axis=0, keepdims=True)
    ref[row : row + 1, :] = total if first else ref[row : row + 1, :] + total


def tiles(count, size):
    return [(start, min(size, count - start)) for start in range(0, count, size)]


def body(
    plan,
    hidden_in,
    text_states,
    time_embed,
    positions,
    modulation,
    query_weight,
    key_weight,
    value_weight,
    out_weight,
    cross_query,
    cross_key,
    cross_value,
    cross_out,
    up_weight,
    down_weight,
    qk_gain,
    norm_gain,
    cotangent,
):
    plan.calls = 0
    low, full_type = jnp.bfloat16, jnp.float32
    rows, width = hidden_in.shape
    length = rows * plan.tensor
    here = out_weight.shape[0]
    heads = here // HEAD_DIM
    hidden_units = up_weight.shape[1]
    text_rows, text_width = length, text_states.shape[1]
    part = width // plan.dp
    text_part = text_width // plan.dp
    shape = (length, width)

    top = jnp.concatenate([modulation, norm_gain[None], jnp.zeros((1, part), low)], axis=0)
    side = jnp.pad(qk_gain, ((0, 8 - heads), (0, 0)))
    small = jnp.concatenate([top, side], axis=1).astype(full_type)
    time_rows = jnp.pad(time_embed[0], ((0, 2), (0, 0)))
    (mixing, gains, self_whole), full = plan.open(
        hidden_in, time_rows, small, [query_weight, key_weight, value_weight, out_weight.T]
    )
    query_full, key_full, value_full, out_full = full
    cosine, sine = rotary_tables(positions, HEAD_DIM)

    def forward(kinds_of_gain, angles, inputs, weights, gain_ref, kinds, scratch, links, partial):
        query_in, other_in = inputs
        query_w, key_w, value_w, out_w = weights
        query_raw, key_raw, value, query, key, attended, logs, inverse = kinds
        exchange = Exchange(links, *scratch)
        key_raw[...] = jnp.dot(other_in[...], key_w[...], preferred_element_type=full_type)
        query_raw[...] = jnp.dot(query_in[...], query_w[...], preferred_element_type=full_type)
        exchange.start(square_columns(query_raw[...], key_raw[...]))
        value[...] = jnp.dot(
            other_in[...], value_w[...], preferred_element_type=full_type
        ).astype(low)
        inverse[...] = exchange.finish(lambda total: lax.rsqrt(total / D + EPSILON))
        for index, (raw, out) in enumerate(((query_raw, query), (key_raw, key))):
            shape_norm(
                raw,
                inverse[:, index : index + 1],
                gains_of(gain_ref, kinds_of_gain[index], heads),
                angles,
                out,
                heads,
            )
        attend(query, key, value, attended, logs, heads)
        for start, size in tiles(width, 512):
            partial[:, start : start + size] = product_back(
                attended[...], out_w[start : start + size, :]
            ).astype(low)

    kept_kinds = [
        ((length, here), full_type),
        ((length, here), full_type),
        ((length, here), low),
        ((length, here), low),
        ((length, here), low),
        ((length, here), low),
        ((length, HEAD_DIM), full_type),
        ((length, HEAD_DIM), full_type),
    ]

    def self_pre(links, near, kinds, scratch, partial):
        whole, gain_ref, cosine_ref, sine_ref = near[:4]
        forward(
            (0, 1),
            (cosine_ref, sine_ref),
            (whole, whole),
            near[4:8],
            gain_ref,
            kinds[:8],
            scratch,
            links,
            partial,
        )

    def after_self(total, where, near, kinds, first):
        hidden_ref, mixing_ref = near[8:]
        branch_ref, resid_ref = kinds[8:]
        branch_ref[where, :] = total
        resid = hidden_ref[where, :] + total * mixing_ref[2:3]
        resid_ref[where, :] = resid
        unit, _ = normed(resid)
        return (unit * mixing_ref[6:7]).astype(low)

    kept, cross_whole, full, (text_all,), _, _ = plan.phase(
        "self_forward",
        [self_whole, gains, cosine, sine, query_full, key_full, value_full, out_full]
        + [hidden_in, mixing],
        kept_kinds + [((rows, width), full_type)] * 2,
        exchange_scratch(length, plan.tensor),
        self_pre,
        after_self,
        True,
        shape,
        shards=[cross_key, cross_value, cross_query, cross_out.T],
        lines=[text_states],
    )
    self_kept, (self_branch, resid_self) = kept[:8], kept[8:]
    cross_key_full, cross_value_full, cross_query_full, cross_out_full = full

    def cross_begin(links, near, kinds, scratch):
        mixing_ref, cotangent_ref = near[8:]
        whole = kinds[9]
        mine = piece_of(whole, links.z, rows, 0, rows)
        mine[...] = (cotangent_ref[...] * mixing_ref[5:6]).astype(low)
        line = DirectGather(links, whole, rows)
        line.start(mine)
        return line

    def cross_end(line, links, near, kinds, scratch):
        line.finish()

    def cross_pre(links, near, kinds, scratch, partial):
        whole, text, gain_ref = near[:3]
        forward(
            (2, 3), None, (whole, text), near[3:7], gain_ref, kinds[:8], scratch, links, partial
        )

    def after_cross(total, where, near, kinds, first):
        resid_ref, mixing_ref = near[7:9]
        resid = resid_ref[where, :] + total
        kinds[8][where, :] = resid
        unit, _ = normed(resid)
        return (unit * (1.0 + mixing_ref[4:5]) + mixing_ref[3:4]).astype(low)

    kept, feed_whole, full, _, _, _ = plan.phase(
        "cross_forward",
        [cross_whole, text_all, gains]
        + [cross_query_full, cross_key_full, cross_value_full, cross_out_full]
        + [resid_self, mixing, cotangent],
        kept_kinds + [((rows, width), full_type), ((length, width), low)],
        exchange_scratch(length, plan.tensor),
        cross_pre,
        after_cross,
        True,
        shape,
        shards=[up_weight, down_weight.T],
        begin=cross_begin,
        end=cross_end,
    )
    cross_kept, (resid_cross, feed_grad_whole) = kept[:8], kept[8:]
    up_full, down_full = full

    def feed_pre(links, near, kinds, scratch, partial):
        whole, grad_whole, up, down = near[:4]
        activated, grad_raw = scratch
        root = 0.7978845608028654

        def tile(start, size):
            lanes = pl.ds(start, size)
            for first in range(0, length, 256):
                block = slice(first, first + 256)
                raw = jnp.dot(whole[block, :], up[:, lanes], preferred_element_type=full_type)
                grad = jnp.dot(grad_whole[block, :], down[:, lanes], preferred_element_type=full_type)
                square = raw * raw
                bend = jnp.tanh(root * raw * (1.0 + 0.044715 * square))
                half = 0.5 + 0.5 * bend
                activated[block, lanes] = (raw * half).astype(low)
                slope = half + 0.5 * raw * (1.0 - bend * bend) * root * (
                    1.0 + 3.0 * 0.044715 * square
                )
                grad_raw[block, lanes] = (grad * slope).astype(low)

        whole_tiles = hidden_units // 512

        def one(step, _):
            tile(pl.multiple_of(step * 512, 512), 512)
            return 0

        lax.fori_loop(0, whole_tiles, one, 0)
        if hidden_units % 512:
            tile(whole_tiles * 512, hidden_units % 512)
        for start, size in tiles(width, 512):
            partial[:, start : start + size] = product_back(
                grad_raw[...], up[start : start + size, :]
            ).astype(low)

    def feed_tasks(near, kinds, scratch):
        down, activated = near[3], scratch[0]

        def one(start, size):
            kinds[2][:, start : start + size] = product_back(
                activated[...], down[start : start + size, :]
            ).astype(low)

        return [functools.partial(one, start, size) for start, size in tiles(width, 512)]

    def before_feed(total, where, near, kinds, first):
        resid_ref, cotangent_ref, mixing_ref = near[4:]
        grad_ref, sums_ref = kinds[:2]
        unit, inverse = normed(resid_ref[where, :])
        add_sum(sums_ref, 0, total, first)
        add_sum(sums_ref, 1, total * unit, first)
        grad = cotangent_ref[where, :] + normed_back(
            unit, inverse, total * (1.0 + mixing_ref[4:5])
        )
        grad_ref[where, :] = grad
        return grad.astype(low)

    kept, cross_grad_whole, _, _, made, _ = plan.phase(
        "feed",
        [feed_whole, feed_grad_whole, up_full, down_full, resid_cross, cotangent, mixing],
        [((rows, width), full_type), ((8, width), full_type), ((length, width), low)],
        [pltpu.VMEM((length, hidden_units), low), pltpu.VMEM((length, hidden_units), low)],
        feed_pre,
        before_feed,
        True,
        shape,
        jobs=[
            (lambda n, k, s: n[1], lambda n, k, s: s[0], part, hidden_units, True),
            (lambda n, k, s: n[0], lambda n, k, s: s[1], part, hidden_units, False),
        ],
        tasks=feed_tasks,
        exchange=False,
    )
    grad_resid_cross, feed_sums, feed_partial = kept
    sum_down, near_up = made

    def backward(kinds_of_gain, angles, refs, gain_ref, grad_outs, scratch, links, partial):
        (grad_whole, query_w, key_w, value_w, out_w) = refs[:5]
        query_raw, key_raw, value, query, key, attended, logs, inverse = refs[5:]
        gain_query_ref, gain_key_ref, query_out, key_out, value_out = grad_outs
        grad_attended, grad_query, grad_key, grad_value = scratch[3:7]
        exchange = Exchange(links, *scratch[:3])
        grad_attended[...] = jnp.dot(
            grad_whole[...], out_w[...], preferred_element_type=full_type
        ).astype(low)
        attend_back(
            query, key, value, logs, grad_attended, (grad_query, grad_key, grad_value), heads
        )
        sides = (
            (query_raw, inverse[:, 0:1], gains_of(gain_ref, kinds_of_gain[0], heads)),
            (key_raw, inverse[:, 1:2], gains_of(gain_ref, kinds_of_gain[1], heads)),
        )
        exchange.start(
            [
                norm_dots(*sides[0], angles, grad_query, gain_query_ref, heads),
                norm_dots(*sides[1], angles, grad_key, gain_key_ref, heads),
            ]
        )
        value_out[...] = grad_value[...].astype(low)
        dots = exchange.finish()
        norm_pull(*sides[0], dots[:, 0:1], grad_query, query_out, heads)
        norm_pull(*sides[1], dots[:, 1:2], grad_key, key_out, heads)
        pairs = [(query_out, query_w)]
        if angles is not None:
            pairs += [(key_out, key_w), (value_out, value_w)]
        for start, size in tiles(width, 512):
            total = 0.0
            for grads, weight in pairs:
                total = total + product_back(grads[...], weight[start : start + size, :])
            partial[:, start : start + size] = total.astype(low)

    back_scratch = exchange_scratch(length, plan.tensor) + [
        pltpu.VMEM((length, here), low),
        pltpu.VMEM((length, here), full_type),
        pltpu.VMEM((length, here), full_type),
        pltpu.VMEM((length, here), full_type),
        pltpu.VMEM((length, here), low),
        pltpu.VMEM((length, here), low),
        pltpu.VMEM((length, here), low),
    ]

    def cross_back_begin(links, near, kinds, scratch):
        late = DirectReduce(links, near[22], scratch[10], rows)
        late.start()
        return late

    def cross_back_end(late, links, near, kinds, scratch):
        cotangent_ref, mixing_ref, resid_ref = near[19:22]
        late.arrive()
        for start in range(0, rows, 32):
            where = slice(start, start + 32)
            total = late.total(start, 32)
            kinds[2][where, :] = resid_ref[where, :] + total * mixing_ref[5:6]
            add_sum(kinds[1], 2, cotangent_ref[where, :] * total, start == 0)
        late.finish()

    def cross_back_pre(links, near, kinds, scratch, partial):
        backward(
            (2, 3),
            None,
            near[:13],
            near[13],
            (kinds[4], kinds[5], *scratch[7:10]),
            scratch,
            links,
            partial,
        )

    def cross_back_tasks(near, kinds, scratch):
        key_w, value_w = near[2], near[3]

        def one(start, size):
            block = slice(start, start + size)
            kinds[3][:, block] = (
                product_back(scratch[8][...], key_w[block, :])
                + product_back(scratch[9][...], value_w[block, :])
            ).astype(low)

        return [functools.partial(one, start, size) for start, size in tiles(text_width, 1024)]

    def before_cross(total, where, near, kinds, first):
        resid_ref, grad_ref, branch_ref = near[16:19]
        mixing_ref = near[20]
        out_ref, sums_ref = kinds[:2]
        unit, inverse = normed(resid_ref[where, :])
        add_sum(sums_ref, 1, total * unit, first)
        grad = grad_ref[where, :] + normed_back(unit, inverse, total * mixing_ref[6:7])
        out_ref[where, :] = grad
        add_sum(sums_ref, 0, grad * branch_ref[where, :], first)
        return (grad * mixing_ref[2:3]).astype(low)

    kept, self_grad_whole, _, _, made, (sum_up,) = plan.phase(
        "cross_back",
        [cross_grad_whole, cross_query_full, cross_key_full, cross_value_full, cross_out_full]
        + list(cross_kept)
        + [gains, cross_whole, text_all]
        + [resid_self, grad_resid_cross, self_branch, cotangent, mixing, resid_cross]
        + [feed_partial],
        [
            ((rows, width), full_type),
            ((8, width), full_type),
            ((rows, width), full_type),
            ((text_rows, text_width), low),
            ((8, HEAD_DIM), full_type),
            ((8, HEAD_DIM), full_type),
        ],
        back_scratch + [pltpu.VMEM((plan.tensor - 1, rows, width), low)],
        cross_back_pre,
        before_cross,
        True,
        shape,
        sums=[near_up],
        jobs=[
            (lambda n, k, s: n[15], lambda n, k, s: s[8], text_part, here, False),
            (lambda n, k, s: n[15], lambda n, k, s: s[9], text_part, here, False),
            (lambda n, k, s: n[14], lambda n, k, s: s[7], part, here, False),
            (lambda n, k, s: n[0], lambda n, k, s: n[10], part, here, False),
        ],
        tasks=cross_back_tasks,
        begin=cross_back_begin,
        end=cross_back_end,
    )
    grad_resid_self, cross_sums, block_out, text_partial, gain_cross_query, gain_cross_key = kept
    grad_text = lax.psum_scatter(
        text_partial, "tensor", scatter_dimension=0, tiled=True
    ).astype(full_type)

    def self_back_pre(links, near, kinds, scratch, partial):
        backward(
            (0, 1),
            (near[14], near[15]),
            near[:13],
            near[13],
            (kinds[2], kinds[3], *scratch[7:10]),
            scratch,
            links,
            partial,
        )

    def before_self(total, where, near, kinds, first):
        hidden_ref, grad_ref, mixing_ref = near[17:]
        out_ref, sums_ref = kinds[:2]
        unit, inverse = normed(hidden_ref[where, :])
        add_sum(sums_ref, 0, total, first)
        add_sum(sums_ref, 1, total * unit, first)
        out_ref[where, :] = grad_ref[where, :] + normed_back(
            unit, inverse, total * (1.0 + mixing_ref[1:2])
        )

    kept, _, _, _, made, sums = plan.phase(
        "self_back",
        [self_grad_whole, query_full, key_full, value_full, out_full]
        + list(self_kept)
        + [gains, cosine, sine, self_whole, hidden_in, grad_resid_self, mixing],
        [
            ((rows, width), full_type),
            ((8, width), full_type),
            ((8, HEAD_DIM), full_type),
            ((8, HEAD_DIM), full_type),
        ],
        back_scratch,
        self_back_pre,
        before_self,
        False,
        shape,
        sums=made,
        jobs=[
            (lambda n, k, s: n[16], lambda n, k, s: s[7], part, here, True),
            (lambda n, k, s: n[16], lambda n, k, s: s[8], part, here, True),
            (lambda n, k, s: n[16], lambda n, k, s: s[9], part, here, True),
            (lambda n, k, s: n[0], lambda n, k, s: n[10], part, here, True),
        ],
    )
    grad_hidden, self_sums, gain_query, gain_key = kept
    sum_cross_key, sum_cross_value, sum_cross_query, sum_cross_out = sums
    sum_query, sum_key, sum_value, sum_out = made

    time_part = jnp.concatenate(
        [
            self_sums[:2],
            cross_sums[:1],
            feed_sums[:2],
            cross_sums[2:3],
            cross_sums[1:2],
            jnp.zeros((1, width), full_type),
        ],
        axis=0,
    )
    gain_part = jnp.concatenate([gain_query, gain_key, gain_cross_query, gain_cross_key], axis=1)
    time_total, all_total, gain_total = plan.close(time_part, gain_part)
    dp = lax.axis_index("dp")
    mine = lax.dynamic_slice_in_dim(all_total, dp * part, part, axis=1)
    gain_width = qk_gain.shape[1]
    gain_mine = lax.dynamic_slice_in_dim(gain_total[:heads], dp * gain_width, gain_width, axis=1)
    return (
        block_out,
        grad_hidden,
        grad_text,
        time_total[None, :6],
        mine[:6],
        sum_query,
        sum_key,
        sum_value,
        sum_out.T,
        sum_cross_query,
        sum_cross_key,
        sum_cross_value,
        sum_cross_out.T,
        sum_up,
        sum_down.T,
        gain_mine,
        mine[6],
    )


def solution(mesh):
    return jax.shard_map(
        functools.partial(body, Plan(mesh)),
        mesh=mesh,
        in_specs=(
            P(("dp", "tensor"), None),
            P(("dp", "tensor"), None),
            P("dp", None, None),
            P(None, "dp"),
            P(None, "dp"),
            P("dp", "tensor"),
            P("dp", "tensor"),
            P("dp", "tensor"),
            P("tensor", "dp"),
            P("dp", "tensor"),
            P("dp", "tensor"),
            P("dp", "tensor"),
            P("tensor", "dp"),
            P("dp", "tensor"),
            P("tensor", "dp"),
            P("tensor", "dp"),
            P("dp"),
            P(("dp", "tensor"), None),
        ),
        out_specs=(
            P(("dp", "tensor"), None),
            P(("dp", "tensor"), None),
            P(("dp", "tensor"), None),
            P("dp", None, None),
            P(None, "dp"),
            P("dp", "tensor"),
            P("dp", "tensor"),
            P("dp", "tensor"),
            P("tensor", "dp"),
            P("dp", "tensor"),
            P("dp", "tensor"),
            P("dp", "tensor"),
            P("tensor", "dp"),
            P("dp", "tensor"),
            P("tensor", "dp"),
            P("tensor", "dp"),
            P("dp"),
        ),
        check_vma=False,
    )
```

time: 844 us -> 725 us (0.86)
  matrix products: 127 us -> 0 us
  Pallas kernels: 585 us -> 673 us
  local copies, waits for them, and re-layouts: 63.3 us -> 22.9 us
  other arithmetic: 47.5 us -> 7.76 us
    dot_general x42 -> x0, matrix products: 127 us -> none  [the longest x10 35 us: weight_grad(): lax.dot_general(inputs, grads, CONTRACT_FIRST, preferred_element_type=jnp...]
    pallas_call x11 -> x7, Pallas kernels: 585 us -> 673 us  [call(): pl.pallas_call(kernel, name=name, out_shape=[jax.ShapeDtypeStruct(shape,...]
    convert_element_type x4 -> x0, local copies, waits for them, and re-layouts: 21.2 us -> none  [the longest x1 10.1 us: body(): grad_up = weight_grad(feed_whole, grad_up_raw).astype(low)]
    convert_element_type x11 -> x2, other arithmetic: 17 us -> 3.5 us  [the longest x1 2.83 us: body(): grad_text = lax.psum_scatter(text_partial, 'tensor', scatter_dimension=0,...]
    reduce_sum x6 -> x0, other arithmetic: 9.38 us -> none  [the longest x4 8.31 us: scaled(): return values * lax.rsqrt(total[:, None] / D + EPSILON) * gain]
    unnamed x181 -> x46, local copies, waits for them, and re-layouts: 17 us -> 13.1 us
  transfers between devices with their start and end apart: 3 -> 1, of which waited for: 0 -> 0; matrix products, arithmetic and copies ran while one was open for 15% -> 1% of each run, Pallas kernels for 47% -> 17%
where the time goes in v2:
time: 725 us; the launch traced here: 718 us
  Pallas kernels  673 us (93%)
  local copies, waits for them, and re-layouts  22.9 us (3%)
  between operations  14.7 us (2%)
  other arithmetic  7.76 us (1%)
    pallas_call x7, Pallas kernels, call(): pl.pallas_call(kernel, name=name, out_shape=[jax.ShapeDtypeStruct(shape,...  673 us
  transfers between devices with their start and end apart: 1, of which 0 were waited for; matrix products, arithmetic and copies ran while one was open for 1% of the time, Pallas kernels for 17%

profile of v2, /device:TPU:0, one launch (start us, length us, event | category | flops | bytes accessed | tf_op | source)
XLA Modules:
  0.0 717.9 jit_solution(17100404809407077670)
XLA Ops:
  7.2 0.0 copy-start.12
  7.2 0.0 copy-start.15
  7.2 0.0 reduce-scatter.2.cloned.1.call-start
  7.3 0.7 convert_element_type.14
  8.0 0.1 broadcast_in_dim.33
  8.1 0.1 mul.72
  8.2 0.1 broadcast_in_dim.32
  8.2 0.1 mul.67
  8.3 0.8 copy.39
  9.1 0.7 broadcast_in_dim.30
  9.8 0.1 broadcast_multiply_fusion.2
  9.9 0.6 pad.8.refs_1_
  10.5 0.2 broadcast_multiply_fusion.1
  10.7 1.9 sine_multiply_fusion
  12.6 0.0 copy-done.12
  12.6 0.0 copy-done.15
  12.7 0.7 fusion.2.refs_2_
  13.3 48.4 %open.1 = (f32[8,1536]{1,0:T(8,128)}, f32[8,512]{1,0:T(8,128)}, bf16[512,1536]{1,0:T(8,128)(2,1)}, bf16[1536,384]{1,0:T(8,128)(2,1)}, bf16[1536,384]{1,0:T(8,128...) custom-call(f32[128,1536]{1,0:T(8,128)} %refs_17_.1, f32[8,1536]{1,0:T(8,128)} %pad.8.refs_1_, ...), custom_call_target="tpu_custom_call" | custom-call | tf_op jit(solution)/shard_map/open/pallas_call | solution.py:706
  61.7 165.4 %self_forward.1 = (f32[512,384]{1,0:T(8,128)}, f32[512,384]{1,0:T(8,128)}, bf16[512,384]{1,0:T(8,128)(2,1)}, bf16[512,384]{1,0:T(8,128)(2,1)}, bf16[512,384]{1,0...) custom-call(bf16[512,1536]{1,0:T(8,128)(2,1)} %get-tuple-element.86., ...), custom_call_target="tpu_custom_call" | custom-call | tf_op jit(solution)/shard_map/self_forward/pallas_call | solution.py:706
  227.2 111.5 %cross_forward.1 = (f32[512,384]{1,0:T(8,128)}, f32[512,384]{1,0:T(8,128)}, bf16[512,384]{1,0:T(8,128)(2,1)}, bf16[512,384]{1,0:T(8,128)(2,1)}, bf16[512,384]{1,...) custom-call(bf16[512,1536]{1,0:T(8,128)(2,1)} %get-tuple-element.93., ...), custom_call_target="tpu_custom_call" | custom-call | tf_op jit(solution)/shard_map/cross_forward/pallas_call | solution.py:706
  338.7 109.8 %feed.1 = (f32[128,1536]{1,0:T(8,128)}, f32[8,1536]{1,0:T(8,128)}, bf16[512,1536]{1,0:T(8,128)(2,1)}, bf16[512,1536]{1,0:T(8,128)(2,1)}, f32[192,2240]{1,0:T(8,128)}, /*index=5*/bf16[4,192,2240]{2,1,0:T(8,128)(2,1)}) custom-call(bf16[512,1536]{1,0:T(8,128)(2,1)} %get-tuple-element.100.refs_0_, bf16[512,1536]{1,0:T(8,128)(2,1)} %get-tuple-element.101.refs_1_, ...), custom_call_target="tpu_custom_call" | custom-call | tf_op jit(solution)/shard_map/feed/pallas_call | solution.py:706
  448.5 112.7 %cross_back.1 = (f32[128,1536]{1,0:T(8,128)}, f32[8,1536]{1,0:T(8,128)}, f32[128,1536]{1,0:T(8,128)}, bf16[512,4096]{1,0:T(8,128)(2,1)}, f32[8,128]{1,0:T(8,128)...) custom-call(bf16[512,1536]{1,0:T(8,128)(2,1)} %get-tuple-element.105, ...), custom_call_target="tpu_custom_call" | custom-call | tf_op jit(solution)/shard_map/cross_back/pallas_call | solution.py:706
  561.2 0.0 reduce-scatter.2.cloned.1.call-update
  561.2 0.0 copy-start.13
  561.2 0.0 copy-start.14
  561.2 101.2 %self_back.1 = (f32[128,1536]{1,0:T(8,128)}, f32[8,1536]{1,0:T(8,128)}, f32[8,128]{1,0:T(8,128)}, f32[8,128]{1,0:T(8,128)}, f32[192,384]{1,0:T(8,128)}, /*index=...) custom-call(bf16[512,1536]{1,0:T(8,128)(2,1)} %get-tuple-element.119, ...), custom_call_target="tpu_custom_call" | custom-call | tf_op jit(solution)/shard_map/self_back/pallas_call | solution.py:706
  662.4 0.8 slice.39
  663.2 0.8 slice.41
  664.0 0.9 fusion.4
  665.0 0.7 concatenate.18.refs_0_
  665.7 0.0 copy-done.13
  665.7 0.0 copy-done.14
  665.7 1.3 pad_maximum_fusion.1.refs_1_
  667.0 23.6 %close.1 = (f32[8,1536]{1,0:T(8,128)}, f32[8,1536]{1,0:T(8,128)}, f32[8,512]{1,0:T(8,128)}) custom-call(f32[8,1536]{1,0:T(8,128)} %concatenate.18.refs_0_, f32[8,512]{1,0:T(8,128)} %pad_maximum_fusion.1.refs_1_), custom_call_target="tpu_custom_call" | custom-call | tf_op jit(solution)/shard_map/close/pallas_call | solution.py:706
  690.6 0.8 slice_bitcast_fusion
  691.4 0.7 copy.36
  692.0 0.7 slice.46
  692.7 1.3 dynamic-slice.1
  694.1 0.6 constant_dynamic-slice_fusion.1
  694.7 1.4 constant_dynamic-slice_fusion
  696.1 2.8 convert_element_type.15
  698.9 0.0 copy-done.2
  699.0 0.9 copy.52
  699.8 0.5 copy-done.5
  700.4 0.9 copy.53
  701.2 0.0 copy-done.11
  701.3 0.7 copy.54
  702.0 0.0 copy-done.10
  702.0 0.7 copy.55
  702.7 0.0 copy-done.9
  702.7 0.7 copy.56
  703.4 0.0 copy-done.8
  703.4 0.7 copy.57
  704.1 0.0 copy-done.7
  704.1 0.7 copy.58
  704.8 0.0 copy-done.4
  704.8 0.9 copy.59
  705.7 0.0 copy-done.3
  705.7 0.9 copy.60
  706.6 0.0 copy-done.6
  706.6 0.7 copy.61
  707.3 1.2 copy.62
  708.5 0.9 copy-done
  709.4 1.2 copy.63
  (20 shorter events, 0.1 us)
Async XLA Ops:
  7.2 5.5 copy-start.12
  7.2 5.5 copy-start.15
  7.2 688.9 %reduce-scatter.2.cloned.1.call-start = ((), (), s32[]{:S(2)}) async-start(), calls=%async_computation.1 | async-start | bytes 5242880 | tf_op jit(solution)/shard_map/reduce_scatter | solution.py:1427
  561.2 104.4 %copy-start.13 = (f32[8,128]{1,0:T(8,128)S(1)}, f32[8,128]{1,0:T(8,128)}, u32[]{:S(2)}) copy-start(f32[8,128]{1,0:T(8,128)} %get-tuple-element.140) | copy-start | bytes 12292
  561.2 104.4 %copy-start.14 = (f32[8,128]{1,0:T(8,128)S(1)}, f32[8,128]{1,0:T(8,128)}, u32[]{:S(2)}) copy-start(f32[8,128]{1,0:T(8,128)} %get-tuple-element.141) | copy-start | bytes 12292
  696.1 2.8 copy-start.2
  698.9 1.4 copy-start.5
  698.9 2.3 copy-start.11
  699.0 3.0 copy-start.10
  700.4 2.3 copy-start.9
  700.4 3.0 copy-start.8
  700.4 3.8 copy-start.7
  701.3 3.6 copy-start.4
  702.7 3.0 copy-start.3
  704.8 1.8 copy-start.6
  704.8 2.5 copy-start.1
  707.3 2.1 copy-start
Sparse Core Ops, SparseCore 0:
  561.3 100.3 reduce-scatter.1

commit v3 on v2

--- a/solution.py
+++ b/solution.py
@@ -8,7 +8,7 @@
 from jax.sharding import PartitionSpec as P
 
 MESH = pl.DeviceIdType.MESH
-VMEM_BYTES = 60 * 2**20
+VMEM_BYTES = 62 * 2**20
 
 HEAD_DIM = 128
 D = 1536
@@ -245,6 +245,27 @@
         when(z == 0, from_first)
         when(z == last, from_last)
 
+    def first_at(self, distance, piece):
+        z, last = self.links.z, self.links.size - 1
+        when(
+            z == 0,
+            lambda: self.move(self.part(distance, piece), 1, distance, piece).start(),
+        )
+        when(
+            z == last,
+            lambda: self.move(self.part(last - distance, piece), -1, distance, piece).start(),
+        )
+
+    def stages(self, piece):
+        last = self.links.size - 1
+
+        def one(distance):
+            self.first_at(distance, piece)
+            if distance < last:
+                self.step(distance, piece)
+
+        return [functools.partial(one, distance) for distance in range(last, 0, -1)]
+
     def clear(self):
         z, last = self.links.z, self.links.size - 1
 
@@ -397,41 +418,6 @@
     def finish(self):
         for move in self.moves:
             move.wait_recv()
-        for move in self.moves:
-            move.wait_send()
-
-
-class DirectReduce:
-    def __init__(self, links, partial, land, rows):
-        self.links, self.partial, self.land, self.rows = links, partial, land, rows
-        self.slots = [links.slot() for _ in range(links.size - 1)]
-
-    def start(self):
-        links = self.links
-        self.moves = []
-        for step, slot in enumerate(self.slots, 1):
-            target = lax.rem(links.z + step, links.size)
-            move = links.copy(
-                piece_of(self.partial, target, self.rows, 0, self.rows),
-                self.land.at[step - 1],
-                (links.dp, target),
-                slot,
-            )
-            move.start()
-            self.moves.append(move)
-
-    def arrive(self):
-        for move in self.moves:
-            move.wait_recv()
-
-    def total(self, start, count):
-        total = piece_of(self.partial, self.links.z, self.rows, start, count)[...]
-        total = total.astype(jnp.float32)
-        for index in range(self.links.size - 1):
-            total = total + self.land[index, start : start + count, :].astype(jnp.float32)
-        return total
-
-    def finish(self):
         for move in self.moves:
             move.wait_send()
 
@@ -811,11 +797,12 @@
         begin=None,
         end=None,
         exchange=True,
+        far=(),
     ):
         length, width = shape
         rows = length // self.tensor
         pieces = self.pieces
-        shards, lines, sums = list(shards), list(lines), list(sums)
+        shards, lines, sums, far = list(shards), list(lines), list(sums), list(far)
         moving = shards if self.cube else []
         adding = sums if self.cube else []
         jobs = list(jobs)
@@ -839,8 +826,9 @@
                 job_scratch.append(pltpu.VMEM((3, part, columns), jnp.bfloat16))
                 job_outputs.append(((part, columns), jnp.float32, True))
             else:
-                seats.append((products[key], None, len(job_outputs)))
-                job_outputs.append(((4, part, columns), jnp.bfloat16, True))
+                seats.append((products[key], len(job_scratch), len(job_outputs)))
+                job_scratch.append(pltpu.VMEM((4, part, columns), jnp.bfloat16))
+                job_outputs.append(((4, part, columns), jnp.bfloat16, False))
         sum_scratch, sum_outputs = [], []
         for item in adding:
             _, part, columns = item.shape
@@ -849,15 +837,47 @@
             sum_outputs.append(((part, columns), jnp.float32, True))
 
         def body(links, ins, outs, rest):
-            near_refs, ins = ins[:count_near], ins[count_near:]
+            near_far, ins = ins[:count_near], ins[count_near:]
             shard_refs, ins = ins[: len(moving)], ins[len(moving) :]
-            line_refs, sum_refs = ins[: len(lines)], ins[len(lines) :]
-            kind_refs, outs = outs[:count_kinds], outs[count_kinds:]
+            line_refs, ins = ins[: len(lines)], ins[len(lines) :]
+            sum_refs, far_refs = ins[: len(adding)], ins[len(adding) :]
+            kind_far, outs = outs[:count_kinds], outs[count_kinds:]
             if gather:
-                whole_ref, outs = outs[0], outs[1:]
+                whole_far, outs = outs[0], outs[1:]
             full_refs, outs = outs[: len(moving)], outs[len(moving) :]
             line_outs, outs = outs[: len(lines)], outs[len(lines) :]
             job_refs, added_refs = outs[: len(jobs)], outs[len(jobs) :]
+            near_refs, rest = rest[:count_near], rest[count_near:]
+            loads = {}
+            for index in order:
+                copy = links.here(near_far[index], near_refs[index])
+                copy.start()
+                loads.setdefault(near[index][1], []).append(copy)
+
+            def ready(group):
+                for copy in loads.pop(group, []):
+                    copy.wait()
+
+            links.ready = ready
+            kind_refs, stores = [], []
+            for far_ref, (_, _, when_done) in zip(kind_far, kinds):
+                if when_done is None:
+                    kind_refs.append(far_ref)
+                else:
+                    kind_refs.append(rest[0])
+                    rest = rest[1:]
+
+            def store(source, target):
+                stores.append(links.here(source, target))
+                stores[-1].start()
+
+            def store_kinds(moment):
+                for held, far_ref, (_, _, when_done) in zip(kind_refs, kind_far, kinds):
+                    if when_done == moment:
+                        store(held, far_ref)
+
+            if gather:
+                whole_ref, rest = rest[0], rest[1:]
             partial_ref, land_right, land_left = rest[:3]
             user, rest = rest[3 : 3 + count_scratch], rest[3 + count_scratch :]
             job_rest, sum_rest = rest[: len(job_scratch)], rest[len(job_scratch) :]
@@ -885,10 +905,16 @@
                     links.here(source, piece_of(item.whole, links.z, item.rows, 0, item.rows))
                 )
                 copies[-1].start()
-            state = begin(links, near_refs, kind_refs, user) if begin else None
-            pre(links, near_refs, kind_refs, user, partial_ref)
-
-            queue = list(tasks(near_refs, kind_refs, user)) if tasks else []
+            state = begin(links, near_refs, kind_refs, user, far_refs) if begin else (None, [])
+            ticks = state[1]
+            pre(links, near_refs, kind_refs, user, partial_ref, ticks)
+            for run in ticks:
+                run()
+            store_kinds("pre")
+            for group in sorted(loads):
+                ready(group)
+
+            queue = list(tasks(links, near_refs, kind_refs, user, far_refs)) if tasks else []
             fresh, busy, cleared = [], {}, []
             for (left, right, part, columns, now), seat in zip(jobs, seats):
                 left_ref, right_ref = left(near_refs, kind_refs, user), right(near_refs, kind_refs, user)
@@ -904,7 +930,7 @@
 
                     queue += [functools.partial(whole, start) for start in range(4)]
                     continue
-                held = job_rest[seat[1]] if now else out
+                held = job_rest[seat[1]]
                 item = CoreSum(links, left_ref, right_ref, job_rest[seat[0]], held)
                 if seat[0] in busy:
                     queue.append(busy[seat[0]].clear)
@@ -915,6 +941,8 @@
                     chip = ChipSum(links, held, out, job_rest[seat[1] + 1])
                     queue.append(chip.start)
                     fresh.append(chip)
+                else:
+                    queue.append(functools.partial(store, held, out))
             queue += [item.forward for item in gathers]
             queue += [item.tail for item in gathers]
 
@@ -942,16 +970,22 @@
             for copy in copies:
                 copy.wait()
             if end:
-                end(state, links, near_refs, kind_refs, user)
+                end(state[0], links, near_refs, kind_refs, user)
+            store_kinds("post")
+            if gather:
+                store(whole_ref, whole_far)
             reduce.finish()
             if gather:
                 line.finish()
-
-        inputs = [(item, True) for item in near]
-        inputs += [(item, False) for item in moving + lines + adding]
-        outputs = [(form, kind, True) for form, kind in kinds]
+            for copy in stores:
+                copy.wait()
+
+        order = sorted(range(count_near), key=lambda index: near[index][1])
+        inputs = [(item, False) for item, _ in near]
+        inputs += [(item, False) for item in moving + lines + adding + far]
+        outputs = [(form, kind, False) for form, kind, _ in kinds]
         if gather:
-            outputs.append(((length, width), jnp.bfloat16, True))
+            outputs.append(((length, width), jnp.bfloat16, False))
         outputs += self.gather_outputs(moving)
         outputs += [
             ((item.shape[0] * self.tensor, item.shape[1]), item.dtype, False) for item in lines
@@ -963,7 +997,10 @@
                 body,
                 inputs,
                 outputs,
-                [
+                [pltpu.VMEM(item.shape, item.dtype) for item, _ in near]
+                + [pltpu.VMEM(form, kind) for form, kind, moment in kinds if moment]
+                + ([pltpu.VMEM((length, width), jnp.bfloat16)] if gather else [])
+                + [
                     pltpu.VMEM((length, width), jnp.bfloat16),
                     pltpu.VMEM((self.tensor - 1, rows, width), jnp.bfloat16),
                     pltpu.VMEM((self.tensor - 1, rows, width), jnp.bfloat16),
@@ -1055,6 +1092,11 @@
     ref[row : row + 1, :] = total if first else ref[row : row + 1, :] + total
 
 
+def tick(ticks):
+    if ticks:
+        ticks.pop(0)()
+
+
 def tiles(count, size):
     return [(start, min(size, count - start)) for start in range(0, count, size)]
 
@@ -1102,18 +1144,23 @@
     query_full, key_full, value_full, out_full = full
     cosine, sine = rotary_tables(positions, HEAD_DIM)
 
-    def forward(kinds_of_gain, angles, inputs, weights, gain_ref, kinds, scratch, links, partial):
+    def forward(kinds_of_gain, angles, inputs, weights, gain_ref, kinds, scratch, links, partial, ticks):
         query_in, other_in = inputs
         query_w, key_w, value_w, out_w = weights
         query_raw, key_raw, value, query, key, attended, logs, inverse = kinds
         exchange = Exchange(links, *scratch)
+        links.ready(0)
+        query_raw[...] = jnp.dot(query_in[...], query_w[...], preferred_element_type=full_type)
+        links.ready(1)
         key_raw[...] = jnp.dot(other_in[...], key_w[...], preferred_element_type=full_type)
-        query_raw[...] = jnp.dot(query_in[...], query_w[...], preferred_element_type=full_type)
         exchange.start(square_columns(query_raw[...], key_raw[...]))
+        links.ready(2)
         value[...] = jnp.dot(
             other_in[...], value_w[...], preferred_element_type=full_type
         ).astype(low)
         inverse[...] = exchange.finish(lambda total: lax.rsqrt(total / D + EPSILON))
+        tick(ticks)
+        links.ready(3)
         for index, (raw, out) in enumerate(((query_raw, query), (key_raw, key))):
             shape_norm(
                 raw,
@@ -1124,23 +1171,25 @@
                 heads,
             )
         attend(query, key, value, attended, logs, heads)
+        tick(ticks)
+        links.ready(4)
         for start, size in tiles(width, 512):
             partial[:, start : start + size] = product_back(
                 attended[...], out_w[start : start + size, :]
             ).astype(low)
 
     kept_kinds = [
-        ((length, here), full_type),
-        ((length, here), full_type),
-        ((length, here), low),
-        ((length, here), low),
-        ((length, here), low),
-        ((length, here), low),
-        ((length, HEAD_DIM), full_type),
-        ((length, HEAD_DIM), full_type),
+        ((length, here), full_type, "pre"),
+        ((length, here), full_type, "pre"),
+        ((length, here), low, "pre"),
+        ((length, here), low, "pre"),
+        ((length, here), low, "pre"),
+        ((length, here), low, "pre"),
+        ((length, HEAD_DIM), full_type, "pre"),
+        ((length, HEAD_DIM), full_type, "pre"),
     ]
 
-    def self_pre(links, near, kinds, scratch, partial):
+    def self_pre(links, near, kinds, scratch, partial, ticks):
         whole, gain_ref, cosine_ref, sine_ref = near[:4]
         forward(
             (0, 1),
@@ -1152,6 +1201,7 @@
             scratch,
             links,
             partial,
+            ticks,
         )
 
     def after_self(total, where, near, kinds, first):
@@ -1163,38 +1213,50 @@
         unit, _ = normed(resid)
         return (unit * mixing_ref[6:7]).astype(low)
 
-    kept, cross_whole, full, (text_all,), _, _ = plan.phase(
+    text_after, self_whole = lax.optimization_barrier((text_states, self_whole))
+    text_all = lax.all_gather(text_after, "tensor", axis=0, tiled=True)
+    kept, cross_whole, full, _, _, _ = plan.phase(
         "self_forward",
-        [self_whole, gains, cosine, sine, query_full, key_full, value_full, out_full]
-        + [hidden_in, mixing],
-        kept_kinds + [((rows, width), full_type)] * 2,
+        [(self_whole, 0), (gains, 3), (cosine, 3), (sine, 3), (query_full, 0), (key_full, 1)]
+        + [(value_full, 2), (out_full, 4), (hidden_in, 5), (mixing, 5)],
+        kept_kinds + [((rows, width), full_type, "post")] * 2,
         exchange_scratch(length, plan.tensor),
         self_pre,
         after_self,
         True,
         shape,
-        shards=[cross_key, cross_value, cross_query, cross_out.T],
-        lines=[text_states],
+        shards=[cross_key, cross_value, cross_query, cross_out.T, up_weight, down_weight.T],
     )
     self_kept, (self_branch, resid_self) = kept[:8], kept[8:]
-    cross_key_full, cross_value_full, cross_query_full, cross_out_full = full
-
-    def cross_begin(links, near, kinds, scratch):
+    cross_key_full, cross_value_full, cross_query_full, cross_out_full = full[:4]
+    up_full, down_full = full[4:]
+
+    def cross_begin(links, near, kinds, scratch, far):
+        links.ready(-1)
         mixing_ref, cotangent_ref = near[8:]
         whole = kinds[9]
         mine = piece_of(whole, links.z, rows, 0, rows)
         mine[...] = (cotangent_ref[...] * mixing_ref[5:6]).astype(low)
-        line = DirectGather(links, whole, rows)
-        line.start(mine)
-        return line
+        line = LineGather(links, whole, rows, 1)
+        line.start(0)
+        return line, [functools.partial(line.step, hop, 0) for hop in range(links.size - 1)]
 
     def cross_end(line, links, near, kinds, scratch):
         line.finish()
 
-    def cross_pre(links, near, kinds, scratch, partial):
+    def cross_pre(links, near, kinds, scratch, partial, ticks):
         whole, text, gain_ref = near[:3]
         forward(
-            (2, 3), None, (whole, text), near[3:7], gain_ref, kinds[:8], scratch, links, partial
+            (2, 3),
+            None,
+            (whole, text),
+            near[3:7],
+            gain_ref,
+            kinds[:8],
+            scratch,
+            links,
+            partial,
+            ticks,
         )
 
     def after_cross(total, where, near, kinds, first):
@@ -1204,33 +1266,49 @@
         unit, _ = normed(resid)
         return (unit * (1.0 + mixing_ref[4:5]) + mixing_ref[3:4]).astype(low)
 
-    kept, feed_whole, full, _, _, _ = plan.phase(
+    kept, feed_whole, _, _, _, _ = plan.phase(
         "cross_forward",
-        [cross_whole, text_all, gains]
-        + [cross_query_full, cross_key_full, cross_value_full, cross_out_full]
-        + [resid_self, mixing, cotangent],
-        kept_kinds + [((rows, width), full_type), ((length, width), low)],
+        [(cross_whole, 0), (text_all, 1), (gains, 3), (cross_query_full, 0), (cross_key_full, 1)]
+        + [(cross_value_full, 2), (cross_out_full, 4), (resid_self, 5), (mixing, -1)]
+        + [(cotangent, -1)],
+        kept_kinds + [((rows, width), full_type, "post"), ((length, width), low, "post")],
         exchange_scratch(length, plan.tensor),
         cross_pre,
         after_cross,
         True,
         shape,
-        shards=[up_weight, down_weight.T],
         begin=cross_begin,
         end=cross_end,
     )
     cross_kept, (resid_cross, feed_grad_whole) = kept[:8], kept[8:]
-    up_full, down_full = full
-
-    def feed_pre(links, near, kinds, scratch, partial):
-        whole, grad_whole, up, down = near[:4]
-        activated, grad_raw = scratch
+
+    feed_tiles = tiles(hidden_units, 512)
+
+    def feed_begin(links, near, kinds, scratch, far):
+        copies = []
+        for start, size in feed_tiles:
+            lanes = pl.ds(start, size)
+            pair = [
+                links.here(far[which].at[:, lanes], scratch[2 + which].at[:, lanes])
+                for which in range(2)
+            ]
+            for copy in pair:
+                copy.start()
+            copies.append(pair)
+        return None, copies
+
+    def feed_pre(links, near, kinds, scratch, partial, copies):
+        whole, grad_whole = near[:2]
+        activated, grad_raw, up, down = scratch
         root = 0.7978845608028654
-
-        def tile(start, size):
-            lanes = pl.ds(start, size)
-            for first in range(0, length, 256):
-                block = slice(first, first + 256)
+        links.ready(0)
+        for (begin, size), pair in zip(feed_tiles, copies):
+            lanes = slice(begin, begin + size)
+            for copy in pair:
+                copy.wait()
+
+            def one(step, _, lanes=lanes):
+                block = pl.ds(pl.multiple_of(step * 256, 256), 256)
                 raw = jnp.dot(whole[block, :], up[:, lanes], preferred_element_type=full_type)
                 grad = jnp.dot(grad_whole[block, :], down[:, lanes], preferred_element_type=full_type)
                 square = raw * raw
@@ -1241,23 +1319,17 @@
                     1.0 + 3.0 * 0.044715 * square
                 )
                 grad_raw[block, lanes] = (grad * slope).astype(low)
-
-        whole_tiles = hidden_units // 512
-
-        def one(step, _):
-            tile(pl.multiple_of(step * 512, 512), 512)
-            return 0
-
-        lax.fori_loop(0, whole_tiles, one, 0)
-        if hidden_units % 512:
-            tile(whole_tiles * 512, hidden_units % 512)
+                return 0
+
+            lax.fori_loop(0, length // 256, one, 0)
+        copies.clear()
         for start, size in tiles(width, 512):
             partial[:, start : start + size] = product_back(
                 grad_raw[...], up[start : start + size, :]
             ).astype(low)
 
-    def feed_tasks(near, kinds, scratch):
-        down, activated = near[3], scratch[0]
+    def feed_tasks(links, near, kinds, scratch, far):
+        activated, down = scratch[0], scratch[3]
 
         def one(start, size):
             kinds[2][:, start : start + size] = product_back(
@@ -1267,7 +1339,7 @@
         return [functools.partial(one, start, size) for start, size in tiles(width, 512)]
 
     def before_feed(total, where, near, kinds, first):
-        resid_ref, cotangent_ref, mixing_ref = near[4:]
+        resid_ref, cotangent_ref, mixing_ref = near[2:]
         grad_ref, sums_ref = kinds[:2]
         unit, inverse = normed(resid_ref[where, :])
         add_sum(sums_ref, 0, total, first)
@@ -1280,35 +1352,46 @@
 
     kept, cross_grad_whole, _, _, made, _ = plan.phase(
         "feed",
-        [feed_whole, feed_grad_whole, up_full, down_full, resid_cross, cotangent, mixing],
-        [((rows, width), full_type), ((8, width), full_type), ((length, width), low)],
-        [pltpu.VMEM((length, hidden_units), low), pltpu.VMEM((length, hidden_units), low)],
+        [(feed_whole, 0), (feed_grad_whole, 0), (resid_cross, 1), (cotangent, 1), (mixing, 1)],
+        [
+            ((rows, width), full_type, "post"),
+            ((8, width), full_type, "post"),
+            ((length, width), low, "post"),
+        ],
+        [pltpu.VMEM((length, hidden_units), low)] * 2
+        + [pltpu.VMEM((width, hidden_units), low)] * 2,
         feed_pre,
         before_feed,
         True,
         shape,
         jobs=[
-            (lambda n, k, s: n[1], lambda n, k, s: s[0], part, hidden_units, True),
+            (lambda n, k, s: n[1], lambda n, k, s: s[0], part, hidden_units, False),
             (lambda n, k, s: n[0], lambda n, k, s: s[1], part, hidden_units, False),
         ],
         tasks=feed_tasks,
+        begin=feed_begin,
+        far=[up_full, down_full],
         exchange=False,
     )
     grad_resid_cross, feed_sums, feed_partial = kept
-    sum_down, near_up = made
-
-    def backward(kinds_of_gain, angles, refs, gain_ref, grad_outs, scratch, links, partial):
+    near_down, near_up = made
+
+    def backward(kinds_of_gain, angles, refs, gain_ref, grad_outs, scratch, links, partial, ticks):
         (grad_whole, query_w, key_w, value_w, out_w) = refs[:5]
         query_raw, key_raw, value, query, key, attended, logs, inverse = refs[5:]
         gain_query_ref, gain_key_ref, query_out, key_out, value_out = grad_outs
         grad_attended, grad_query, grad_key, grad_value = scratch[3:7]
         exchange = Exchange(links, *scratch[:3])
+        links.ready(0)
         grad_attended[...] = jnp.dot(
             grad_whole[...], out_w[...], preferred_element_type=full_type
         ).astype(low)
+        links.ready(1)
         attend_back(
             query, key, value, logs, grad_attended, (grad_query, grad_key, grad_value), heads
         )
+        tick(ticks)
+        links.ready(2)
         sides = (
             (query_raw, inverse[:, 0:1], gains_of(gain_ref, kinds_of_gain[0], heads)),
             (key_raw, inverse[:, 1:2], gains_of(gain_ref, kinds_of_gain[1], heads)),
@@ -1321,8 +1404,10 @@
         )
         value_out[...] = grad_value[...].astype(low)
         dots = exchange.finish()
+        tick(ticks)
         norm_pull(*sides[0], dots[:, 0:1], grad_query, query_out, heads)
         norm_pull(*sides[1], dots[:, 1:2], grad_key, key_out, heads)
+        links.ready(3)
         pairs = [(query_out, query_w)]
         if angles is not None:
             pairs += [(key_out, key_w), (value_out, value_w)]
@@ -1342,48 +1427,77 @@
         pltpu.VMEM((length, here), low),
     ]
 
-    def cross_back_begin(links, near, kinds, scratch):
-        late = DirectReduce(links, near[22], scratch[10], rows)
-        late.start()
-        return late
+    kept_groups = (2, 2, 1, 1, 1, 4, 1, 2)
+
+    def cross_back_begin(links, near, kinds, scratch, far):
+        links.ready(-1)
+        late = LineReduce(links, near[20], scratch[10], scratch[11], rows, 1)
+        late.clear()
+        first, *others = late.stages(0)
+        first()
+        return late, others
 
     def cross_back_end(late, links, near, kinds, scratch):
-        cotangent_ref, mixing_ref, resid_ref = near[19:22]
-        late.arrive()
-        for start in range(0, rows, 32):
-            where = slice(start, start + 32)
-            total = late.total(start, 32)
-            kinds[2][where, :] = resid_ref[where, :] + total * mixing_ref[5:6]
-            add_sum(kinds[1], 2, cotangent_ref[where, :] * total, start == 0)
+        cotangent_ref, mixing_ref, resid_ref = near[17:20]
+        total = late.total(0)
+        kinds[2][...] = resid_ref[...] + total * mixing_ref[5:6]
+        add_sum(kinds[1], 2, cotangent_ref[...] * total, True)
         late.finish()
 
-    def cross_back_pre(links, near, kinds, scratch, partial):
+    def cross_back_pre(links, near, kinds, scratch, partial, ticks):
         backward(
             (2, 3),
             None,
-            near[:13],
-            near[13],
+            (near[0], near[1], None, None, *near[2:11]),
+            near[11],
             (kinds[4], kinds[5], *scratch[7:10]),
             scratch,
             links,
             partial,
-        )
-
-    def cross_back_tasks(near, kinds, scratch):
-        key_w, value_w = near[2], near[3]
-
-        def one(start, size):
-            block = slice(start, start + size)
-            kinds[3][:, block] = (
-                product_back(scratch[8][...], key_w[block, :])
-                + product_back(scratch[9][...], value_w[block, :])
+            ticks,
+        )
+
+    def cross_back_tasks(links, near, kinds, scratch, far):
+        held, loaded = scratch[12:14]
+        size = held.shape[2]
+        out_copies, loads = [], {}
+
+        def load(index):
+            loads[index] = [
+                links.here(weight.at[pl.ds(index * size, size)], loaded.at[index % 2, which])
+                for which, weight in enumerate(far)
+            ]
+            for copy in loads[index]:
+                copy.start()
+
+        def one(index):
+            if index >= 2:
+                out_copies[index - 2].wait()
+            for copy in loads[index]:
+                copy.wait()
+            stage = held.at[index % 2]
+            stage[...] = (
+                product_back(scratch[8][...], loaded[index % 2, 0])
+                + product_back(scratch[9][...], loaded[index % 2, 1])
             ).astype(low)
-
-        return [functools.partial(one, start, size) for start, size in tiles(text_width, 1024)]
+            if index + 2 < text_width // size:
+                load(index + 2)
+            copy = links.here(stage, kinds[3].at[:, pl.ds(index * size, size)])
+            copy.start()
+            out_copies.append(copy)
+
+        def last():
+            for copy in out_copies[-2:]:
+                copy.wait()
+
+        load(0)
+        load(1)
+        steps = [functools.partial(one, index) for index in range(text_width // size)]
+        return steps + [last]
 
     def before_cross(total, where, near, kinds, first):
-        resid_ref, grad_ref, branch_ref = near[16:19]
-        mixing_ref = near[20]
+        resid_ref, grad_ref, branch_ref = near[14:17]
+        mixing_ref = near[18]
         out_ref, sums_ref = kinds[:2]
         unit, inverse = normed(resid_ref[where, :])
         add_sum(sums_ref, 1, total * unit, first)
@@ -1392,43 +1506,45 @@
         add_sum(sums_ref, 0, grad * branch_ref[where, :], first)
         return (grad * mixing_ref[2:3]).astype(low)
 
-    kept, self_grad_whole, _, _, made, (sum_up,) = plan.phase(
+    kept, self_grad_whole, _, _, made, (sum_down, sum_up) = plan.phase(
         "cross_back",
-        [cross_grad_whole, cross_query_full, cross_key_full, cross_value_full, cross_out_full]
-        + list(cross_kept)
-        + [gains, cross_whole, text_all]
-        + [resid_self, grad_resid_cross, self_branch, cotangent, mixing, resid_cross]
-        + [feed_partial],
+        [(cross_grad_whole, 0), (cross_query_full, 3), (cross_out_full, 0)]
+        + list(zip(cross_kept, kept_groups))
+        + [(gains, 2), (cross_whole, 4), (text_all, 4), (resid_self, 4), (grad_resid_cross, 4)]
+        + [(self_branch, 4), (cotangent, 4), (mixing, 4), (resid_cross, 4), (feed_partial, -1)],
         [
-            ((rows, width), full_type),
-            ((8, width), full_type),
-            ((rows, width), full_type),
-            ((text_rows, text_width), low),
-            ((8, HEAD_DIM), full_type),
-            ((8, HEAD_DIM), full_type),
+            ((rows, width), full_type, "post"),
+            ((8, width), full_type, "post"),
+            ((rows, width), full_type, "post"),
+            ((text_rows, text_width), low, None),
+            ((8, HEAD_DIM), full_type, "pre"),
+            ((8, HEAD_DIM), full_type, "pre"),
         ],
-        back_scratch + [pltpu.VMEM((plan.tensor - 1, rows, width), low)],
+        back_scratch
+        + [pltpu.VMEM((plan.tensor - 1, rows, width), low)] * 2
+        + [pltpu.VMEM((2, text_rows, 1024), low), pltpu.VMEM((2, 2, 1024, here), low)],
         cross_back_pre,
         before_cross,
         True,
         shape,
-        sums=[near_up],
+        sums=[near_down, near_up],
         jobs=[
-            (lambda n, k, s: n[15], lambda n, k, s: s[8], text_part, here, False),
-            (lambda n, k, s: n[15], lambda n, k, s: s[9], text_part, here, False),
-            (lambda n, k, s: n[14], lambda n, k, s: s[7], part, here, False),
-            (lambda n, k, s: n[0], lambda n, k, s: n[10], part, here, False),
+            (lambda n, k, s: n[13], lambda n, k, s: s[8], text_part, here, False),
+            (lambda n, k, s: n[13], lambda n, k, s: s[9], text_part, here, False),
+            (lambda n, k, s: n[12], lambda n, k, s: s[7], part, here, False),
+            (lambda n, k, s: n[0], lambda n, k, s: n[8], part, here, False),
         ],
         tasks=cross_back_tasks,
         begin=cross_back_begin,
         end=cross_back_end,
+        far=[cross_key_full, cross_value_full],
     )
     grad_resid_self, cross_sums, block_out, text_partial, gain_cross_query, gain_cross_key = kept
     grad_text = lax.psum_scatter(
         text_partial, "tensor", scatter_dimension=0, tiled=True
     ).astype(full_type)
 
-    def self_back_pre(links, near, kinds, scratch, partial):
+    def self_back_pre(links, near, kinds, scratch, partial, ticks):
         backward(
             (0, 1),
             (near[14], near[15]),
@@ -1438,6 +1554,7 @@
             scratch,
             links,
             partial,
+            ticks,
         )
 
     def before_self(total, where, near, kinds, first):
@@ -1452,14 +1569,15 @@
 
     kept, _, _, _, made, sums = plan.phase(
         "self_back",
-        [self_grad_whole, query_full, key_full, value_full, out_full]
-        + list(self_kept)
-        + [gains, cosine, sine, self_whole, hidden_in, grad_resid_self, mixing],
+        [(self_grad_whole, 0), (query_full, 3), (key_full, 3), (value_full, 3), (out_full, 0)]
+        + list(zip(self_kept, kept_groups))
+        + [(gains, 2), (cosine, 2), (sine, 2), (self_whole, 4), (hidden_in, 4)]
+        + [(grad_resid_self, 4), (mixing, 4)],
         [
-            ((rows, width), full_type),
-            ((8, width), full_type),
-            ((8, HEAD_DIM), full_type),
-            ((8, HEAD_DIM), full_type),
+            ((rows, width), full_type, "post"),
+            ((8, width), full_type, "post"),
+            ((8, HEAD_DIM), full_type, "pre"),
+            ((8, HEAD_DIM), full_type, "pre"),
         ],
         back_scratch,
         self_back_pre,

time: 725 us -> 615 us (0.85)
  Pallas kernels: 673 us -> 562 us
    pallas_call x7, Pallas kernels: 673 us -> 562 us  [call(): pl.pallas_call(kernel, name=name, out_shape=[jax.ShapeDtypeStruct(shape,...]
  transfers between devices with their start and end apart: 1 -> 2, of which waited for: 0 -> 0; matrix products, arithmetic and copies ran while one was open for 1% -> 2% of each run, Pallas kernels for 17% -> 40%
where the time goes in v3:
time: 615 us; the launch traced here: 608 us
  Pallas kernels  562 us (91%)
  local copies, waits for them, and re-layouts  22.9 us (4%)
  between operations  14.7 us (2%)
  other arithmetic  7.74 us (1%)
    pallas_call x7, Pallas kernels, call(): pl.pallas_call(kernel, name=name, out_shape=[jax.ShapeDtypeStruct(shape,...  562 us
    unnamed x44, local copies, waits for them, and re-layouts  13.1 us
  transfers between devices with their start and end apart: 2, of which 0 were waited for; matrix products, arithmetic and copies ran while one was open for 2% of the time, Pallas kernels for 40%

profile of v3, /device:TPU:0, one launch (start us, length us, event | category | flops | bytes accessed | tf_op | source)
XLA Modules:
  0.0 607.7 jit_solution(627290973140052587)
XLA Ops:
  7.2 0.0 copy-start.12
  7.2 0.0 all-gather.2.cloned.1.call-start
  7.2 0.8 copy.39
  8.0 0.7 broadcast_in_dim.30
  8.7 0.6 pad.8.refs_1_
  9.3 1.4 fusion.2.refs_2_
  10.7 48.4 %open.1 = (f32[8,1536]{1,0:T(8,128)}, f32[8,512]{1,0:T(8,128)}, bf16[512,1536]{1,0:T(8,128)(2,1)}, bf16[1536,384]{1,0:T(8,128)(2,1)}, bf16[1536,384]{1,0:T(8,128...) custom-call(f32[128,1536]{1,0:T(8,128)} %refs_17_.3, f32[8,1536]{1,0:T(8,128)} %pad.8.refs_1_, ...), custom_call_target="tpu_custom_call" | custom-call | tf_op jit(solution)/shard_map/open/pallas_call | solution.py:692
  59.0 0.0 all-gather.2.cloned.1.call-update
  59.1 0.0 reduce-scatter.2.cloned.1.call-start
  59.1 0.0 copy-done.12
  59.2 0.1 broadcast_in_dim.33
  59.2 0.1 mul.72
  59.3 0.1 broadcast_in_dim.32
  59.4 0.1 mul.67
  59.5 0.1 broadcast_multiply_fusion.2
  59.7 0.2 broadcast_multiply_fusion.1
  59.9 1.9 sine_multiply_fusion
  61.8 123.2 %self_forward.1 = (f32[512,384]{1,0:T(8,128)}, f32[512,384]{1,0:T(8,128)}, bf16[512,384]{1,0:T(8,128)(2,1)}, bf16[512,384]{1,0:T(8,128)(2,1)}, bf16[512,384]{1,0...) custom-call(bf16[512,1536]{1,0:T(8,128)(2,1)} %get-tuple-element.89., ...), custom_call_target="tpu_custom_call" | custom-call | tf_op jit(solution)/shard_map/self_forward/pallas_call | solution.py:692
  184.9 0.0 all-gather.2.cloned.1.call-done.refs_1_.refs_13_
  185.0 90.9 %cross_forward.1 = (f32[512,384]{1,0:T(8,128)}, f32[512,384]{1,0:T(8,128)}, bf16[512,384]{1,0:T(8,128)(2,1)}, bf16[512,384]{1,0:T(8,128)(2,1)}, bf16[512,384]{1,...) custom-call(bf16[512,1536]{1,0:T(8,128)(2,1)} %get-tuple-element.96., ...), custom_call_target="tpu_custom_call" | custom-call | tf_op jit(solution)/shard_map/cross_forward/pallas_call | solution.py:692
  275.9 79.7 %feed.1 = (f32[128,1536]{1,0:T(8,128)}, f32[8,1536]{1,0:T(8,128)}, bf16[512,1536]{1,0:T(8,128)(2,1)}, bf16[512,1536]{1,0:T(8,128)(2,1)}, bf16[4,192,2240]{2,1,0:T(8,128)(2,1)}, /*index=5*/bf16[4,192,2240]{2,1,0:T(8,128)(2,1)}) custom-call(bf16[512,1536]{1,0:T(8,128)(2,1)} %get-tuple-element.103.refs_0_, bf16[512,1536]{1,0:T(8,128)(2,1)} %get-tuple-element.104.refs_1_, ...), custom_call_target="tpu_custom_call" | custom-call | tf_op jit(solution)/shard_map/feed/pallas_call | solution.py:692
  355.6 97.6 %cross_back.1 = (f32[128,1536]{1,0:T(8,128)}, f32[8,1536]{1,0:T(8,128)}, f32[128,1536]{1,0:T(8,128)}, bf16[512,4096]{1,0:T(8,128)(2,1)}, f32[8,128]{1,0:T(8,128)...) custom-call(bf16[512,1536]{1,0:T(8,128)(2,1)} %get-tuple-element.108, ...), custom_call_target="tpu_custom_call" | custom-call | tf_op jit(solution)/shard_map/cross_back/pallas_call | solution.py:692
  453.1 0.0 reduce-scatter.2.cloned.1.call-update
  453.2 0.0 copy-start.13
  453.2 0.0 copy-start.14
  453.2 101.2 %self_back.1 = (f32[128,1536]{1,0:T(8,128)}, f32[8,1536]{1,0:T(8,128)}, f32[8,128]{1,0:T(8,128)}, f32[8,128]{1,0:T(8,128)}, f32[192,384]{1,0:T(8,128)}, /*index=...) custom-call(bf16[512,1536]{1,0:T(8,128)(2,1)} %get-tuple-element.123, ...), custom_call_target="tpu_custom_call" | custom-call | tf_op jit(solution)/shard_map/self_back/pallas_call | solution.py:692
  554.4 0.8 slice.39
  555.2 0.8 slice.41
  556.0 0.9 fusion.4
  557.0 0.7 concatenate.18.refs_0_
  557.6 0.0 copy-done.13
  557.6 0.0 copy-done.14
  557.6 1.3 pad_maximum_fusion.1.refs_1_
  558.9 21.4 %close.1 = (f32[8,1536]{1,0:T(8,128)}, f32[8,1536]{1,0:T(8,128)}, f32[8,512]{1,0:T(8,128)}) custom-call(f32[8,1536]{1,0:T(8,128)} %concatenate.18.refs_0_, f32[8,512]{1,0:T(8,128)} %pad_maximum_fusion.1.refs_1_), custom_call_target="tpu_custom_call" | custom-call | tf_op jit(solution)/shard_map/close/pallas_call | solution.py:692
  580.3 0.8 slice_bitcast_fusion
  581.1 0.7 copy.36
  581.8 0.7 slice.46
  582.5 1.3 dynamic-slice.1
  583.9 0.6 constant_dynamic-slice_fusion.1
  584.5 1.4 constant_dynamic-slice_fusion
  585.9 2.8 convert_element_type.15
  588.7 0.0 copy-done.2
  588.7 0.9 copy.52
  589.6 0.5 copy-done.5
  590.1 0.9 copy.53
  591.0 0.0 copy-done.11
  591.0 0.7 copy.54
  591.7 0.0 copy-done.10
  591.7 0.7 copy.55
  592.5 0.0 copy-done.9
  592.5 0.7 copy.56
  593.2 0.0 copy-done.8
  593.2 0.7 copy.57
  593.9 0.0 copy-done.7
  593.9 0.7 copy.58
  594.6 0.0 copy-done.4
  594.6 0.9 copy.59
  595.5 0.0 copy-done.3
  595.5 0.9 copy.60
  596.4 0.0 copy-done.6
  596.4 0.7 copy.61
  597.1 1.2 copy.62
  598.3 0.9 copy-done
  599.2 1.2 copy.63
  (21 shorter events, 0.1 us)
Async XLA Ops:
  7.2 51.9 %copy-start.12 = (s32[3,512]{1,0:T(4,128)S(1)}, s32[3,512]{1,0:T(4,128)}, u32[]{:S(2)}) copy-start(s32[3,512]{1,0:T(4,128)} %param.21) | copy-start | bytes 18436
  7.2 177.8 %all-gather.2.cloned.1.call-start = ((), (), s32[]{:S(2)}) async-start(), calls=%async_computation.1 | async-start | bytes 5242880 | tf_op jit(solution)/shard_map/all_gather | solution.py:1217
  59.1 526.8 %reduce-scatter.2.cloned.1.call-start = ((), (), s32[]{:S(2)}) async-start(), calls=%async_computation.2 | async-start | bytes 5242880 | tf_op jit(solution)/shard_map/reduce_scatter | solution.py:1543
  453.2 104.5 %copy-start.13 = (f32[8,128]{1,0:T(8,128)S(1)}, f32[8,128]{1,0:T(8,128)}, u32[]{:S(2)}) copy-start(f32[8,128]{1,0:T(8,128)} %get-tuple-element.144) | copy-start | bytes 12292
  453.2 104.4 %copy-start.14 = (f32[8,128]{1,0:T(8,128)S(1)}, f32[8,128]{1,0:T(8,128)}, u32[]{:S(2)}) copy-start(f32[8,128]{1,0:T(8,128)} %get-tuple-element.145) | copy-start | bytes 12292
  585.9 2.8 copy-start.2
  588.7 1.4 copy-start.5
  588.7 2.3 copy-start.11
  588.7 3.0 copy-start.10
  590.1 2.3 copy-start.9
  590.1 3.0 copy-start.8
  590.1 3.8 copy-start.7
  591.0 3.6 copy-start.4
  592.5 3.0 copy-start.3
  594.6 1.8 copy-start.6
  594.6 2.5 copy-start.1
  597.1 2.1 copy-start
Sparse Core Ops, SparseCore 0:
  59.2 109.4 all-gather.1
  453.3 105.0 reduce-scatter.1

commit v4 on v3

--- a/solution.py
+++ b/solution.py
@@ -113,12 +113,12 @@
                 ((lax.rem(self.dp + k, self.dp_size), self.z), None)
                 for k in range(1, self.dp_size)
             ]
-        if "bits" in groups:
+        if "bits" in groups and "dpall" not in groups:
             bit = 1
             while bit < self.dp_size:
                 peers.append(((flip(self.dp, bit), self.z), None))
                 bit *= 2
-        if "diag" in groups:
+        if "diag" in groups and "dpall" not in groups:
             peers.append(((flip(flip(self.dp, 2), 4), self.z), None))
         for device, cond in peers:
             when(
@@ -747,10 +747,8 @@
                 line.start(piece)
             for piece in range(4):
                 line.steps(piece)
-                if piece < len(gathers):
-                    gathers[piece].forward()
-            for item in gathers[4:]:
-                item.forward()
+                for item in gathers[2 * piece : 2 * piece + 2]:
+                    item.forward()
             for item in gathers:
                 item.tail()
             for item in gathers:
@@ -798,10 +796,12 @@
         end=None,
         exchange=True,
         far=(),
+        settle_small=None,
     ):
         length, width = shape
         rows = length // self.tensor
         pieces = self.pieces
+        near = [(item if isinstance(item, list) else [item], group) for item, group in near]
         shards, lines, sums, far = list(shards), list(lines), list(sums), list(far)
         moving = shards if self.cube else []
         adding = sums if self.cube else []
@@ -837,7 +837,10 @@
             sum_outputs.append(((part, columns), jnp.float32, True))
 
         def body(links, ins, outs, rest):
-            near_far, ins = ins[:count_near], ins[count_near:]
+            near_far = []
+            for item, _ in near:
+                near_far.append(ins[: len(item)])
+                ins = ins[len(item) :]
             shard_refs, ins = ins[: len(moving)], ins[len(moving) :]
             line_refs, ins = ins[: len(lines)], ins[len(lines) :]
             sum_refs, far_refs = ins[: len(adding)], ins[len(adding) :]
@@ -850,9 +853,15 @@
             near_refs, rest = rest[:count_near], rest[count_near:]
             loads = {}
             for index in order:
-                copy = links.here(near_far[index], near_refs[index])
-                copy.start()
-                loads.setdefault(near[index][1], []).append(copy)
+                start = 0
+                for source in near_far[index]:
+                    target = near_refs[index]
+                    if len(near_far[index]) > 1:
+                        target = target.at[:, pl.ds(start, source.shape[1])]
+                        start += source.shape[1]
+                    copy = links.here(source, target)
+                    copy.start()
+                    loads.setdefault(near[index][1], []).append(copy)
 
             def ready(group):
                 for copy in loads.pop(group, []):
@@ -887,6 +896,8 @@
                 groups |= {"bits"} if self.cube else set()
             if adding or here:
                 groups |= {"diag"}
+            if settle_small:
+                groups |= {"dpall"}
             links.greet(groups)
             gathers = [CubeGather(links, a, b) for a, b in zip(shard_refs, full_refs)]
             straight = [
@@ -963,6 +974,8 @@
             if gather:
                 stages += [functools.partial(line.step, hop) for hop in range(links.size - 1)]
             wave(stages, pieces, queue)
+            if settle_small:
+                small = settle_small(links, near_refs, kind_refs, user)
             for item in gathers + old + fresh + straight:
                 item.finish()
             for item in busy.values():
@@ -971,6 +984,8 @@
                 copy.wait()
             if end:
                 end(state[0], links, near_refs, kind_refs, user)
+            if settle_small:
+                small()
             store_kinds("post")
             if gather:
                 store(whole_ref, whole_far)
@@ -981,7 +996,7 @@
                 copy.wait()
 
         order = sorted(range(count_near), key=lambda index: near[index][1])
-        inputs = [(item, False) for item, _ in near]
+        inputs = [(item, False) for items, _ in near for item in items]
         inputs += [(item, False) for item in moving + lines + adding + far]
         outputs = [(form, kind, False) for form, kind, _ in kinds]
         if gather:
@@ -997,7 +1012,13 @@
                 body,
                 inputs,
                 outputs,
-                [pltpu.VMEM(item.shape, item.dtype) for item, _ in near]
+                [
+                    pltpu.VMEM(
+                        (*items[0].shape[:-1], sum(item.shape[-1] for item in items)),
+                        items[0].dtype,
+                    )
+                    for items, _ in near
+                ]
                 + [pltpu.VMEM(form, kind) for form, kind, moment in kinds if moment]
                 + ([pltpu.VMEM((length, width), jnp.bfloat16)] if gather else [])
                 + [
@@ -1025,66 +1046,6 @@
 
     def scatter(self, grad):
         return lax.psum_scatter(grad, "dp", scatter_dimension=0, tiled=True).astype(jnp.float32)
-
-    def close(self, time_part, gain_part):
-        bits = [1 << k for k in range(self.dp.bit_length() - 1)]
-
-        def body(links, ins, outs, scratch):
-            time_ref, gain_ref = ins[:2]
-            total_ref, all_ref, gains_ref = outs[:3]
-            land, held, held_gain, come, come_gain = scratch[:5]
-            links.greet({"zall", "bits"})
-            moves = []
-            for step in range(1, self.tensor):
-                target = lax.rem(links.z + step, self.tensor)
-                move = links.copy(time_ref, land.at[links.z], (links.dp, target), links.slot())
-                move.start()
-                moves.append(move)
-            land[links.z] = time_ref[...]
-            held_gain[0] = gain_ref[...]
-            for move in moves:
-                move.wait_recv()
-            total = land[0]
-            for index in range(1, self.tensor):
-                total = total + land[index]
-            total_ref[...] = total
-            held[0] = total
-            for index, bit in enumerate(bits):
-                target = (flip(links.dp, bit), links.z)
-                one = links.copy(held.at[index], come.at[index], target, links.slot())
-                two = links.copy(held_gain.at[index], come_gain.at[index], target, links.slot())
-                one.start()
-                two.start()
-                one.wait_recv()
-                two.wait_recv()
-                held[index + 1] = held[index] + come[index]
-                held_gain[index + 1] = held_gain[index] + come_gain[index]
-                moves += [one, two]
-            all_ref[...] = held[len(bits)]
-            gains_ref[...] = held_gain[len(bits)]
-            for move in moves:
-                move.wait_send()
-
-        levels = len(bits)
-        results = self.call(
-            "close",
-            body,
-            [(time_part, True), (gain_part, True)],
-            [
-                (time_part.shape, jnp.float32, True),
-                (time_part.shape, jnp.float32, True),
-                (gain_part.shape, jnp.float32, True),
-            ],
-            [
-                pltpu.VMEM((self.tensor, *time_part.shape), jnp.float32),
-                pltpu.VMEM((levels + 1, *time_part.shape), jnp.float32),
-                pltpu.VMEM((levels + 1, *gain_part.shape), jnp.float32),
-                pltpu.VMEM((levels, *time_part.shape), jnp.float32),
-                pltpu.VMEM((levels, *gain_part.shape), jnp.float32),
-            ],
-            80,
-        )
-        return results
 
 
 def add_sum(ref, row, values, first):
@@ -1558,7 +1519,7 @@
         )
 
     def before_self(total, where, near, kinds, first):
-        hidden_ref, grad_ref, mixing_ref = near[17:]
+        hidden_ref, grad_ref, mixing_ref = near[17:20]
         out_ref, sums_ref = kinds[:2]
         unit, inverse = normed(hidden_ref[where, :])
         add_sum(sums_ref, 0, total, first)
@@ -1567,19 +1528,92 @@
             unit, inverse, total * (1.0 + mixing_ref[1:2])
         )
 
+    gain_width = qk_gain.shape[1]
+
+    def settle_small(links, near, kinds, scratch):
+        feed_ref, cross_ref, gain_cross_query_ref, gain_cross_key_ref = near[20:]
+        self_ref, gain_query_ref, gain_key_ref, time_ref, slice_ref = kinds[1:]
+        mine, line_land, stage, land = scratch[10:]
+        z, dp = links.z, links.dp
+        mine[...] = jnp.concatenate(
+            [
+                self_ref[0:2, :],
+                cross_ref[0:1, :],
+                feed_ref[0:2, :],
+                cross_ref[2:3, :],
+                cross_ref[1:2, :],
+                jnp.zeros((1, width), full_type),
+            ],
+            axis=0,
+        )
+        moves = []
+        for step in range(1, plan.tensor):
+            target = lax.rem(z + step, plan.tensor)
+            move = links.copy(mine, line_land.at[z], (dp, target), links.slot())
+            move.start()
+            moves.append(move)
+        line_land[z] = mine[...]
+        gain_rows = jnp.concatenate(
+            [gain_query_ref[...], gain_key_ref[...]]
+            + [gain_cross_query_ref[...], gain_cross_key_ref[...]],
+            axis=1,
+        )
+        for move in moves:
+            move.wait_recv()
+        total = line_land[0]
+        for index in range(1, plan.tensor):
+            total = total + line_land[index]
+        time_ref[0, :, :] = total[:6]
+        for index in range(plan.dp):
+            stage[index] = jnp.concatenate(
+                [
+                    total[:, index * part : (index + 1) * part],
+                    gain_rows[:, index * gain_width : (index + 1) * gain_width],
+                ],
+                axis=1,
+            )
+        land[dp] = stage[dp]
+        others = []
+        for step in range(1, plan.dp):
+            target = lax.rem(dp + step, plan.dp)
+            move = links.copy(stage.at[target], land.at[dp], (target, z), links.slot())
+            move.start()
+            others.append(move)
+
+        def finish():
+            for move in others:
+                move.wait_recv()
+            summed = land[0]
+            for index in range(1, plan.dp):
+                summed = summed + land[index]
+            slice_ref[...] = summed
+            for move in moves + others:
+                move.wait_send()
+
+        return finish
+
     kept, _, _, _, made, sums = plan.phase(
         "self_back",
         [(self_grad_whole, 0), (query_full, 3), (key_full, 3), (value_full, 3), (out_full, 0)]
         + list(zip(self_kept, kept_groups))
         + [(gains, 2), (cosine, 2), (sine, 2), (self_whole, 4), (hidden_in, 4)]
-        + [(grad_resid_self, 4), (mixing, 4)],
+        + [(grad_resid_self, 4), (mixing, 4), (feed_sums, 4), (cross_sums, 4)]
+        + [(gain_cross_query, 4), (gain_cross_key, 4)],
         [
             ((rows, width), full_type, "post"),
             ((8, width), full_type, "post"),
             ((8, HEAD_DIM), full_type, "pre"),
             ((8, HEAD_DIM), full_type, "pre"),
+            ((1, 6, width), full_type, "post"),
+            ((8, part + gain_width), full_type, "post"),
         ],
-        back_scratch,
+        back_scratch
+        + [
+            pltpu.VMEM((8, width), full_type),
+            pltpu.VMEM((plan.tensor, 8, width), full_type),
+            pltpu.VMEM((plan.dp, 8, part + gain_width), full_type),
+            pltpu.VMEM((plan.dp, 8, part + gain_width), full_type),
+        ],
         self_back_pre,
         before_self,
         False,
@@ -1591,34 +1625,18 @@
             (lambda n, k, s: n[16], lambda n, k, s: s[9], part, here, True),
             (lambda n, k, s: n[0], lambda n, k, s: n[10], part, here, True),
         ],
+        settle_small=settle_small,
     )
-    grad_hidden, self_sums, gain_query, gain_key = kept
+    grad_hidden, _, _, _, grad_time, mine = kept
     sum_cross_key, sum_cross_value, sum_cross_query, sum_cross_out = sums
     sum_query, sum_key, sum_value, sum_out = made
 
-    time_part = jnp.concatenate(
-        [
-            self_sums[:2],
-            cross_sums[:1],
-            feed_sums[:2],
-            cross_sums[2:3],
-            cross_sums[1:2],
-            jnp.zeros((1, width), full_type),
-        ],
-        axis=0,
-    )
-    gain_part = jnp.concatenate([gain_query, gain_key, gain_cross_query, gain_cross_key], axis=1)
-    time_total, all_total, gain_total = plan.close(time_part, gain_part)
-    dp = lax.axis_index("dp")
-    mine = lax.dynamic_slice_in_dim(all_total, dp * part, part, axis=1)
-    gain_width = qk_gain.shape[1]
-    gain_mine = lax.dynamic_slice_in_dim(gain_total[:heads], dp * gain_width, gain_width, axis=1)
     return (
         block_out,
         grad_hidden,
         grad_text,
-        time_total[None, :6],
-        mine[:6],
+        grad_time,
+        mine[:6, :part],
         sum_query,
         sum_key,
         sum_value,
@@ -1629,8 +1647,8 @@
         sum_cross_out.T,
         sum_up,
         sum_down.T,
-        gain_mine,
-        mine[6],
+        mine[:heads, part:],
+        mine[6, :part],
     )
 
 

time: 615 us -> 592 us (0.963)
  Pallas kernels: 562 us -> 545 us
    pallas_call x7 -> x6, Pallas kernels: 562 us -> 545 us  [call(): pl.pallas_call(kernel, name=name, out_shape=[jax.ShapeDtypeStruct(shape,...]
    unnamed x44 -> x43, local copies, waits for them, and re-layouts: 13.1 us -> 14.5 us
  transfers between devices with their start and end apart: 2 -> 2, of which waited for: 0 -> 0; matrix products, arithmetic and copies ran while one was open for 2% -> 1% of each run, Pallas kernels for 40% -> 40%
where the time goes in v4:
time: 592 us; the launch traced here: 585 us
  Pallas kernels  545 us (92%)
  local copies, waits for them, and re-layouts  18.7 us (3%)
  between operations  14.7 us (2%)
  other arithmetic  6.45 us (1%)
    pallas_call x6, Pallas kernels, call(): pl.pallas_call(kernel, name=name, out_shape=[jax.ShapeDtypeStruct(shape,...  545 us
    unnamed x43, local copies, waits for them, and re-layouts  14.5 us
  transfers between devices with their start and end apart: 2, of which 0 were waited for; matrix products, arithmetic and copies ran while one was open for 1% of the time, Pallas kernels for 40%

profile of v4, /device:TPU:0, one launch (start us, length us, event | category | flops | bytes accessed | tf_op | source)
XLA Modules:
  0.0 584.6 jit_solution(4288139504106121631)
XLA Ops:
  7.2 0.0 copy-start.13
  7.2 0.0 all-gather.2.cloned.1.call-start
  7.2 0.7 broadcast_in_dim.24
  7.9 0.8 copy.39
  8.7 0.6 pad.8.refs_1_
  9.3 1.4 fusion.2.refs_2_
  10.7 44.9 %open.1 = (f32[8,1536]{1,0:T(8,128)}, f32[8,512]{1,0:T(8,128)}, bf16[512,1536]{1,0:T(8,128)(2,1)}, bf16[1536,384]{1,0:T(8,128)(2,1)}, bf16[1536,384]{1,0:T(8,128...) custom-call(f32[128,1536]{1,0:T(8,128)} %refs_17_.3, f32[8,1536]{1,0:T(8,128)} %pad.8.refs_1_, ...), custom_call_target="tpu_custom_call" | custom-call | tf_op jit(solution)/shard_map/open/pallas_call | solution.py:692
  55.6 0.0 all-gather.2.cloned.1.call-update
  55.6 0.0 reduce-scatter.2.cloned.1.call-start
  55.7 0.0 copy-done.13
  55.7 0.1 broadcast_in_dim.27
  55.8 0.1 mul.66
  55.9 0.1 broadcast_in_dim.26
  56.0 0.1 mul.61
  56.1 0.1 broadcast_multiply_fusion.2
  56.3 0.2 broadcast_multiply_fusion.1
  56.5 1.9 sine_multiply_fusion
  58.4 123.3 %self_forward.1 = (f32[512,384]{1,0:T(8,128)}, f32[512,384]{1,0:T(8,128)}, bf16[512,384]{1,0:T(8,128)(2,1)}, bf16[512,384]{1,0:T(8,128)(2,1)}, bf16[512,384]{1,0...) custom-call(bf16[512,1536]{1,0:T(8,128)(2,1)} %get-tuple-element.85., ...), custom_call_target="tpu_custom_call" | custom-call | tf_op jit(solution)/shard_map/self_forward/pallas_call | solution.py:692
  181.6 0.0 all-gather.2.cloned.1.call-done.refs_1_.refs_13_
  181.7 90.7 %cross_forward.1 = (f32[512,384]{1,0:T(8,128)}, f32[512,384]{1,0:T(8,128)}, bf16[512,384]{1,0:T(8,128)(2,1)}, bf16[512,384]{1,0:T(8,128)(2,1)}, bf16[512,384]{1,...) custom-call(bf16[512,1536]{1,0:T(8,128)(2,1)} %get-tuple-element.92., ...), custom_call_target="tpu_custom_call" | custom-call | tf_op jit(solution)/shard_map/cross_forward/pallas_call | solution.py:692
  272.4 79.8 %feed.1 = (f32[128,1536]{1,0:T(8,128)}, f32[8,1536]{1,0:T(8,128)}, bf16[512,1536]{1,0:T(8,128)(2,1)}, bf16[512,1536]{1,0:T(8,128)(2,1)}, bf16[4,192,2240]{2,1,0:T(8,128)(2,1)}, /*index=5*/bf16[4,192,2240]{2,1,0:T(8,128)(2,1)}) custom-call(bf16[512,1536]{1,0:T(8,128)(2,1)} %get-tuple-element.99.refs_0_, bf16[512,1536]{1,0:T(8,128)(2,1)} %get-tuple-element.100.refs_1_, ...), custom_call_target="tpu_custom_call" | custom-call | tf_op jit(solution)/shard_map/feed/pallas_call | solution.py:692
  352.2 97.7 %cross_back.1 = (f32[128,1536]{1,0:T(8,128)}, f32[8,1536]{1,0:T(8,128)}, f32[128,1536]{1,0:T(8,128)}, bf16[512,4096]{1,0:T(8,128)(2,1)}, f32[8,128]{1,0:T(8,128)...) custom-call(bf16[512,1536]{1,0:T(8,128)(2,1)} %get-tuple-element.104, ...), custom_call_target="tpu_custom_call" | custom-call | tf_op jit(solution)/shard_map/cross_back/pallas_call | solution.py:692
  449.9 0.0 reduce-scatter.2.cloned.1.call-update
  449.9 108.2 %self_back.1 = (f32[128,1536]{1,0:T(8,128)}, f32[8,1536]{1,0:T(8,128)}, f32[8,128]{1,0:T(8,128)}, f32[8,128]{1,0:T(8,128)}, f32[1,6,1536]{2,1,0:T(8,128)}, /*ind...) custom-call(bf16[512,1536]{1,0:T(8,128)(2,1)} %get-tuple-element.119, ...), custom_call_target="tpu_custom_call" | custom-call | tf_op jit(solution)/shard_map/self_back/pallas_call | solution.py:692
  558.1 1.3 slice.23
  559.4 1.3 slice.22
  560.7 1.5 copy.36
  562.1 0.0 copy-start.2
  562.1 0.0 reduce-scatter.2.cloned.1.call-done
  562.1 2.8 convert_element_type.15
  565.0 0.0 copy-start.5
  565.0 0.0 copy-done.2
  565.0 0.0 copy-start.12
  565.0 0.0 copy-start.11
  565.0 0.0 copy-start.10
  565.0 0.9 copy.53
  565.9 0.5 copy-done.5
  566.4 0.0 copy-start.9
  566.4 0.0 copy-start.8
  566.4 0.9 copy.54
  567.3 0.0 copy-done.12
  567.3 0.0 copy-start.7
  567.3 0.0 copy-start.4
  567.3 0.6 copy.55
  567.9 0.0 copy-done.11
  567.9 0.7 copy.56
  568.6 0.0 copy-done.10
  568.6 0.7 copy.57
  569.3 0.0 copy-done.9
  569.3 0.7 copy.58
  570.0 0.0 copy-done.8
  570.0 0.7 copy.59
  570.8 0.0 copy-done.7
  570.8 0.7 copy.60
  571.5 0.0 copy-done.4
  571.5 0.9 copy.61
  572.4 0.0 copy-done.3
  572.4 0.9 copy.62
  573.2 0.0 copy-done.6
  573.2 0.7 copy.63
  574.0 0.0 copy-done.1
  574.0 1.2 copy.64
  575.2 0.9 copy-done
  576.1 1.2 copy.65
  (10 shorter events, 0.0 us)
Async XLA Ops:
  7.2 48.5 %copy-start.13 = (s32[3,512]{1,0:T(4,128)S(1)}, s32[3,512]{1,0:T(4,128)}, u32[]{:S(2)}) copy-start(s32[3,512]{1,0:T(4,128)} %param.21) | copy-start | bytes 18436
  7.2 174.5 %all-gather.2.cloned.1.call-start = ((), (), s32[]{:S(2)}) async-start(), calls=%async_computation.1 | async-start | bytes 5242880 | tf_op jit(solution)/shard_map/all_gather | solution.py:1178
  55.6 506.5 %reduce-scatter.2.cloned.1.call-start = ((), (), s32[]{:S(2)}) async-start(), calls=%async_computation.2 | async-start | bytes 5242880 | tf_op jit(solution)/shard_map/reduce_scatter | solution.py:1504
  562.1 2.8 copy-start.2
  565.0 1.4 copy-start.5
  565.0 2.3 copy-start.12
  565.0 2.9 copy-start.11
  565.0 3.6 copy-start.10
  566.4 2.9 copy-start.9
  566.4 3.6 copy-start.8
  567.3 3.5 copy-start.7
  567.3 4.2 copy-start.4
  569.3 3.0 copy-start.3
  571.5 1.8 copy-start.6
  571.5 2.5 copy-start.1
  574.0 2.1 copy-start
Sparse Core Ops, SparseCore 0:
  55.8 109.5 all-gather.1
  450.0 108.1 reduce-scatter.1

commit v5 on v4

--- a/solution.py
+++ b/solution.py
@@ -153,10 +153,16 @@
         part = self.block(index, piece)
         return self.links.copy(part, part, (self.links.dp, self.links.z + way), slot)
 
-    def start(self, piece):
-        z, last = self.links.z, self.links.size - 1
-        when(z < last, lambda: self.move(z, piece, 1, self.right[0][piece]).start())
-        when(z > 0, lambda: self.move(z, piece, -1, self.left[0][piece]).start())
+    def start(self, piece, source=None):
+        links = self.links
+        z, last = links.z, links.size - 1
+
+        def go(way, slot):
+            mine = self.block(z, piece)
+            links.copy(mine if source is None else source, mine, (links.dp, z + way), slot).start()
+
+        when(z < last, lambda: go(1, self.right[0][piece]))
+        when(z > 0, lambda: go(-1, self.left[0][piece]))
 
     def step(self, hop, piece):
         z, last = self.links.z, self.links.size - 1
@@ -398,28 +404,6 @@
         for move in self.sent:
             move.wait_send()
         self.own.wait()
-
-
-class DirectGather:
-    def __init__(self, links, whole, rows):
-        self.links, self.whole, self.rows = links, whole, rows
-        self.slots = [links.slot() for _ in range(links.size - 1)]
-
-    def start(self, source):
-        links = self.links
-        mine = piece_of(self.whole, links.z, self.rows, 0, self.rows)
-        self.moves = [
-            links.copy(source, mine, (links.dp, lax.rem(links.z + step, links.size)), slot)
-            for step, slot in enumerate(self.slots, 1)
-        ]
-        for move in self.moves:
-            move.start()
-
-    def finish(self):
-        for move in self.moves:
-            move.wait_recv()
-        for move in self.moves:
-            move.wait_send()
 
 
 class Exchange:
@@ -676,6 +660,8 @@
         self.cube = self.dp == 8
         self.calls = 0
         self.pieces = 4
+        self.chunk = 1024
+        self.counts = (1, 2, 3)
 
     def call(self, name, body, inputs, outputs, scratch, copies):
         self.calls += 1
@@ -900,9 +886,22 @@
                 groups |= {"dpall"}
             links.greet(groups)
             gathers = [CubeGather(links, a, b) for a, b in zip(shard_refs, full_refs)]
-            straight = [
-                DirectGather(links, b, a.shape[0]) for a, b in zip(line_refs, line_outs)
-            ]
+            chunked, line_steps = [], []
+            for source, target in zip(line_refs, line_outs):
+                size = self.chunk
+                parts = []
+                for start in range(0, source.shape[1], size):
+                    lanes = pl.ds(start, size)
+                    item = LineGather(links, target.at[:, lanes], source.shape[0], 1)
+                    parts.append(
+                        [functools.partial(item.start, 0, source.at[:, lanes])]
+                        + [functools.partial(item.step, hop, 0) for hop in range(links.size - 1)]
+                    )
+                    chunked.append(item)
+                for turn_at in range(len(parts) + links.size - 1):
+                    for index, steps in enumerate(parts):
+                        if 0 <= turn_at - index < links.size:
+                            line_steps.append(steps[turn_at - index])
             old = [
                 ChipSum(links, a, b, sum_rest[2 * k], sum_rest[2 * k + 1])
                 for k, (a, b) in enumerate(zip(sum_refs, added_refs))
@@ -910,14 +909,24 @@
             for item in gathers + old:
                 item.start()
             copies = []
-            for item, source in zip(straight, line_refs):
-                item.start(source)
+            for source, target in zip(line_refs, line_outs):
                 copies.append(
-                    links.here(source, piece_of(item.whole, links.z, item.rows, 0, item.rows))
+                    links.here(
+                        source, piece_of(target, links.z, source.shape[0], 0, source.shape[0])
+                    )
                 )
                 copies[-1].start()
+
+            def line_some(count):
+                for _ in range(min(count, len(line_steps))):
+                    line_steps.pop(0)()
+
+            if line_steps:
+                line_some(self.counts[0])
             state = begin(links, near_refs, kind_refs, user, far_refs) if begin else (None, [])
             ticks = state[1]
+            if line_steps:
+                ticks = [functools.partial(line_some, count) for count in self.counts[1:]]
             pre(links, near_refs, kind_refs, user, partial_ref, ticks)
             for run in ticks:
                 run()
@@ -956,6 +965,12 @@
                     queue.append(functools.partial(store, held, out))
             queue += [item.forward for item in gathers]
             queue += [item.tail for item in gathers]
+            if line_steps:
+                plain, queue = queue, []
+                total = len(line_steps)
+                for index, run in enumerate(line_steps):
+                    queue.append(run)
+                    queue += plain[len(plain) * index // total : len(plain) * (index + 1) // total]
 
             reduce = LineReduce(links, partial_ref, land_right, land_left, rows, pieces)
             line = LineGather(links, whole_ref, rows, pieces) if gather else None
@@ -976,7 +991,7 @@
             wave(stages, pieces, queue)
             if settle_small:
                 small = settle_small(links, near_refs, kind_refs, user)
-            for item in gathers + old + fresh + straight:
+            for item in gathers + old + fresh + chunked:
                 item.finish()
             for item in busy.values():
                 item.clear()
@@ -1174,9 +1189,7 @@
         unit, _ = normed(resid)
         return (unit * mixing_ref[6:7]).astype(low)
 
-    text_after, self_whole = lax.optimization_barrier((text_states, self_whole))
-    text_all = lax.all_gather(text_after, "tensor", axis=0, tiled=True)
-    kept, cross_whole, full, _, _, _ = plan.phase(
+    kept, cross_whole, full, (text_all,), _, _ = plan.phase(
         "self_forward",
         [(self_whole, 0), (gains, 3), (cosine, 3), (sine, 3), (query_full, 0), (key_full, 1)]
         + [(value_full, 2), (out_full, 4), (hidden_in, 5), (mixing, 5)],
@@ -1186,11 +1199,11 @@
         after_self,
         True,
         shape,
-        shards=[cross_key, cross_value, cross_query, cross_out.T, up_weight, down_weight.T],
+        shards=[cross_key, cross_value, cross_query, cross_out.T],
+        lines=[text_states],
     )
     self_kept, (self_branch, resid_self) = kept[:8], kept[8:]
     cross_key_full, cross_value_full, cross_query_full, cross_out_full = full[:4]
-    up_full, down_full = full[4:]
 
     def cross_begin(links, near, kinds, scratch, far):
         links.ready(-1)
@@ -1227,7 +1240,7 @@
         unit, _ = normed(resid)
         return (unit * (1.0 + mixing_ref[4:5]) + mixing_ref[3:4]).astype(low)
 
-    kept, feed_whole, _, _, _, _ = plan.phase(
+    kept, feed_whole, (up_full, down_full), _, _, _ = plan.phase(
         "cross_forward",
         [(cross_whole, 0), (text_all, 1), (gains, 3), (cross_query_full, 0), (cross_key_full, 1)]
         + [(cross_value_full, 2), (cross_out_full, 4), (resid_self, 5), (mixing, -1)]
@@ -1238,6 +1251,7 @@
         after_cross,
         True,
         shape,
+        shards=[up_weight, down_weight.T],
         begin=cross_begin,
         end=cross_end,
     )

time: 592 us -> 590 us (level)
    unnamed x43 -> x41, local copies, waits for them, and re-layouts: 14.5 us -> 14.5 us
  transfers between devices with their start and end apart: 2 -> 1, of which waited for: 0 -> 0; matrix products, arithmetic and copies ran while one was open for 1% -> 1% of each run, Pallas kernels for 40% -> 18%
where the time goes in v5:
time: 590 us; the launch traced here: 580 us
  Pallas kernels  540 us (92%)
  local copies, waits for them, and re-layouts  18.7 us (3%)
  between operations  14.6 us (2%)
  other arithmetic  7.13 us (1%)
    pallas_call x6, Pallas kernels, call(): pl.pallas_call(kernel, name=name, out_shape=[jax.ShapeDtypeStruct(shape,...  540 us
    unnamed x41, local copies, waits for them, and re-layouts  14.5 us
  transfers between devices with their start and end apart: 1, of which 0 were waited for; matrix products, arithmetic and copies ran while one was open for 1% of the time, Pallas kernels for 18%

profile of v5, /device:TPU:0, one launch (start us, length us, event | category | flops | bytes accessed | tf_op | source)
XLA Modules:
  0.0 580.4 jit_solution(6761391960188475767)
XLA Ops:
  7.2 0.0 reduce-scatter.2.cloned.1.call-start
  7.3 0.7 broadcast_in_dim.24
  7.9 0.7 convert_element_type.14
  8.6 0.1 broadcast_in_dim.27
  8.7 0.1 mul.66
  8.8 0.1 broadcast_in_dim.26
  8.9 0.1 mul.61
  9.0 0.8 copy.39
  9.8 0.6 pad.8.refs_1_
  10.4 0.1 broadcast_multiply_fusion.2
  10.5 0.2 broadcast_multiply_fusion.1
  10.7 1.4 fusion.2.refs_2_
  12.1 1.9 sine_multiply_fusion
  14.0 44.9 %open.1 = (f32[8,1536]{1,0:T(8,128)}, f32[8,512]{1,0:T(8,128)}, bf16[512,1536]{1,0:T(8,128)(2,1)}, bf16[1536,384]{1,0:T(8,128)(2,1)}, bf16[1536,384]{1,0:T(8,128...) custom-call(f32[128,1536]{1,0:T(8,128)} %refs_17_.3, f32[8,1536]{1,0:T(8,128)} %pad.8.refs_1_, ...), custom_call_target="tpu_custom_call" | custom-call | tf_op jit(solution)/shard_map/open/pallas_call | solution.py:678
  58.9 116.1 %self_forward.1 = (f32[512,384]{1,0:T(8,128)}, f32[512,384]{1,0:T(8,128)}, bf16[512,384]{1,0:T(8,128)(2,1)}, bf16[512,384]{1,0:T(8,128)(2,1)}, bf16[512,384]{1,0...) custom-call(bf16[512,1536]{1,0:T(8,128)(2,1)} %get-tuple-element.83., ...), custom_call_target="tpu_custom_call" | custom-call | tf_op jit(solution)/shard_map/self_forward/pallas_call | solution.py:678
  175.1 93.2 %cross_forward.1 = (f32[512,384]{1,0:T(8,128)}, f32[512,384]{1,0:T(8,128)}, bf16[512,384]{1,0:T(8,128)(2,1)}, bf16[512,384]{1,0:T(8,128)(2,1)}, bf16[512,384]{1,...) custom-call(bf16[512,1536]{1,0:T(8,128)(2,1)} %get-tuple-element.90., ...), custom_call_target="tpu_custom_call" | custom-call | tf_op jit(solution)/shard_map/cross_forward/pallas_call | solution.py:678
  268.3 82.0 %feed.1 = (f32[128,1536]{1,0:T(8,128)}, f32[8,1536]{1,0:T(8,128)}, bf16[512,1536]{1,0:T(8,128)(2,1)}, bf16[512,1536]{1,0:T(8,128)(2,1)}, bf16[4,192,2240]{2,1,0:T(8,128)(2,1)}, /*index=5*/bf16[4,192,2240]{2,1,0:T(8,128)(2,1)}) custom-call(bf16[512,1536]{1,0:T(8,128)(2,1)} %get-tuple-element.97.refs_0_, bf16[512,1536]{1,0:T(8,128)(2,1)} %get-tuple-element.98.refs_1_, ...), custom_call_target="tpu_custom_call" | custom-call | tf_op jit(solution)/shard_map/feed/pallas_call | solution.py:678
  350.3 98.8 %cross_back.1 = (f32[128,1536]{1,0:T(8,128)}, f32[8,1536]{1,0:T(8,128)}, f32[128,1536]{1,0:T(8,128)}, bf16[512,4096]{1,0:T(8,128)(2,1)}, f32[8,128]{1,0:T(8,128)...) custom-call(bf16[512,1536]{1,0:T(8,128)(2,1)} %get-tuple-element.102, ...), custom_call_target="tpu_custom_call" | custom-call | tf_op jit(solution)/shard_map/cross_back/pallas_call | solution.py:678
  449.1 0.0 reduce-scatter.2.cloned.1.call-update
  449.2 104.8 %self_back.1 = (f32[128,1536]{1,0:T(8,128)}, f32[8,1536]{1,0:T(8,128)}, f32[8,128]{1,0:T(8,128)}, f32[8,128]{1,0:T(8,128)}, f32[1,6,1536]{2,1,0:T(8,128)}, /*ind...) custom-call(bf16[512,1536]{1,0:T(8,128)(2,1)} %get-tuple-element.117, ...), custom_call_target="tpu_custom_call" | custom-call | tf_op jit(solution)/shard_map/self_back/pallas_call | solution.py:678
  554.0 1.3 slice.23
  555.2 1.3 slice.22
  556.6 1.5 copy.36
  558.0 0.0 copy-start.2
  558.0 0.0 reduce-scatter.2.cloned.1.call-done
  558.0 2.8 convert_element_type.15
  560.8 0.0 copy-start.5
  560.8 0.0 copy-done.2
  560.8 0.0 copy-start.12
  560.8 0.0 copy-start.11
  560.9 0.0 copy-start.10
  560.9 0.9 copy.53
  561.7 0.5 copy-done.5
  562.3 0.0 copy-start.9
  562.3 0.0 copy-start.8
  562.3 0.9 copy.54
  563.1 0.0 copy-done.12
  563.1 0.0 copy-start.7
  563.1 0.0 copy-start.4
  563.1 0.6 copy.55
  563.7 0.0 copy-done.11
  563.8 0.7 copy.56
  564.5 0.0 copy-done.10
  564.5 0.7 copy.57
  565.2 0.0 copy-done.9
  565.2 0.0 copy-start.3
  565.2 0.7 copy.58
  565.9 0.0 copy-done.8
  565.9 0.7 copy.59
  566.6 0.0 copy-done.7
  566.6 0.7 copy.60
  567.3 0.0 copy-done.4
  567.3 0.0 copy-start.6
  567.3 0.0 copy-start.1
  567.3 0.9 copy.61
  568.2 0.0 copy-done.3
  568.2 0.9 copy.62
  569.1 0.0 copy-done.6
  569.1 0.7 copy.63
  569.8 0.0 copy-done.1
  569.8 0.0 copy-start
  569.8 1.2 copy.64
  571.0 0.9 copy-done
  571.9 1.2 copy.65
  (5 shorter events, 0.0 us)
Async XLA Ops:
  7.2 550.8 %reduce-scatter.2.cloned.1.call-start = ((), (), s32[]{:S(2)}) async-start(), calls=%async_computation.1 | async-start | bytes 5242880 | tf_op jit(solution)/shard_map/reduce_scatter | solution.py:1518
  558.0 2.8 copy-start.2
  560.8 1.4 copy-start.5
  560.8 2.3 copy-start.12
  560.8 2.9 copy-start.11
  560.9 3.6 copy-start.10
  562.3 2.9 copy-start.9
  562.3 3.6 copy-start.8
  563.1 3.5 copy-start.7
  563.1 4.2 copy-start.4
  565.2 3.0 copy-start.3
  567.3 1.8 copy-start.6
  567.3 2.5 copy-start.1
  569.8 2.1 copy-start
Sparse Core Ops, SparseCore 0:
  449.3 104.7 reduce-scatter.1

commit v6 on v5

--- a/solution.py
+++ b/solution.py
@@ -341,7 +341,7 @@
         for index, stage in enumerate(stages):
             if 0 <= step - index < pieces:
                 stage(step - index)
-        until = len(queue) * (step + 1) // count
+        until = min(len(queue), len(queue) * (step + 1) * 2 // (count * 1))
         for run in queue[done:until]:
             run()
         done = until
@@ -928,13 +928,12 @@
             if line_steps:
                 ticks = [functools.partial(line_some, count) for count in self.counts[1:]]
             pre(links, near_refs, kind_refs, user, partial_ref, ticks)
-            for run in ticks:
-                run()
             store_kinds("pre")
             for group in sorted(loads):
                 ready(group)
 
-            queue = list(tasks(links, near_refs, kind_refs, user, far_refs)) if tasks else []
+            queue = list(ticks)
+            queue += tasks(links, near_refs, kind_refs, user, far_refs) if tasks else []
             fresh, busy, cleared = [], {}, []
             for (left, right, part, columns, now), seat in zip(jobs, seats):
                 left_ref, right_ref = left(near_refs, kind_refs, user), right(near_refs, kind_refs, user)

time: 590 us -> 564 us (0.956)
  Pallas kernels: 540 us -> 516 us
    pallas_call x6, Pallas kernels: 540 us -> 516 us  [call(): pl.pallas_call(kernel, name=name, out_shape=[jax.ShapeDtypeStruct(shape,...]
  transfers between devices with their start and end apart: 1 -> 1, of which waited for: 0 -> 0; matrix products, arithmetic and copies ran while one was open for 1% -> 1% of each run, Pallas kernels for 18% -> 19%
where the time goes in v6:
time: 564 us; the launch traced here: 556 us
  Pallas kernels  516 us (91%)
  local copies, waits for them, and re-layouts  18.7 us (3%)
  between operations  14.6 us (3%)
  other arithmetic  7.13 us (1%)
    pallas_call x6, Pallas kernels, call(): pl.pallas_call(kernel, name=name, out_shape=[jax.ShapeDtypeStruct(shape,...  516 us
    unnamed x41, local copies, waits for them, and re-layouts  14.5 us
  transfers between devices with their start and end apart: 1, of which 0 were waited for; matrix products, arithmetic and copies ran while one was open for 1% of the time, Pallas kernels for 19%

profile of v6, /device:TPU:0, one launch (start us, length us, event | category | flops | bytes accessed | tf_op | source)
XLA Modules:
  0.0 556.4 jit_solution(1763029133901271176)
XLA Ops:
  7.2 0.0 reduce-scatter.2.cloned.1.call-start
  7.3 0.7 broadcast_in_dim.24
  7.9 0.7 convert_element_type.14
  8.6 0.1 broadcast_in_dim.27
  8.7 0.1 mul.66
  8.8 0.1 broadcast_in_dim.26
  8.9 0.1 mul.61
  9.0 0.8 copy.39
  9.8 0.6 pad.8.refs_1_
  10.4 0.1 broadcast_multiply_fusion.2
  10.5 0.2 broadcast_multiply_fusion.1
  10.7 1.4 fusion.2.refs_2_
  12.1 1.9 sine_multiply_fusion
  14.0 44.9 %open.1 = (f32[8,1536]{1,0:T(8,128)}, f32[8,512]{1,0:T(8,128)}, bf16[512,1536]{1,0:T(8,128)(2,1)}, bf16[1536,384]{1,0:T(8,128)(2,1)}, bf16[1536,384]{1,0:T(8,128...) custom-call(f32[128,1536]{1,0:T(8,128)} %refs_17_.3, f32[8,1536]{1,0:T(8,128)} %pad.8.refs_1_, ...), custom_call_target="tpu_custom_call" | custom-call | tf_op jit(solution)/shard_map/open/pallas_call | solution.py:678
  58.9 114.8 %self_forward.1 = (f32[512,384]{1,0:T(8,128)}, f32[512,384]{1,0:T(8,128)}, bf16[512,384]{1,0:T(8,128)(2,1)}, bf16[512,384]{1,0:T(8,128)(2,1)}, bf16[512,384]{1,0...) custom-call(bf16[512,1536]{1,0:T(8,128)(2,1)} %get-tuple-element.83., ...), custom_call_target="tpu_custom_call" | custom-call | tf_op jit(solution)/shard_map/self_forward/pallas_call | solution.py:678
  173.7 80.1 %cross_forward.1 = (f32[512,384]{1,0:T(8,128)}, f32[512,384]{1,0:T(8,128)}, bf16[512,384]{1,0:T(8,128)(2,1)}, bf16[512,384]{1,0:T(8,128)(2,1)}, bf16[512,384]{1,...) custom-call(bf16[512,1536]{1,0:T(8,128)(2,1)} %get-tuple-element.90., ...), custom_call_target="tpu_custom_call" | custom-call | tf_op jit(solution)/shard_map/cross_forward/pallas_call | solution.py:678
  253.8 78.7 %feed.1 = (f32[128,1536]{1,0:T(8,128)}, f32[8,1536]{1,0:T(8,128)}, bf16[512,1536]{1,0:T(8,128)(2,1)}, bf16[512,1536]{1,0:T(8,128)(2,1)}, bf16[4,192,2240]{2,1,0:T(8,128)(2,1)}, /*index=5*/bf16[4,192,2240]{2,1,0:T(8,128)(2,1)}) custom-call(bf16[512,1536]{1,0:T(8,128)(2,1)} %get-tuple-element.97.refs_0_, bf16[512,1536]{1,0:T(8,128)(2,1)} %get-tuple-element.98.refs_1_, ...), custom_call_target="tpu_custom_call" | custom-call | tf_op jit(solution)/shard_map/feed/pallas_call | solution.py:678
  332.4 93.1 %cross_back.1 = (f32[128,1536]{1,0:T(8,128)}, f32[8,1536]{1,0:T(8,128)}, f32[128,1536]{1,0:T(8,128)}, bf16[512,4096]{1,0:T(8,128)(2,1)}, f32[8,128]{1,0:T(8,128)...) custom-call(bf16[512,1536]{1,0:T(8,128)(2,1)} %get-tuple-element.102, ...), custom_call_target="tpu_custom_call" | custom-call | tf_op jit(solution)/shard_map/cross_back/pallas_call | solution.py:678
  425.6 0.0 reduce-scatter.2.cloned.1.call-update
  425.6 104.3 %self_back.1 = (f32[128,1536]{1,0:T(8,128)}, f32[8,1536]{1,0:T(8,128)}, f32[8,128]{1,0:T(8,128)}, f32[8,128]{1,0:T(8,128)}, f32[1,6,1536]{2,1,0:T(8,128)}, /*ind...) custom-call(bf16[512,1536]{1,0:T(8,128)(2,1)} %get-tuple-element.117, ...), custom_call_target="tpu_custom_call" | custom-call | tf_op jit(solution)/shard_map/self_back/pallas_call | solution.py:678
  529.9 1.3 slice.23
  531.2 1.3 slice.22
  532.5 1.5 copy.36
  534.0 0.0 copy-start.2
  534.0 0.0 reduce-scatter.2.cloned.1.call-done
  534.0 2.8 convert_element_type.15
  536.8 0.0 copy-start.5
  536.8 0.0 copy-done.2
  536.8 0.0 copy-start.12
  536.8 0.0 copy-start.11
  536.8 0.0 copy-start.10
  536.8 0.9 copy.53
  537.7 0.5 copy-done.5
  538.2 0.0 copy-start.9
  538.2 0.0 copy-start.8
  538.2 0.9 copy.54
  539.1 0.0 copy-done.12
  539.1 0.0 copy-start.7
  539.1 0.0 copy-start.4
  539.1 0.6 copy.55
  539.7 0.0 copy-done.11
  539.7 0.7 copy.56
  540.4 0.0 copy-done.10
  540.4 0.7 copy.57
  541.1 0.0 copy-done.9
  541.1 0.0 copy-start.3
  541.2 0.7 copy.58
  541.9 0.0 copy-done.8
  541.9 0.7 copy.59
  542.6 0.0 copy-done.7
  542.6 0.7 copy.60
  543.3 0.0 copy-done.4
  543.3 0.0 copy-start.6
  543.3 0.0 copy-start.1
  543.3 0.9 copy.61
  544.2 0.0 copy-done.3
  544.2 0.9 copy.62
  545.1 0.0 copy-done.6
  545.1 0.7 copy.63
  545.8 0.0 copy-done.1
  545.8 0.0 copy-start
  545.8 1.2 copy.64
  547.0 0.9 copy-done
  547.9 1.2 copy.65
  (5 shorter events, 0.0 us)
Async XLA Ops:
  7.2 526.8 %reduce-scatter.2.cloned.1.call-start = ((), (), s32[]{:S(2)}) async-start(), calls=%async_computation.1 | async-start | bytes 5242880 | tf_op jit(solution)/shard_map/reduce_scatter | solution.py:1517
  534.0 2.8 copy-start.2
  536.8 1.4 copy-start.5
  536.8 2.3 copy-start.12
  536.8 2.9 copy-start.11
  536.8 3.6 copy-start.10
  538.2 2.9 copy-start.9
  538.2 3.6 copy-start.8
  539.1 3.5 copy-start.7
  539.1 4.2 copy-start.4
  541.1 3.0 copy-start.3
  543.3 1.8 copy-start.6
  543.3 2.5 copy-start.1
  545.8 2.1 copy-start
Sparse Core Ops, SparseCore 0:
  425.7 104.8 reduce-scatter.1

commit v7 on v6

--- a/solution.py
+++ b/solution.py
@@ -334,14 +334,14 @@
     ]
 
 
-def wave(stages, pieces, queue):
+def wave(stages, pieces, queue, rate=4):
     count = pieces + len(stages) - 1
     done = 0
     for step in range(count):
         for index, stage in enumerate(stages):
             if 0 <= step - index < pieces:
                 stage(step - index)
-        until = min(len(queue), len(queue) * (step + 1) * 2 // (count * 1))
+        until = min(len(queue), len(queue) * (step + 1) * rate // (2 * count))
         for run in queue[done:until]:
             run()
         done = until
@@ -987,7 +987,7 @@
             stages = reduce_stages(reduce) + [settle]
             if gather:
                 stages += [functools.partial(line.step, hop) for hop in range(links.size - 1)]
-            wave(stages, pieces, queue)
+            wave(stages, pieces, queue, 3 if moving else 4)
             if settle_small:
                 small = settle_small(links, near_refs, kind_refs, user)
             for item in gathers + old + fresh + chunked:

time: 564 us -> 563 us (level)
  no operation moved by 1% of the time
where the time goes in v7:
time: 563 us; the launch traced here: 555 us
  Pallas kernels  515 us (91%)
  local copies, waits for them, and re-layouts  18.7 us (3%)
  between operations  14.6 us (3%)
  other arithmetic  7.13 us (1%)
    pallas_call x6, Pallas kernels, call(): pl.pallas_call(kernel, name=name, out_shape=[jax.ShapeDtypeStruct(shape,...  515 us
    unnamed x41, local copies, waits for them, and re-layouts  14.5 us
  transfers between devices with their start and end apart: 1, of which 0 were waited for; matrix products, arithmetic and copies ran while one was open for 1% of the time, Pallas kernels for 19%

profile of v7, /device:TPU:0, one launch (start us, length us, event | category | flops | bytes accessed | tf_op | source)
XLA Modules:
  0.0 555.3 jit_solution(7423922636025657133)
XLA Ops:
  7.2 0.0 reduce-scatter.2.cloned.1.call-start
  7.3 0.7 broadcast_in_dim.24
  7.9 0.7 convert_element_type.14
  8.6 0.1 broadcast_in_dim.27
  8.7 0.1 mul.66
  8.8 0.1 broadcast_in_dim.26
  8.9 0.1 mul.61
  9.0 0.8 copy.39
  9.8 0.6 pad.8.refs_1_
  10.4 0.1 broadcast_multiply_fusion.2
  10.5 0.2 broadcast_multiply_fusion.1
  10.7 1.4 fusion.2.refs_2_
  12.1 1.9 sine_multiply_fusion
  14.0 44.9 %open.1 = (f32[8,1536]{1,0:T(8,128)}, f32[8,512]{1,0:T(8,128)}, bf16[512,1536]{1,0:T(8,128)(2,1)}, bf16[1536,384]{1,0:T(8,128)(2,1)}, bf16[1536,384]{1,0:T(8,128...) custom-call(f32[128,1536]{1,0:T(8,128)} %refs_17_.3, f32[8,1536]{1,0:T(8,128)} %pad.8.refs_1_, ...), custom_call_target="tpu_custom_call" | custom-call | tf_op jit(solution)/shard_map/open/pallas_call | solution.py:678
  58.9 114.8 %self_forward.1 = (f32[512,384]{1,0:T(8,128)}, f32[512,384]{1,0:T(8,128)}, bf16[512,384]{1,0:T(8,128)(2,1)}, bf16[512,384]{1,0:T(8,128)(2,1)}, bf16[512,384]{1,0...) custom-call(bf16[512,1536]{1,0:T(8,128)(2,1)} %get-tuple-element.83., ...), custom_call_target="tpu_custom_call" | custom-call | tf_op jit(solution)/shard_map/self_forward/pallas_call | solution.py:678
  173.7 78.6 %cross_forward.1 = (f32[512,384]{1,0:T(8,128)}, f32[512,384]{1,0:T(8,128)}, bf16[512,384]{1,0:T(8,128)(2,1)}, bf16[512,384]{1,0:T(8,128)(2,1)}, bf16[512,384]{1,...) custom-call(bf16[512,1536]{1,0:T(8,128)(2,1)} %get-tuple-element.90., ...), custom_call_target="tpu_custom_call" | custom-call | tf_op jit(solution)/shard_map/cross_forward/pallas_call | solution.py:678
  252.3 78.7 %feed.1 = (f32[128,1536]{1,0:T(8,128)}, f32[8,1536]{1,0:T(8,128)}, bf16[512,1536]{1,0:T(8,128)(2,1)}, bf16[512,1536]{1,0:T(8,128)(2,1)}, bf16[4,192,2240]{2,1,0:T(8,128)(2,1)}, /*index=5*/bf16[4,192,2240]{2,1,0:T(8,128)(2,1)}) custom-call(bf16[512,1536]{1,0:T(8,128)(2,1)} %get-tuple-element.97.refs_0_, bf16[512,1536]{1,0:T(8,128)(2,1)} %get-tuple-element.98.refs_1_, ...), custom_call_target="tpu_custom_call" | custom-call | tf_op jit(solution)/shard_map/feed/pallas_call | solution.py:678
  331.0 93.1 %cross_back.1 = (f32[128,1536]{1,0:T(8,128)}, f32[8,1536]{1,0:T(8,128)}, f32[128,1536]{1,0:T(8,128)}, bf16[512,4096]{1,0:T(8,128)(2,1)}, f32[8,128]{1,0:T(8,128)...) custom-call(bf16[512,1536]{1,0:T(8,128)(2,1)} %get-tuple-element.102, ...), custom_call_target="tpu_custom_call" | custom-call | tf_op jit(solution)/shard_map/cross_back/pallas_call | solution.py:678
  424.1 0.0 reduce-scatter.2.cloned.1.call-update
  424.1 104.7 %self_back.1 = (f32[128,1536]{1,0:T(8,128)}, f32[8,1536]{1,0:T(8,128)}, f32[8,128]{1,0:T(8,128)}, f32[8,128]{1,0:T(8,128)}, f32[1,6,1536]{2,1,0:T(8,128)}, /*ind...) custom-call(bf16[512,1536]{1,0:T(8,128)(2,1)} %get-tuple-element.117, ...), custom_call_target="tpu_custom_call" | custom-call | tf_op jit(solution)/shard_map/self_back/pallas_call | solution.py:678
  528.8 1.3 slice.23
  530.1 1.3 slice.22
  531.4 1.5 copy.36
  532.9 0.0 copy-start.2
  532.9 0.0 reduce-scatter.2.cloned.1.call-done
  532.9 2.8 convert_element_type.15
  535.7 0.0 copy-start.5
  535.7 0.0 copy-done.2
  535.7 0.0 copy-start.12
  535.7 0.0 copy-start.11
  535.7 0.0 copy-start.10
  535.7 0.9 copy.53
  536.6 0.5 copy-done.5
  537.1 0.0 copy-start.9
  537.1 0.0 copy-start.8
  537.1 0.9 copy.54
  538.0 0.0 copy-done.12
  538.0 0.0 copy-start.7
  538.0 0.0 copy-start.4
  538.0 0.6 copy.55
  538.6 0.0 copy-done.11
  538.6 0.7 copy.56
  539.3 0.0 copy-done.10
  539.3 0.7 copy.57
  540.0 0.0 copy-done.9
  540.1 0.0 copy-start.3
  540.1 0.7 copy.58
  540.8 0.0 copy-done.8
  540.8 0.7 copy.59
  541.5 0.0 copy-done.7
  541.5 0.7 copy.60
  542.2 0.0 copy-done.4
  542.2 0.0 copy-start.6
  542.2 0.0 copy-start.1
  542.2 0.9 copy.61
  543.1 0.0 copy-done.3
  543.1 0.9 copy.62
  544.0 0.0 copy-done.6
  544.0 0.7 copy.63
  544.7 0.0 copy-done.1
  544.7 0.0 copy-start
  544.7 1.2 copy.64
  545.9 0.9 copy-done
  546.8 1.2 copy.65
  (5 shorter events, 0.0 us)
Async XLA Ops:
  7.2 525.7 %reduce-scatter.2.cloned.1.call-start = ((), (), s32[]{:S(2)}) async-start(), calls=%async_computation.1 | async-start | bytes 5242880 | tf_op jit(solution)/shard_map/reduce_scatter | solution.py:1517
  532.9 2.8 copy-start.2
  535.7 1.4 copy-start.5
  535.7 2.3 copy-start.12
  535.7 2.9 copy-start.11
  535.7 3.6 copy-start.10
  537.1 2.9 copy-start.9
  537.1 3.6 copy-start.8
  538.0 3.5 copy-start.7
  538.0 4.2 copy-start.4
  540.1 3.0 copy-start.3
  542.2 1.8 copy-start.6
  542.2 2.5 copy-start.1
  544.7 2.1 copy-start
Sparse Core Ops, SparseCore 0:
  424.3 105.0 reduce-scatter.1
